TPU v7x, 128 devices: a whole 4x4x4 slice. The times are simulated.
128 devices in a mesh: prod: 4 (over y_lo, core), sae: 32 (over x, z, y_hi).
Axes of the slice: x: 4, y: 4 (y_hi: 2, y_lo: 2; y = y_hi * 2 + y_lo), z: 4, core: 2. Of those that a mesh axis runs over, the one named last changes fastest.
Arguments:
- head_outputs: bfloat16 [512, 2048], P('sae', 'prod'), may hold values from -13 to 13
- out_weight: bfloat16 [2048, 4608], P('prod'), may hold values from -0.28726213 to 0.28726213
- residual_input: bfloat16 [512, 4608], P('sae'), may hold values from -6 to 6
- post_gain: float32 [4608], replicated, may hold values from 0.1 to 1.9
- encoder_weight: bfloat16 [4608, 65536], P(None, ('prod', 'sae')), may hold values from -0.09375 to 0.09375
- encoder_bias: float32 [65536], P(('prod', 'sae')), may hold values from -3 to 3
- decoder_weight: bfloat16 [65536, 4608], P(('prod', 'sae')), may hold values from -0.15625 to 0.15625
- decoder_bias: float32 [4608], replicated, may hold values from -3 to 3
Outputs:
- grad_encoder: bfloat16 [4608, 65536], P(None, ('prod', 'sae'))
- grad_encoder_bias: float32 [65536], P(('prod', 'sae'))
- grad_decoder: bfloat16 [65536, 4608], P(('prod', 'sae'))
All inputs are finite; a program needn't handle non-finite values.
Results may differ from a plain program's by a relative error of at most 0.0064.
Values may be sent and summed in bfloat16 or wider, within the bound.
No kernel may reach another device: no remote copies, remote signals or barrier semaphores. Data moves between devices by JAX's collectives and lax.ppermute only.
A program may use at most 128 MiB of HBM per device.

v0:
```python
import jax
import jax.numpy as jnp
from jax import lax
from jax.sharding import PartitionSpec as P

sparsity_weight = 4.0
norm_epsilon = 1e-06


def local(
    head_outputs,
    out_weight,
    residual_input,
    post_gain,
    encoder_weight,
    encoder_bias,
    decoder_weight,
    decoder_bias,
):
    partial_value = jnp.dot(head_outputs, out_weight, preferred_element_type=jnp.float32)
    projected = lax.psum(partial_value, "prod")
    normed = (
        projected
        * lax.rsqrt(jnp.mean(projected * projected, axis=1, keepdims=True) + norm_epsilon)
        * post_gain
    )
    stream = (residual_input.astype(jnp.float32) + normed).astype(jnp.bfloat16)
    all_rows = lax.all_gather(stream, "sae", axis=0, tiled=True)
    centred = (all_rows.astype(jnp.float32) - decoder_bias).astype(jnp.bfloat16)
    preact = jnp.dot(centred, encoder_weight, preferred_element_type=jnp.float32) + encoder_bias
    rectified = jnp.maximum(preact, 0.0)
    activations = jnp.square(rectified).astype(jnp.bfloat16)
    total_rows = all_rows.shape[0]
    row_count = total_rows // (lax.axis_size("prod") * lax.axis_size("sae"))
    summed = lax.psum_scatter(
        jnp.dot(activations, decoder_weight, preferred_element_type=jnp.float32),
        ("prod", "sae"),
        scatter_dimension=0,
        tiled=True,
    )
    own_start = (lax.axis_index("prod") * lax.axis_size("sae") + lax.axis_index("sae")) * row_count
    own_stream = lax.dynamic_slice_in_dim(all_rows, own_start, row_count)
    grad_recon = (
        2.0 * (summed + decoder_bias - own_stream.astype(jnp.float32)) / total_rows
    ).astype(jnp.bfloat16)
    all_errors = lax.all_gather(grad_recon, ("prod", "sae"), axis=0, tiled=True)
    decoder_wide = decoder_weight.astype(jnp.float32)
    row_norms = jnp.sqrt(jnp.sum(decoder_wide * decoder_wide, axis=1) + norm_epsilon)
    grad_acts = jnp.einsum(
        "td,ld->tl", all_errors, decoder_weight, preferred_element_type=jnp.float32
    )
    grad_acts = grad_acts + sparsity_weight * row_norms / total_rows
    grad_pre = (grad_acts * 2.0 * rectified).astype(jnp.bfloat16)
    grad_encoder = jnp.einsum("td,tl->dl", centred, grad_pre, preferred_element_type=jnp.float32)
    grad_encoder_bias = jnp.sum(grad_pre.astype(jnp.float32), axis=0)
    act_sum = jnp.sum(activations.astype(jnp.float32), axis=0)
    grad_decoder = jnp.einsum(
        "tl,td->ld", activations, all_errors, preferred_element_type=jnp.float32
    )
    grad_decoder = (
        grad_decoder + sparsity_weight / total_rows * (act_sum / row_norms)[:, None] * decoder_wide
    )
    return (grad_encoder.astype(jnp.bfloat16), grad_encoder_bias, grad_decoder.astype(jnp.bfloat16))


def solution(mesh):
    placed = (
        P("sae", "prod"),
        P("prod", None),
        P("sae", None),
        P(),
        P(None, ("prod", "sae")),
        P(("prod", "sae")),
        P(("prod", "sae"), None),
        P(),
    )
    return jax.shard_map(
        local,
        mesh=mesh,
        in_specs=placed,
        out_specs=(P(None, ("prod", "sae")), P(("prod", "sae")), P(("prod", "sae"), None)),
        check_vma=False,
    )
```

profile of v0, /device:TPU:1, one launch (start us, length us, event | category | flops | bytes accessed | tf_op | source)
XLA Modules:
  0.0 655.8 jit_solution(8733462571281269789)
XLA Ops:
  7.2 0.0 copy-start
  7.2 0.0 copy-start.2
  7.2 0.0 copy-start.3
  7.2 0.0 copy-start.5
  7.2 0.0 copy-start.4
  7.2 0.0 all-reduce.4.cloned.1.call-start
  7.3 0.6 copy-done
  7.9 3.8 fusion.14
  11.7 0.0 all-reduce.4.cloned.1.call-update
  11.7 0.0 all-gather.4.cloned.1.call-start
  11.7 40.3 %all-reduce.4.cloned.1.call-done = f32[16,4608]{1,0:T(8,128)} async-done(((f32[16,4608]{1,0:T(8,128)}), f32[16,4608]{1,0:T(8,128)}) %all-reduce.4.cloned.1.call-update) | async-done | bytes 294928 | tf_op jit(solution)/shard_map/psum | solution.py:21
  52.0 1.1 multiply_reduce_fusion
  53.1 0.0 copy-done.2
  53.1 0.0 copy-done.3
  53.1 1.7 add_convert_fusion
  54.9 0.0 all-gather.4.cloned.1.call-update
  54.9 0.0 all-reduce.6.cloned.1.call-start
  54.9 84.0 %all-gather.4.cloned.1.call-done = bf16[512,4608]{1,0:T(8,128)(2,1)} async-done(((bf16[16,4608]{1,0:T(8,128)(2,1)}), bf16[512,4608]{1,0:T(8,128)(2,1)}) %all-gather.4.cloned.1.call-update) | async-done | bytes 4718608 | tf_op jit(solution)/shard_map/all_gather | solution.py:28
  139.0 0.0 copy-done.5
  139.0 5.9 convert_reduce_fusion
  144.9 7.4 %fusion.13 = f32[512,4608]{1,0:T(8,128)} fusion(bf16[512,4608]{1,0:T(8,128)(2,1)} %param.14, f32[512,512]{1,0:T(8,128)S(1)} %get-tuple-element.6), kind=kOutput, calls=%fused_computation.27 | convolution fusion | flops 2416443392 | bytes 15204352 | tf_op jit(solution)/shard_map/dot_general | solution.py:36
  152.3 0.0 all-reduce.6.cloned.1.call-update
  152.3 0.0 all-gather.6.cloned.1.call-start
  152.4 162.2 %all-reduce.6.cloned.1.call-done = f32[512,4608]{1,0:T(8,128)} async-done(((f32[512,4608]{1,0:T(8,128)}), f32[512,4608]{1,0:T(8,128)}) %all-reduce.6.cloned.1.call-update) | async-done | bytes 9437200
  314.5 1.6 fusion.12
  316.2 0.0 all-gather.6.cloned.1.call-update
  316.2 3.3 fusion
  319.5 304.1 %all-gather.6.cloned.1.call-done = bf16[128,4,4608]{2,1,0:T(4,128)(2,1)} async-done(((bf16[1,4,4608]{2,1,0:T(4,128)(2,1)}), bf16[128,4,4608]{2,1,0:T(4,128)(2,1)}) %all-gather.6.cloned.1.call-update) | async-done | bytes 4718608 | tf_op jit(solution)/shard_map/all_gather | solution.py:46
  623.6 7.2 %reshape.32 = bf16[512,4608]{1,0:T(8,128)(2,1)} reshape(bf16[128,4,4608]{2,1,0:T(4,128)(2,1)} %all-gather.6.cloned.1.call-done) | data formatting | bytes 9437184
  630.8 7.1 %convert_reduce_fusion.1 = (f32[512]{0:T(512)}, bf16[512,512]{1,0:T(8,128)(2,1)S(1)}) fusion(f32[512,512]{1,0:T(8,128)S(1)} %get-tuple-element.6, f32[512]{0:T(512)S(1)} %get-tuple-element.4, bf16[512,4608]{1,0:T(8,128)(2,1)} %reshape.32, bf16[512,4608]{1,0:T(8,128)(2,1)} %param.14), kind=kOutput, calls=%fused_computation.15 | convolution fusion | flops 2417491456 | bytes 11014144 | tf_op jit(solution)/shard_map/td,ld->tl/dot_general | solution.py:49
  638.0 4.5 fusion.2
  642.5 6.7 %convolution_convert_fusion = bf16[4608,512]{1,0:T(8,128)(2,1)} fusion(bf16[512,512]{1,0:T(8,128)(2,1)S(1)} %get-tuple-element.8, bf16[512,4608]{1,0:T(8,128)(2,1)} %all-gather.4.cloned.1.call-done, f32[4608]{0:T(1024)S(1)} %copy-done.4), kind=kOutput, calls=%fused_computation.6 | convolution fusion | flops 2425356288 | bytes 9979904 | tf_op jit(solution)/shard_map/td,tl->dl/dot_general | solution.py:54
  (10 shorter events, 0.0 us)
Async XLA Ops:
  7.2 0.7 copy-start
  7.2 45.9 %copy-start.2 = (bf16[16,4608]{1,0:T(8,128)(2,1)S(1)}, bf16[16,4608]{1,0:T(8,128)(2,1)}, u32[]{:S(2)}) copy-start(bf16[16,4608]{1,0:T(8,128)(2,1)} %param.10) | copy-start | bytes 442372
  7.2 45.9 %copy-start.3 = (f32[4608]{0:T(1024)S(1)}, f32[4608]{0:T(1024)}, u32[]{:S(2)}) copy-start(f32[4608]{0:T(1024)} %param.11) | copy-start | bytes 55300
  7.2 131.8 %copy-start.5 = (f32[512]{0:T(512)S(1)}, f32[512]{0:T(512)}, u32[]{:S(2)}) copy-start(f32[512]{0:T(512)} %param.13) | copy-start | bytes 6148
  7.2 131.8 %copy-start.4 = (f32[4608]{0:T(1024)S(1)}, f32[4608]{0:T(1024)}, u32[]{:S(2)}) copy-start(f32[4608]{0:T(1024)} %param.15) | copy-start | bytes 55300
  7.2 44.8 %all-reduce.4.cloned.1.call-start = ((), (), s32[]{:S(2)}) async-start(), calls=%async_computation | async-start | bytes 589824 | tf_op jit(solution)/shard_map/psum | solution.py:21
  11.7 127.3 %all-gather.4.cloned.1.call-start = ((), (), s32[]{:S(2)}) async-start(), calls=%async_computation.1 | async-start | bytes 4866048 | tf_op jit(solution)/shard_map/all_gather | solution.py:28
  54.9 259.6 %all-reduce.6.cloned.1.call-start = ((), (), s32[]{:S(2)}) async-start(), calls=%async_computation.3 | async-start | bytes 18874368
  152.3 471.3 %all-gather.6.cloned.1.call-start = ((), (), s32[]{:S(2)}) async-start(), calls=%async_computation.2 | async-start | bytes 4755456 | tf_op jit(solution)/shard_map/all_gather | solution.py:46
  623.6 14.4 %slice-start = ((s8[4718592]{0:T(1024)(128)(4,1)}), s8[524288]{0:T(1024)(128)(4,1)S(1)}, s32[]{:S(2)}) async-start(s8[4718592]{0:T(1024)(128)(4,1)} %bitcast.10), calls=%async_computation.4 | async-start | bytes 1048576
  630.8 7.1 %slice-start.1 = ((s8[4718592]{0:T(1024)(128)(4,1)}), s8[4194304]{0:T(1024)(128)(4,1)S(1)}, s32[]{:S(2)}) async-start(s8[4718592]{0:T(1024)(128)(4,1)} %bitcast.10), calls=%async_computation.5 | async-start | bytes 8388608
  630.8 7.1 %copy-start.1 = (bf16[512,4608]{1,0:T(8,128)(2,1)S(1)}, bf16[512,4608]{1,0:T(8,128)(2,1)}, u32[]{:S(2)}) copy-start(bf16[512,4608]{1,0:T(8,128)(2,1)} %reshape.32) | copy-start | bytes 14155780
Sparse Core Ops, SparseCore 0:
  11.8 40.1 all-reduce.3
  55.5 83.3 all-gather.3
  152.4 162.0 all-reduce.5
  316.7 306.8 all-gather.5
where the time goes:
time: 656 us
  waiting for transfers between devices  591 us (90%)
  matrix products  35.5 us (5%)
  between operations  13.8 us (2%)
  local copies, waits for them, and re-layouts  7.88 us (1%)
  other arithmetic  7.82 us (1%)
    all_gather x1, waiting for transfers between devices, local(): all_errors = lax.all_gather(grad_recon, ('prod', 'sae'), axis=0, tiled=True)  304 us
    unnamed x5, waiting for transfers between devices  162 us
    all_gather x1, waiting for transfers between devices, local(): all_rows = lax.all_gather(stream, 'sae', axis=0, tiled=True)  84 us
    psum x1, waiting for transfers between devices, local(): projected = lax.psum(partial_value, 'prod')  40.3 us
  transfers between devices with their start and end apart: 4, of which 4 were waited for; matrix products, arithmetic and copies ran while one was open for 1% of the time, Pallas kernels for 0%

commit v1 on v0

v1 whole, which is shorter than its diff:
```python
import jax
import jax.numpy as jnp
from jax import lax
from jax.sharding import PartitionSpec as P

sparsity_weight = 4.0
norm_epsilon = 1e-06
TOKENS = 512
D = 4608
HALF = D // 2
AXES = ("prod", "sae")
bf16 = jnp.bfloat16
f32 = jnp.float32


def place(x, y, z, c):
    return ((y % 2) * 2 + c) * 32 + (x * 4 + z) * 2 + y // 2


def route(step):
    pairs = []
    for x in range(4):
        for y in range(4):
            for z in range(4):
                for c in range(2):
                    tx, ty, tz, tc = step(x, y, z, c)
                    pairs.append((place(x, y, z, c), place(tx % 4, ty % 4, tz % 4, tc % 2)))
    return pairs


def move(value, step):
    return lax.ppermute(value, AXES, route(step))


def to_core(value):
    return move(value, lambda x, y, z, c: (x, y, z, 1 - c))


def to_major(value, d):
    return move(value, lambda x, y, z, c: (x + d, y, z, c) if c == 0 else (x, y, z + d, c))


def to_minor(value, d):
    return move(value, lambda x, y, z, c: (x, y, z + d, c) if c == 0 else (x + d, y, z, c))


def to_y(value, d):
    return move(value, lambda x, y, z, c: (x, y + d, z, c))


def gather(value, to):
    return [value] + [to(value, -d) for d in (1, 2, 3)]


def scatter_sum(pieces, to):
    got = [to(pieces[d], d) for d in (1, 2, 3)]
    total = pieces[0].astype(f32)
    for g in got:
        total = total + g.astype(f32)
    return total


def swap_blocks(value):
    return value.reshape(4, 4, 32, value.shape[-1]).transpose(1, 0, 2, 3).reshape(value.shape)


def local(
    head_outputs,
    out_weight,
    residual_input,
    post_gain,
    encoder_weight,
    encoder_bias,
    decoder_weight,
    decoder_bias,
):
    here = lax.axis_index("prod")
    low = here // 2 == 0
    first = here % 2 == 0

    def own_half(v):
        return jnp.where(first, v[..., :HALF], v[..., HALF:])

    def other_half(v):
        return jnp.where(first, v[..., HALF:], v[..., :HALF])

    heads = jnp.where(low, head_outputs, jnp.roll(head_outputs, 8, axis=0))
    partial_value = jnp.dot(heads, out_weight, preferred_element_type=f32)
    both = own_half(partial_value) + to_core(other_half(partial_value))
    partner = lax.ppermute(both[8:], "prod", [(0, 2), (2, 0), (1, 3), (3, 1)])
    projected = both[:8] + partner
    squares = jnp.broadcast_to(jnp.sum(projected * projected, axis=1, keepdims=True), (8, 128))
    squares = (squares + to_core(squares))[:, :1]
    gain = own_half(post_gain)
    normed = projected * lax.rsqrt(squares / D + norm_epsilon) * gain
    residual = own_half(jnp.where(low, residual_input[:8], residual_input[8:]))
    stream = (residual.astype(f32) + normed).astype(bf16)

    bias_own = own_half(decoder_bias)
    stream = jnp.concatenate(gather(stream, to_y))
    centred = (stream.astype(f32) - bias_own).astype(bf16)
    centred = jnp.concatenate(gather(centred, to_minor))
    centred_own = jnp.concatenate(gather(centred, to_major))
    centred_other = swap_blocks(to_core(centred_own))

    def whole(own, other):
        return jnp.concatenate(
            [jnp.where(first, own, other), jnp.where(first, other, own)], axis=1
        )

    centred = whole(centred_own, centred_other)
    preact = jnp.dot(centred, encoder_weight, preferred_element_type=f32) + encoder_bias
    rectified = jnp.maximum(preact, 0.0)
    activations = jnp.square(rectified).astype(bf16)

    recon = jnp.dot(activations, decoder_weight, preferred_element_type=f32).astype(bf16)
    recon = own_half(recon).astype(f32) + to_core(swap_blocks(other_half(recon))).astype(f32)
    recon = recon.astype(bf16)
    recon = scatter_sum(jnp.split(recon, 4), to_major).astype(bf16)
    recon = scatter_sum(jnp.split(recon, 4), to_minor).astype(bf16)
    summed = recon.astype(f32)
    for d in (1, 2, 3):
        summed = summed + jnp.roll(to_y(recon, -d), 8 * d, axis=0).astype(f32)
    grad_recon = (2.0 * (summed + bias_own - stream.astype(f32)) / TOKENS).astype(bf16)

    errors = jnp.concatenate(gather(grad_recon, to_minor))
    errors_own = jnp.concatenate(gather(errors, to_major))
    all_errors = whole(errors_own, swap_blocks(to_core(errors_own)))

    decoder_wide = decoder_weight.astype(f32)
    row_norms = jnp.sqrt(jnp.sum(decoder_wide * decoder_wide, axis=1) + norm_epsilon)
    grad_acts = jnp.einsum("td,ld->tl", all_errors, decoder_weight, preferred_element_type=f32)
    grad_acts = grad_acts + sparsity_weight * row_norms / TOKENS
    grad_pre = (grad_acts * 2.0 * rectified).astype(bf16)
    grad_encoder = jnp.einsum("td,tl->dl", centred, grad_pre, preferred_element_type=f32)
    grad_encoder_bias = jnp.sum(grad_pre.astype(f32), axis=0)
    act_sum = jnp.sum(activations.astype(f32), axis=0)
    grad_decoder = jnp.einsum("tl,td->ld", activations, all_errors, preferred_element_type=f32)
    grad_decoder = (
        grad_decoder + sparsity_weight / TOKENS * (act_sum / row_norms)[:, None] * decoder_wide
    )
    return (grad_encoder.astype(bf16), grad_encoder_bias, grad_decoder.astype(bf16))


def solution(mesh):
    placed = (
        P("sae", "prod"),
        P("prod", None),
        P("sae", None),
        P(),
        P(None, ("prod", "sae")),
        P(("prod", "sae")),
        P(("prod", "sae"), None),
        P(),
    )
    return jax.shard_map(
        local,
        mesh=mesh,
        in_specs=placed,
        out_specs=(P(None, ("prod", "sae")), P(("prod", "sae")), P(("prod", "sae"), None)),
        check_vma=False,
    )
```

time: 656 us -> 155 us (0.24)
  waiting for transfers between devices: 591 us -> 74.3 us
  starting transfers between devices: 0.16 us -> 49.9 us
  matrix products: 35.5 us -> 21.3 us
  between operations: 13.8 us -> 0.99 us
    all_gather x2 -> x0, waiting for transfers between devices: 388 us -> none  [the longest x1 304 us: local(): all_errors = lax.all_gather(grad_recon, ('prod', 'sae'), axis=0, tiled=True)]
    unnamed x5 -> x0, waiting for transfers between devices: 162 us -> none
    ppermute x0 -> x30, waiting for transfers between devices: none -> 74.3 us  [the longest x29 72.4 us: move(): return lax.ppermute(value, AXES, route(step))]
    ppermute x0 -> x30, starting transfers between devices: none -> 49.9 us  [the longest x29 48.4 us: move(): return lax.ppermute(value, AXES, route(step))]
    psum x1 -> x0, waiting for transfers between devices: 40.3 us -> none  [local(): projected = lax.psum(partial_value, 'prod')]
    dot_general x5, matrix products: 28.3 us -> 18.1 us  [the longest x1 5.14 us: local(): jnp.einsum('tl,td->ld', activations, all_errors, preferred_element_type=f32)]
    unnamed x17 -> x26, local copies, waits for them, and re-layouts: 7.88 us -> 0.63 us
  transfers between devices with their start and end apart: 4 -> 30, of which waited for: 4 -> 26; matrix products, arithmetic and copies ran while one was open for 1% -> 1% of each run, Pallas kernels for 0% -> 0%
where the time goes in v1:
time: 155 us; the launch traced here: 152 us
  waiting for transfers between devices  74.3 us (48%)
  starting transfers between devices  49.9 us (32%)
  matrix products  21.3 us (14%)
  other arithmetic  3.93 us (3%)
  local copies, waits for them, and re-layouts  2.11 us (1%)
    ppermute x29, waiting for transfers between devices, move(): return lax.ppermute(value, AXES, route(step))  72.4 us
    ppermute x29, starting transfers between devices, move(): return lax.ppermute(value, AXES, route(step))  48.4 us
    dot_general x1, matrix products, local(): jnp.einsum('tl,td->ld', activations, all_errors, preferred_element_type=f32)  5.14 us
    dot_general x1, matrix products, local(): jnp.einsum('td,tl->dl', centred, grad_pre, preferred_element_type=f32)  4.37 us
    dot_general x1, matrix products, local(): jnp.einsum('td,ld->tl', all_errors, decoder_weight, preferred_element_typ...  3.24 us
    dot_general x1, matrix products, local(): partial_value = jnp.dot(heads, out_weight, preferred_element_type=f32)  3.11 us
  transfers between devices with their start and end apart: 30, of which 26 were waited for; matrix products, arithmetic and copies ran while one was open for 1% of the time, Pallas kernels for 0%

profile of v1, /device:TPU:1, one launch (start us, length us, event | category | flops | bytes accessed | tf_op | source)
XLA Modules:
  0.0 152.5 jit_solution(4352176692905370500)
XLA Ops:
  1.4 3.1 %fusion.14 = f32[16,4608]{1,0:T(8,128)S(1)} fusion(bf16[512,4608]{1,0:T(8,128)(2,1)} %param.9, bf16[16,512]{1,0:T(8,128)(2,1)} %param.8, bf16[8,512]{1,0:T(8,128)(2,1)S(1)} %get-tuple-element.20, bf16[8,512]{1,0:T(8,128)(2,1)S(1)} %get-tuple-element.19, pred[]{:T(512)S(6)} %eq.9), kind=kOutput, calls=%fused_computation.58 | convolution fusion | flops 75538432 | bytes 5046273 | tf_op jit(solution)/shard_map/dot_general | solution.py:88
  8.5 1.8 %collective-permute-done.1 = f32[8,2304]{1,0:T(8,128)S(1)} collective-permute-done((f32[8,2304]{1,0:T(8,128)S(1)}, f32[8,2304]{1,0:T(8,128)S(1)}, u32[]{:S(2)}, u32[]{:S(2)}) %collective-permute-start.1) | collective-permute-done | bytes 73760 | tf_op jit(solution)/shard_map/ppermute | solution.py:90
  10.5 1.6 %collective-permute-start.2 = (f32[8,128]{0,1:T(8,128)S(1)}, f32[8,128]{0,1:T(8,128)S(1)}, u32[]{:S(2)}, u32[]{:S(2)}) collective-permute-start(f32[8,128]{0,1:T(8,128)S(1)} %broadcast_in_dim.2), channel_id=1, source_target_pairs={{0,32},{32,0},{2,34},{34,2},{4,36},{36,4},{6,38},{38,6},{64,96},{9... | collective-permute-start | bytes 12296 | tf_op jit(solution)/shard_map/ppermute | solution.py:32
  14.5 2.6 %collective-permute-start.4 = (bf16[8,2304]{1,0:T(8,128)(2,1)S(1)}, bf16[8,2304]{1,0:T(8,128)(2,1)S(1)}, u32[]{:S(2)}, u32[]{:S(2)}) collective-permute-start(bf16[8,2304]{1,0:T(8,128)(2,1)S(1)} %add_convert_fusion.3), channel_id=1, source_target_pairs={{0,1},{32,33},{2,3},{34,35},{4,5},{36,37},{6,7},{38,39},{64,65},{9... | collective-permute-start | bytes 110600 | tf_op jit(solution)/shard_map/ppermute | solution.py:32
  21.5 2.5 %collective-permute-start.7 = (bf16[32,2304]{1,0:T(8,128)(2,1)S(1)}, bf16[32,2304]{1,0:T(8,128)(2,1)S(1)}, u32[]{:S(2)}, u32[]{:S(2)}) collective-permute-start(bf16[32,2304]{1,0:T(8,128)(2,1)S(1)} %get-tuple-element.6), channel_id=1, source_target_pairs={{0,4},{32,48},{2,6},{34,50},{4,0},{36,52},{6,2},{38,54},{64,68},{9... | collective-permute-start | bytes 442376 | tf_op jit(solution)/shard_map/ppermute | solution.py:32
  25.5 2.6 %collective-permute-done.7 = bf16[32,2304]{1,0:T(8,128)(2,1)S(1)} collective-permute-done((bf16[32,2304]{1,0:T(8,128)(2,1)S(1)}, bf16[32,2304]{1,0:T(8,128)(2,1)S(1)}, u32[]{:S(2)}, u32[]{:S(2)}) %collective-permute-start.7) | collective-permute-done | bytes 147488 | tf_op jit(solution)/shard_map/ppermute | solution.py:32
  28.3 1.5 %collective-permute-start.11 = (bf16[128,2304]{1,0:T(8,128)(2,1)S(1)}, bf16[128,2304]{1,0:T(8,128)(2,1)S(1)}, u32[]{:S(2)}, u32[]{:S(2)}) collective-permute-start(bf16[128,2304]{1,0:T(8,128)(2,1)S(1)} %pad_maximum_fusion.18), channel_id=1, source_target_pairs={{0,8},{32,34},{2,10},{34,36},{4,12},{36,38},{6,14},{38,32},{64,72}... | collective-permute-start | bytes 1769480 | tf_op jit(solution)/shard_map/ppermute | solution.py:32
  29.9 3.6 %collective-permute-start.10 = (bf16[128,2304]{1,0:T(8,128)(2,1)S(1)}, bf16[128,2304]{1,0:T(8,128)(2,1)S(1)}, u32[]{:S(2)}, u32[]{:S(2)}) collective-permute-start(bf16[128,2304]{1,0:T(8,128)(2,1)S(1)} %pad_maximum_fusion.18), channel_id=1, source_target_pairs={{0,16},{32,36},{2,18},{34,38},{4,20},{36,32},{6,22},{38,34},{64,80... | collective-permute-start | bytes 1769480 | tf_op jit(solution)/shard_map/ppermute | solution.py:32
  33.9 12.9 %collective-permute-done.9 = bf16[128,2304]{1,0:T(8,128)(2,1)S(1)} collective-permute-done((bf16[128,2304]{1,0:T(8,128)(2,1)S(1)}, bf16[128,2304]{1,0:T(8,128)(2,1)S(1)}, u32[]{:S(2)}, u32[]{:S(2)}) %collective-permute-start.9) | collective-permute-done | bytes 589856 | tf_op jit(solution)/shard_map/ppermute | solution.py:32
  47.4 4.0 %collective-permute-start.12 = (bf16[512,2304]{1,0:T(8,128)(2,1)S(1)}, bf16[512,2304]{1,0:T(8,128)(2,1)S(1)}, u32[]{:S(2)}, u32[]{:S(2)}) collective-permute-start(bf16[512,2304]{1,0:T(8,128)(2,1)S(1)} %constant_dynamic-update-slice_fusion), channel_id=1, source_target_pairs={{0,32},{32,0},{2,34},{34,2},{4,36},{36,4},{6,38},{38,6},{64,96},{9... | collective-permute-start | bytes 7077896 | tf_op jit(solution)/shard_map/ppermute | solution.py:32
  51.5 4.2 %collective-permute-done.12 = bf16[512,2304]{1,0:T(8,128)(2,1)S(1)} collective-permute-done((bf16[512,2304]{1,0:T(8,128)(2,1)S(1)}, bf16[512,2304]{1,0:T(8,128)(2,1)S(1)}, u32[]{:S(2)}, u32[]{:S(2)}) %collective-permute-start.12) | collective-permute-done | bytes 2359328 | tf_op jit(solution)/shard_map/ppermute | solution.py:32
  56.7 2.6 %convert_reduce_fusion = (f32[512]{0:T(512)S(1)}, f32[512,512]{1,0:T(8,128)S(1)}) fusion(f32[512]{0:T(512)S(1)} %copy-done.3, bf16[4608,512]{1,0:T(8,128)(2,1)S(1)} %bitcast.30, bf16[512,2304]{1,0:T(8,128)(2,1)S(1)} %get-tuple-element.10, bf16[512,2304]{1,0:T(8,128)(2,1)S(1)} %get-tuple-element.9), kind=kOutput, calls=%fused_computation.24 | convolution fusion | flops 2426928640 | bytes 10489856 | tf_op jit(solution)/shard_map/dot_general | solution.py:112
  59.3 2.9 %convolution_convert_fusion.1 = bf16[512,4608]{1,0:T(8,128)(2,1)S(1)} fusion(bf16[512,4608]{1,0:T(8,128)(2,1)S(1)} %bitcast.25, f32[512,512]{1,0:T(8,128)S(1)} %get-tuple-element.24), kind=kOutput, calls=%fused_computation.6 | convolution fusion | flops 2418802688 | bytes 10485760 | tf_op jit(solution)/shard_map/dot_general | solution.py:116
  63.0 4.2 %collective-permute-done.13 = bf16[512,2304]{1,0:T(8,128)(2,1)S(1)} collective-permute-done((bf16[512,2304]{1,0:T(8,128)(2,1)S(1)}, bf16[512,2304]{1,0:T(8,128)(2,1)S(1)}, u32[]{:S(2)}, u32[]{:S(2)}) %collective-permute-start.13) | collective-permute-done | bytes 2359328 | tf_op jit(solution)/shard_map/ppermute | solution.py:32
  69.1 1.9 %collective-permute-start.16 = (bf16[128,2304]{1,0:T(8,128)(2,1)S(1)}, bf16[128,2304]{1,0:T(8,128)(2,1)S(1)}, u32[]{:S(2)}, u32[]{:S(2)}) collective-permute-start(bf16[128,2304]{1,0:T(8,128)(2,1)S(1)} %get-tuple-element.12), channel_id=1, source_target_pairs={{0,24},{32,38},{2,26},{34,32},{4,28},{36,34},{6,30},{38,36},{64,88... | collective-permute-start | bytes 1769480 | tf_op jit(solution)/shard_map/ppermute | solution.py:32
  71.5 7.0 %collective-permute-done.14 = bf16[128,2304]{1,0:T(8,128)(2,1)S(1)} collective-permute-done((bf16[128,2304]{1,0:T(8,128)(2,1)S(1)}, bf16[128,2304]{1,0:T(8,128)(2,1)S(1)}, u32[]{:S(2)}, u32[]{:S(2)}) %collective-permute-start.14) | collective-permute-done | bytes 589856 | tf_op jit(solution)/shard_map/ppermute | solution.py:32
  78.5 5.6 %collective-permute-done.16 = bf16[128,2304]{1,0:T(8,128)(2,1)S(1)} collective-permute-done((bf16[128,2304]{1,0:T(8,128)(2,1)S(1)}, bf16[128,2304]{1,0:T(8,128)(2,1)S(1)}, u32[]{:S(2)}, u32[]{:S(2)}) %collective-permute-start.16) | collective-permute-done | bytes 589856 | tf_op jit(solution)/shard_map/ppermute | solution.py:32
  91.1 2.8 %collective-permute-done.18 = bf16[32,2304]{1,0:T(8,128)(2,1)S(1)} collective-permute-done((bf16[32,2304]{1,0:T(8,128)(2,1)S(1)}, bf16[32,2304]{1,0:T(8,128)(2,1)S(1)}, u32[]{:S(2)}, u32[]{:S(2)}) %collective-permute-start.18) | collective-permute-done | bytes 147488 | tf_op jit(solution)/shard_map/ppermute | solution.py:32
  94.0 2.7 %collective-permute-start.20 = (bf16[32,2304]{1,0:T(8,128)(2,1)S(1)}, bf16[32,2304]{1,0:T(8,128)(2,1)S(1)}, u32[]{:S(2)}, u32[]{:S(2)}) collective-permute-start(bf16[32,2304]{1,0:T(8,128)(2,1)S(1)} %add_convert_fusion.2), channel_id=1, source_target_pairs={{0,65},{32,97},{2,67},{34,99},{4,69},{36,101},{6,71},{38,103},{64,... | collective-permute-start | bytes 442376 | tf_op jit(solution)/shard_map/ppermute | solution.py:32
  97.5 1.7 %collective-permute-done.22 = bf16[32,2304]{1,0:T(8,128)(2,1)S(1)} collective-permute-done((bf16[32,2304]{1,0:T(8,128)(2,1)S(1)}, bf16[32,2304]{1,0:T(8,128)(2,1)S(1)}, u32[]{:S(2)}, u32[]{:S(2)}) %collective-permute-start.22) | collective-permute-done | bytes 147488 | tf_op jit(solution)/shard_map/ppermute | solution.py:32
  99.3 3.0 %collective-permute-done.21 = bf16[32,2304]{1,0:T(8,128)(2,1)S(1)} collective-permute-done((bf16[32,2304]{1,0:T(8,128)(2,1)S(1)}, bf16[32,2304]{1,0:T(8,128)(2,1)S(1)}, u32[]{:S(2)}, u32[]{:S(2)}) %collective-permute-start.21) | collective-permute-done | bytes 147488 | tf_op jit(solution)/shard_map/ppermute | solution.py:32
  102.9 2.2 %collective-permute-start.24 = (bf16[32,2304]{1,0:T(8,128)(2,1)S(1)}, bf16[32,2304]{1,0:T(8,128)(2,1)S(1)}, u32[]{:S(2)}, u32[]{:S(2)}) collective-permute-start(bf16[32,2304]{1,0:T(8,128)(2,1)S(1)} %get-tuple-element.4), channel_id=1, source_target_pairs={{0,4},{32,48},{2,6},{34,50},{4,0},{36,52},{6,2},{38,54},{64,68},{9... | collective-permute-start | bytes 442376 | tf_op jit(solution)/shard_map/ppermute | solution.py:32
  105.8 1.9 %collective-permute-done.25 = bf16[32,2304]{1,0:T(8,128)(2,1)S(1)} collective-permute-done((bf16[32,2304]{1,0:T(8,128)(2,1)S(1)}, bf16[32,2304]{1,0:T(8,128)(2,1)S(1)}, u32[]{:S(2)}, u32[]{:S(2)}) %collective-permute-start.25) | collective-permute-done | bytes 147488 | tf_op jit(solution)/shard_map/ppermute | solution.py:32
  107.7 1.6 %collective-permute-done.24 = bf16[32,2304]{1,0:T(8,128)(2,1)S(1)} collective-permute-done((bf16[32,2304]{1,0:T(8,128)(2,1)S(1)}, bf16[32,2304]{1,0:T(8,128)(2,1)S(1)}, u32[]{:S(2)}, u32[]{:S(2)}) %collective-permute-start.24) | collective-permute-done | bytes 147488 | tf_op jit(solution)/shard_map/ppermute | solution.py:32
  109.9 2.1 %collective-permute-start.28 = (bf16[128,2304]{1,0:T(8,128)(2,1)S(1)}, bf16[128,2304]{1,0:T(8,128)(2,1)S(1)}, u32[]{:S(2)}, u32[]{:S(2)}) collective-permute-start(bf16[128,2304]{1,0:T(8,128)(2,1)S(1)} %pad_maximum_fusion.19), channel_id=1, source_target_pairs={{0,8},{32,34},{2,10},{34,36},{4,12},{36,38},{6,14},{38,32},{64,72}... | collective-permute-start | bytes 1769480 | tf_op jit(solution)/shard_map/ppermute | solution.py:32
  112.0 3.0 %collective-permute-start.27 = (bf16[128,2304]{1,0:T(8,128)(2,1)S(1)}, bf16[128,2304]{1,0:T(8,128)(2,1)S(1)}, u32[]{:S(2)}, u32[]{:S(2)}) collective-permute-start(bf16[128,2304]{1,0:T(8,128)(2,1)S(1)} %pad_maximum_fusion.19), channel_id=1, source_target_pairs={{0,16},{32,36},{2,18},{34,38},{4,20},{36,32},{6,22},{38,34},{64,80... | collective-permute-start | bytes 1769480 | tf_op jit(solution)/shard_map/ppermute | solution.py:32
  115.1 13.4 %collective-permute-done.26 = bf16[128,2304]{1,0:T(8,128)(2,1)S(1)} collective-permute-done((bf16[128,2304]{1,0:T(8,128)(2,1)S(1)}, bf16[128,2304]{1,0:T(8,128)(2,1)S(1)}, u32[]{:S(2)}, u32[]{:S(2)}) %collective-permute-start.26) | collective-permute-done | bytes 589856 | tf_op jit(solution)/shard_map/ppermute | solution.py:32
  129.0 5.9 %collective-permute-start.29 = (bf16[512,2304]{1,0:T(8,128)(2,1)S(1)}, bf16[512,2304]{1,0:T(8,128)(2,1)S(1)}, u32[]{:S(2)}, u32[]{:S(2)}) collective-permute-start(bf16[512,2304]{1,0:T(8,128)(2,1)S(1)} %constant_dynamic-update-slice_fusion.7), channel_id=1, source_target_pairs={{0,32},{32,0},{2,34},{34,2},{4,36},{36,4},{6,38},{38,6},{64,96},{9... | collective-permute-start | bytes 7077896 | tf_op jit(solution)/shard_map/ppermute | solution.py:32
  135.9 3.2 %collective-permute-done.29 = bf16[512,2304]{1,0:T(8,128)(2,1)S(1)} collective-permute-done((bf16[512,2304]{1,0:T(8,128)(2,1)S(1)}, bf16[512,2304]{1,0:T(8,128)(2,1)S(1)}, u32[]{:S(2)}, u32[]{:S(2)}) %collective-permute-start.29) | collective-permute-done | bytes 2359328 | tf_op jit(solution)/shard_map/ppermute | solution.py:32
  139.7 3.2 %convert_reduce_fusion.1 = (f32[512]{0:T(512)}, bf16[512,512]{1,0:T(8,128)(2,1)S(1)}) fusion(f32[512,512]{1,0:T(8,128)S(1)} %get-tuple-element.24, f32[512]{0:T(512)S(1)} %get-tuple-element.22, bf16[512,4608]{1,0:T(8,128)(2,1)S(1)} %bitcast.25, bf16[512,2304]{1,0:T(8,128)(2,1)S(1)} %get-tuple-element.8, bf16[512,2304]{1,0:T(8,128)(2,1)S(1)} %get-tuple-element.7), kind=kOutput, calls=%fused_computation.25 | convolution fusion | flops 2426928640 | bytes 11014144 | tf_op jit(solution)/shard_map/td,ld->tl/dot_general | solution.py:132
  143.0 5.1 %fusion.2 = bf16[512,4608]{1,0:T(8,128)(2,1)} fusion(bf16[512,4608]{1,0:T(8,128)(2,1)S(1)} %bitcast.25, f32[512]{0:T(512)S(1)} %get-tuple-element.21, bf16[512,2304]{1,0:T(8,128)(2,1)S(1)} %get-tuple-element.8, bf16[512,2304]{1,0:T(8,128)(2,1)S(1)} %get-tuple-element.7, f32[512,512]{1,0:T(8,128)S(1)} %get-tuple-element.24), kind=kOutput, calls=%fused_computation.4 | convolution fusion | flops 2435317760 | bytes 15206400 | tf_op jit(solution)/shard_map/tl,td->ld/dot_general | solution.py:138
  148.1 4.4 %convolution_convert_fusion = bf16[4608,512]{1,0:T(8,128)(2,1)} fusion(bf16[512,512]{1,0:T(8,128)(2,1)S(1)} %get-tuple-element.26, bf16[512,2304]{1,0:T(8,128)(2,1)S(1)} %get-tuple-element.10, bf16[512,2304]{1,0:T(8,128)(2,1)S(1)} %get-tuple-element.9), kind=kOutput, calls=%fused_computation.5 | convolution fusion | flops 2427715584 | bytes 9961472 | tf_op jit(solution)/shard_map/td,tl->dl/dot_general | solution.py:135
  (97 shorter events, 30.7 us)
Async XLA Ops:
  1.4 16.9 %copy-start.2 = (f32[4608]{0:T(1024)S(1)}, f32[4608]{0:T(1024)}, u32[]{:S(2)}) copy-start(f32[4608]{0:T(1024)} %param.15) | copy-start | bytes 55300
  4.5 2.5 %collective-permute-start = (f32[16,2304]{1,0:T(8,128)S(1)}, f32[16,2304]{1,0:T(8,128)S(1)}, u32[]{:S(2)}, u32[]{:S(2)}) collective-permute-start(f32[16,2304]{1,0:T(8,128)S(1)} %slice_select_fusion), channel_id=1, source_target_pairs={{0,32},{32,0},{2,34},{34,2},{4,36},{36,4},{6,38},{38,6},{64,96},{9... | collective-permute-start | bytes 442376 | tf_op jit(solution)/shard_map/ppermute | solution.py:32
  7.1 3.3 %collective-permute-start.1 = (f32[8,2304]{1,0:T(8,128)S(1)}, f32[8,2304]{1,0:T(8,128)S(1)}, u32[]{:S(2)}, u32[]{:S(2)}) collective-permute-start(f32[8,2304]{1,0:T(8,128)S(1)} %slice.109), channel_id=1, source_target_pairs={{0,64},{64,0},{32,96},{96,32},{1,65},{65,1},{33,97},{97,33},{2,66}... | collective-permute-start | bytes 221192 | tf_op jit(solution)/shard_map/ppermute | solution.py:90
  10.5 2.5 %collective-permute-start.2 = (f32[8,128]{0,1:T(8,128)S(1)}, f32[8,128]{0,1:T(8,128)S(1)}, u32[]{:S(2)}, u32[]{:S(2)}) collective-permute-start(f32[8,128]{0,1:T(8,128)S(1)} %broadcast_in_dim.2), channel_id=1, source_target_pairs={{0,32},{32,0},{2,34},{34,2},{4,36},{36,4},{6,38},{38,6},{64,96},{9... | collective-permute-start | bytes 12296 | tf_op jit(solution)/shard_map/ppermute | solution.py:32
  13.1 5.1 %collective-permute-start.5 = (bf16[8,2304]{1,0:T(8,128)(2,1)S(1)}, bf16[8,2304]{1,0:T(8,128)(2,1)S(1)}, u32[]{:S(2)}, u32[]{:S(2)}) collective-permute-start(bf16[8,2304]{1,0:T(8,128)(2,1)S(1)} %add_convert_fusion.3), channel_id=1, source_target_pairs={{0,64},{32,96},{2,66},{34,98},{4,68},{36,100},{6,70},{38,102},{64,... | collective-permute-start | bytes 110600 | tf_op jit(solution)/shard_map/ppermute | solution.py:32
  14.5 4.4 %collective-permute-start.4 = (bf16[8,2304]{1,0:T(8,128)(2,1)S(1)}, bf16[8,2304]{1,0:T(8,128)(2,1)S(1)}, u32[]{:S(2)}, u32[]{:S(2)}) collective-permute-start(bf16[8,2304]{1,0:T(8,128)(2,1)S(1)} %add_convert_fusion.3), channel_id=1, source_target_pairs={{0,1},{32,33},{2,3},{34,35},{4,5},{36,37},{6,7},{38,39},{64,65},{9... | collective-permute-start | bytes 110600 | tf_op jit(solution)/shard_map/ppermute | solution.py:32
  17.1 3.1 %collective-permute-start.3 = (bf16[8,2304]{1,0:T(8,128)(2,1)S(1)}, bf16[8,2304]{1,0:T(8,128)(2,1)S(1)}, u32[]{:S(2)}, u32[]{:S(2)}) collective-permute-start(bf16[8,2304]{1,0:T(8,128)(2,1)S(1)} %add_convert_fusion.3), channel_id=1, source_target_pairs={{0,65},{32,97},{2,67},{34,99},{4,69},{36,101},{6,71},{38,103},{64,... | collective-permute-start | bytes 110600 | tf_op jit(solution)/shard_map/ppermute | solution.py:32
  20.3 5.3 %collective-permute-start.8 = (bf16[32,2304]{1,0:T(8,128)(2,1)S(1)}, bf16[32,2304]{1,0:T(8,128)(2,1)S(1)}, u32[]{:S(2)}, u32[]{:S(2)}) collective-permute-start(bf16[32,2304]{1,0:T(8,128)(2,1)S(1)} %get-tuple-element.6), channel_id=1, source_target_pairs={{0,2},{32,40},{2,4},{34,42},{4,6},{36,44},{6,0},{38,46},{64,66},{9... | collective-permute-start | bytes 442376 | tf_op jit(solution)/shard_map/ppermute | solution.py:32
  21.5 6.6 %collective-permute-start.7 = (bf16[32,2304]{1,0:T(8,128)(2,1)S(1)}, bf16[32,2304]{1,0:T(8,128)(2,1)S(1)}, u32[]{:S(2)}, u32[]{:S(2)}) collective-permute-start(bf16[32,2304]{1,0:T(8,128)(2,1)S(1)} %get-tuple-element.6), channel_id=1, source_target_pairs={{0,4},{32,48},{2,6},{34,50},{4,0},{36,52},{6,2},{38,54},{64,68},{9... | collective-permute-start | bytes 442376 | tf_op jit(solution)/shard_map/ppermute | solution.py:32
  24.0 4.3 %collective-permute-start.6 = (bf16[32,2304]{1,0:T(8,128)(2,1)S(1)}, bf16[32,2304]{1,0:T(8,128)(2,1)S(1)}, u32[]{:S(2)}, u32[]{:S(2)}) collective-permute-start(bf16[32,2304]{1,0:T(8,128)(2,1)S(1)} %get-tuple-element.6), channel_id=1, source_target_pairs={{0,6},{32,56},{2,0},{34,58},{4,2},{36,60},{6,4},{38,62},{64,70},{9... | collective-permute-start | bytes 442376 | tf_op jit(solution)/shard_map/ppermute | solution.py:32
  28.3 28.0 %slice-start.2 = ((s8[4718592]{0:T(1024)(128)(4,1)}), s8[4194304]{0:T(1024)(128)(4,1)S(1)}, s32[]{:S(2)}) async-start(s8[4718592]{0:T(1024)(128)(4,1)} %bitcast.29), calls=%async_computation.2 | async-start | bytes 8388608
  28.3 19.1 %collective-permute-start.11 = (bf16[128,2304]{1,0:T(8,128)(2,1)S(1)}, bf16[128,2304]{1,0:T(8,128)(2,1)S(1)}, u32[]{:S(2)}, u32[]{:S(2)}) collective-permute-start(bf16[128,2304]{1,0:T(8,128)(2,1)S(1)} %pad_maximum_fusion.18), channel_id=1, source_target_pairs={{0,8},{32,34},{2,10},{34,36},{4,12},{36,38},{6,14},{38,32},{64,72}... | collective-permute-start | bytes 1769480 | tf_op jit(solution)/shard_map/ppermute | solution.py:32
  29.9 17.5 %collective-permute-start.10 = (bf16[128,2304]{1,0:T(8,128)(2,1)S(1)}, bf16[128,2304]{1,0:T(8,128)(2,1)S(1)}, u32[]{:S(2)}, u32[]{:S(2)}) collective-permute-start(bf16[128,2304]{1,0:T(8,128)(2,1)S(1)} %pad_maximum_fusion.18), channel_id=1, source_target_pairs={{0,16},{32,36},{2,18},{34,38},{4,20},{36,32},{6,22},{38,34},{64,80... | collective-permute-start | bytes 1769480 | tf_op jit(solution)/shard_map/ppermute | solution.py:32
  33.5 13.4 %collective-permute-start.9 = (bf16[128,2304]{1,0:T(8,128)(2,1)S(1)}, bf16[128,2304]{1,0:T(8,128)(2,1)S(1)}, u32[]{:S(2)}, u32[]{:S(2)}) collective-permute-start(bf16[128,2304]{1,0:T(8,128)(2,1)S(1)} %pad_maximum_fusion.18), channel_id=1, source_target_pairs={{0,24},{32,38},{2,26},{34,32},{4,28},{36,34},{6,30},{38,36},{64,88... | collective-permute-start | bytes 1769480 | tf_op jit(solution)/shard_map/ppermute | solution.py:32
  47.4 8.2 %collective-permute-start.12 = (bf16[512,2304]{1,0:T(8,128)(2,1)S(1)}, bf16[512,2304]{1,0:T(8,128)(2,1)S(1)}, u32[]{:S(2)}, u32[]{:S(2)}) collective-permute-start(bf16[512,2304]{1,0:T(8,128)(2,1)S(1)} %constant_dynamic-update-slice_fusion), channel_id=1, source_target_pairs={{0,32},{32,0},{2,34},{34,2},{4,36},{36,4},{6,38},{38,6},{64,96},{9... | collective-permute-start | bytes 7077896 | tf_op jit(solution)/shard_map/ppermute | solution.py:32
  62.6 4.6 %collective-permute-start.13 = (bf16[512,2304]{1,0:T(8,128)(2,1)S(1)}, bf16[512,2304]{1,0:T(8,128)(2,1)S(1)}, u32[]{:S(2)}, u32[]{:S(2)}) collective-permute-start(bf16[512,2304]{1,0:T(8,128)(2,1)S(1)} %bitcast.27), channel_id=1, source_target_pairs={{0,32},{32,0},{2,34},{34,2},{4,36},{36,4},{6,38},{38,6},{64,96},{9... | collective-permute-start | bytes 7077896 | tf_op jit(solution)/shard_map/ppermute | solution.py:32
  68.2 10.3 %collective-permute-start.14 = (bf16[128,2304]{1,0:T(8,128)(2,1)S(1)}, bf16[128,2304]{1,0:T(8,128)(2,1)S(1)}, u32[]{:S(2)}, u32[]{:S(2)}) collective-permute-start(bf16[128,2304]{1,0:T(8,128)(2,1)S(1)} %get-tuple-element.11), channel_id=1, source_target_pairs={{0,8},{32,34},{2,10},{34,36},{4,12},{36,38},{6,14},{38,32},{64,72}... | collective-permute-start | bytes 1769480 | tf_op jit(solution)/shard_map/ppermute | solution.py:32
  69.1 15.0 %collective-permute-start.16 = (bf16[128,2304]{1,0:T(8,128)(2,1)S(1)}, bf16[128,2304]{1,0:T(8,128)(2,1)S(1)}, u32[]{:S(2)}, u32[]{:S(2)}) collective-permute-start(bf16[128,2304]{1,0:T(8,128)(2,1)S(1)} %get-tuple-element.12), channel_id=1, source_target_pairs={{0,24},{32,38},{2,26},{34,32},{4,28},{36,34},{6,30},{38,36},{64,88... | collective-permute-start | bytes 1769480 | tf_op jit(solution)/shard_map/ppermute | solution.py:32
  70.9 14.3 %collective-permute-start.15 = (bf16[128,2304]{1,0:T(8,128)(2,1)S(1)}, bf16[128,2304]{1,0:T(8,128)(2,1)S(1)}, u32[]{:S(2)}, u32[]{:S(2)}) collective-permute-start(bf16[128,2304]{1,0:T(8,128)(2,1)S(1)} %get-tuple-element.13), channel_id=1, source_target_pairs={{0,16},{32,36},{2,18},{34,38},{4,20},{36,32},{6,22},{38,34},{64,80... | collective-permute-start | bytes 1769480 | tf_op jit(solution)/shard_map/ppermute | solution.py:32
  85.6 5.3 %collective-permute-start.17 = (bf16[32,2304]{1,0:T(8,128)(2,1)S(1)}, bf16[32,2304]{1,0:T(8,128)(2,1)S(1)}, u32[]{:S(2)}, u32[]{:S(2)}) collective-permute-start(bf16[32,2304]{1,0:T(8,128)(2,1)S(1)} %get-tuple-element.14), channel_id=1, source_target_pairs={{0,2},{32,40},{2,4},{34,42},{4,6},{36,44},{6,0},{38,46},{64,66},{9... | collective-permute-start | bytes 442376 | tf_op jit(solution)/shard_map/ppermute | solution.py:32
  87.1 4.0 %collective-permute-start.19 = (bf16[32,2304]{1,0:T(8,128)(2,1)S(1)}, bf16[32,2304]{1,0:T(8,128)(2,1)S(1)}, u32[]{:S(2)}, u32[]{:S(2)}) collective-permute-start(bf16[32,2304]{1,0:T(8,128)(2,1)S(1)} %get-tuple-element.15), channel_id=1, source_target_pairs={{0,6},{32,56},{2,0},{34,58},{4,2},{36,60},{6,4},{38,62},{64,70},{9... | collective-permute-start | bytes 442376 | tf_op jit(solution)/shard_map/ppermute | solution.py:32
  88.4 5.5 %collective-permute-start.18 = (bf16[32,2304]{1,0:T(8,128)(2,1)S(1)}, bf16[32,2304]{1,0:T(8,128)(2,1)S(1)}, u32[]{:S(2)}, u32[]{:S(2)}) collective-permute-start(bf16[32,2304]{1,0:T(8,128)(2,1)S(1)} %get-tuple-element.16), channel_id=1, source_target_pairs={{0,4},{32,48},{2,6},{34,50},{4,0},{36,52},{6,2},{38,54},{64,68},{9... | collective-permute-start | bytes 442376 | tf_op jit(solution)/shard_map/ppermute | solution.py:32
  93.9 5.3 %collective-permute-start.22 = (bf16[32,2304]{1,0:T(8,128)(2,1)S(1)}, bf16[32,2304]{1,0:T(8,128)(2,1)S(1)}, u32[]{:S(2)}, u32[]{:S(2)}) collective-permute-start(bf16[32,2304]{1,0:T(8,128)(2,1)S(1)} %add_convert_fusion.2), channel_id=1, source_target_pairs={{0,64},{32,96},{2,66},{34,98},{4,68},{36,100},{6,70},{38,102},{64,... | collective-permute-start | bytes 442376 | tf_op jit(solution)/shard_map/ppermute | solution.py:32
  94.0 5.2 %collective-permute-start.20 = (bf16[32,2304]{1,0:T(8,128)(2,1)S(1)}, bf16[32,2304]{1,0:T(8,128)(2,1)S(1)}, u32[]{:S(2)}, u32[]{:S(2)}) collective-permute-start(bf16[32,2304]{1,0:T(8,128)(2,1)S(1)} %add_convert_fusion.2), channel_id=1, source_target_pairs={{0,65},{32,97},{2,67},{34,99},{4,69},{36,101},{6,71},{38,103},{64,... | collective-permute-start | bytes 442376 | tf_op jit(solution)/shard_map/ppermute | solution.py:32
  96.7 5.6 %collective-permute-start.21 = (bf16[32,2304]{1,0:T(8,128)(2,1)S(1)}, bf16[32,2304]{1,0:T(8,128)(2,1)S(1)}, u32[]{:S(2)}, u32[]{:S(2)}) collective-permute-start(bf16[32,2304]{1,0:T(8,128)(2,1)S(1)} %add_convert_fusion.2), channel_id=1, source_target_pairs={{0,1},{32,33},{2,3},{34,35},{4,5},{36,37},{6,7},{38,39},{64,65},{9... | collective-permute-start | bytes 442376 | tf_op jit(solution)/shard_map/ppermute | solution.py:32
  102.4 5.3 %collective-permute-start.25 = (bf16[32,2304]{1,0:T(8,128)(2,1)S(1)}, bf16[32,2304]{1,0:T(8,128)(2,1)S(1)}, u32[]{:S(2)}, u32[]{:S(2)}) collective-permute-start(bf16[32,2304]{1,0:T(8,128)(2,1)S(1)} %get-tuple-element.4), channel_id=1, source_target_pairs={{0,2},{32,40},{2,4},{34,42},{4,6},{36,44},{6,0},{38,46},{64,66},{9... | collective-permute-start | bytes 442376 | tf_op jit(solution)/shard_map/ppermute | solution.py:32
  102.9 6.3 %collective-permute-start.24 = (bf16[32,2304]{1,0:T(8,128)(2,1)S(1)}, bf16[32,2304]{1,0:T(8,128)(2,1)S(1)}, u32[]{:S(2)}, u32[]{:S(2)}) collective-permute-start(bf16[32,2304]{1,0:T(8,128)(2,1)S(1)} %get-tuple-element.4), channel_id=1, source_target_pairs={{0,4},{32,48},{2,6},{34,50},{4,0},{36,52},{6,2},{38,54},{64,68},{9... | collective-permute-start | bytes 442376 | tf_op jit(solution)/shard_map/ppermute | solution.py:32
  105.2 4.7 %collective-permute-start.23 = (bf16[32,2304]{1,0:T(8,128)(2,1)S(1)}, bf16[32,2304]{1,0:T(8,128)(2,1)S(1)}, u32[]{:S(2)}, u32[]{:S(2)}) collective-permute-start(bf16[32,2304]{1,0:T(8,128)(2,1)S(1)} %get-tuple-element.4), channel_id=1, source_target_pairs={{0,6},{32,56},{2,0},{34,58},{4,2},{36,60},{6,4},{38,62},{64,70},{9... | collective-permute-start | bytes 442376 | tf_op jit(solution)/shard_map/ppermute | solution.py:32
  109.9 19.1 %collective-permute-start.28 = (bf16[128,2304]{1,0:T(8,128)(2,1)S(1)}, bf16[128,2304]{1,0:T(8,128)(2,1)S(1)}, u32[]{:S(2)}, u32[]{:S(2)}) collective-permute-start(bf16[128,2304]{1,0:T(8,128)(2,1)S(1)} %pad_maximum_fusion.19), channel_id=1, source_target_pairs={{0,8},{32,34},{2,10},{34,36},{4,12},{36,38},{6,14},{38,32},{64,72}... | collective-permute-start | bytes 1769480 | tf_op jit(solution)/shard_map/ppermute | solution.py:32
  112.0 16.9 %collective-permute-start.27 = (bf16[128,2304]{1,0:T(8,128)(2,1)S(1)}, bf16[128,2304]{1,0:T(8,128)(2,1)S(1)}, u32[]{:S(2)}, u32[]{:S(2)}) collective-permute-start(bf16[128,2304]{1,0:T(8,128)(2,1)S(1)} %pad_maximum_fusion.19), channel_id=1, source_target_pairs={{0,16},{32,36},{2,18},{34,38},{4,20},{36,32},{6,22},{38,34},{64,80... | collective-permute-start | bytes 1769480 | tf_op jit(solution)/shard_map/ppermute | solution.py:32
  115.1 13.5 %collective-permute-start.26 = (bf16[128,2304]{1,0:T(8,128)(2,1)S(1)}, bf16[128,2304]{1,0:T(8,128)(2,1)S(1)}, u32[]{:S(2)}, u32[]{:S(2)}) collective-permute-start(bf16[128,2304]{1,0:T(8,128)(2,1)S(1)} %pad_maximum_fusion.19), channel_id=1, source_target_pairs={{0,24},{32,38},{2,26},{34,32},{4,28},{36,34},{6,30},{38,36},{64,88... | collective-permute-start | bytes 1769480 | tf_op jit(solution)/shard_map/ppermute | solution.py:32
  129.0 10.1 %collective-permute-start.29 = (bf16[512,2304]{1,0:T(8,128)(2,1)S(1)}, bf16[512,2304]{1,0:T(8,128)(2,1)S(1)}, u32[]{:S(2)}, u32[]{:S(2)}) collective-permute-start(bf16[512,2304]{1,0:T(8,128)(2,1)S(1)} %constant_dynamic-update-slice_fusion.7), channel_id=1, source_target_pairs={{0,32},{32,0},{2,34},{34,2},{4,36},{36,4},{6,38},{38,6},{64,96},{9... | collective-permute-start | bytes 7077896 | tf_op jit(solution)/shard_map/ppermute | solution.py:32
  (6 other events, 25.9 us)

commit v2 on v1

v2 whole, which is shorter than its diff:
```python
import jax
import jax.numpy as jnp
from jax import lax
from jax.sharding import PartitionSpec as P

sparsity_weight = 4.0
norm_epsilon = 1e-06
TOKENS = 512
D = 4608
HALF = D // 2
AXES = ("prod", "sae")
bf16 = jnp.bfloat16
f32 = jnp.float32


def place(x, y, z, c):
    return ((y % 2) * 2 + c) * 32 + (x * 4 + z) * 2 + y // 2


def route(step):
    pairs = []
    for x in range(4):
        for y in range(4):
            for z in range(4):
                for c in range(2):
                    tx, ty, tz, tc = step(x, y, z, c)
                    pairs.append((place(x, y, z, c), place(tx % 4, ty % 4, tz % 4, tc % 2)))
    return pairs


def move(value, step):
    return lax.ppermute(value, AXES, route(step))


def to_core(value):
    return move(value, lambda x, y, z, c: (x, y, z, 1 - c))


def to_major(value, d):
    return move(value, lambda x, y, z, c: (x + d, y, z, c) if c == 0 else (x, y, z + d, c))


def team(members):
    found = {}
    for x in range(4):
        for y in range(4):
            for z in range(4):
                for c in range(2):
                    group, rank = members(x, y, z, c)
                    found.setdefault(group, []).append((rank, place(x, y, z, c)))
    return [[device for _, device in sorted(found[g])] for g in sorted(found)]


def axis_pair(x, z, c):
    return (x, z) if c == 0 else (z, x)


def team8(x, y, z, c):
    major, minor = axis_pair(x, z, c)
    return (c, major, y % 2), (minor, y // 2)


def team16(x, y, z, c):
    major, minor = axis_pair(x, z, c)
    return (c, major), (minor, y)


def exchange(value, members):
    return lax.all_to_all(
        value, AXES, 0, 0, axis_index_groups=team(members), tiled=True
    )


def gather(value, to):
    return [value] + [to(value, -d) for d in (1, 2, 3)]


def swap_blocks(value):
    return value.reshape(4, 4, 32, value.shape[-1]).transpose(1, 0, 2, 3).reshape(value.shape)


def turn(value, by):
    blocks = value.reshape(4, 32, value.shape[-1])
    blocks = lax.dynamic_slice_in_dim(jnp.concatenate([blocks, blocks]), by, 4)
    return blocks.reshape(value.shape)


def local(
    head_outputs,
    out_weight,
    residual_input,
    post_gain,
    encoder_weight,
    encoder_bias,
    decoder_weight,
    decoder_bias,
):
    here = lax.axis_index("prod")
    there = lax.axis_index("sae")
    low = here // 2 == 0
    core = here % 2
    first = core == 0
    minor = jnp.where(first, there // 2 % 4, there // 8)

    def own_half(v):
        return jnp.where(first, v[..., :HALF], v[..., HALF:])

    def other_half(v):
        return jnp.where(first, v[..., HALF:], v[..., :HALF])

    encoder_own = lax.dynamic_slice_in_dim(encoder_weight, core * HALF, HALF, 0)
    encoder_other = lax.dynamic_slice_in_dim(encoder_weight, (1 - core) * HALF, HALF, 0)
    decoder_own = own_half(decoder_weight)
    decoder_other = other_half(decoder_weight)

    partial_value = jnp.dot(head_outputs, out_weight, preferred_element_type=f32)
    both = own_half(partial_value) + to_core(other_half(partial_value))
    projected = both + lax.ppermute(both, "prod", [(0, 2), (2, 0), (1, 3), (3, 1)])
    squares = jnp.broadcast_to(jnp.sum(projected * projected, axis=1, keepdims=True), (16, 128))
    squares = (squares + to_core(squares))[:, :1]
    gain = own_half(post_gain)
    normed = projected * lax.rsqrt(squares / D + norm_epsilon) * gain
    stream = (own_half(residual_input).astype(f32) + normed).astype(bf16)

    bias_own = own_half(decoder_bias)
    centred = (stream.astype(f32) - bias_own).astype(bf16)
    centred = exchange(jnp.broadcast_to(centred, (8, 16, HALF)), team8)
    centred = turn(centred.reshape(128, HALF), minor)
    centred_own = gather(centred, to_major)
    centred_other = jnp.concatenate([to_core(piece) for piece in centred_own])
    centred_own = jnp.concatenate(centred_own)

    def whole(own, other):
        other = swap_blocks(other)
        return jnp.concatenate(
            [jnp.where(first, own, other), jnp.where(first, other, own)], axis=1
        )

    preact = jnp.dot(centred_own, encoder_own, preferred_element_type=f32)
    preact = preact + swap_blocks(
        jnp.dot(centred_other, encoder_other, preferred_element_type=f32)
    )
    rectified = jnp.maximum(preact + encoder_bias, 0.0)
    activations = jnp.square(rectified).astype(bf16)
    swapped = swap_blocks(activations)

    pieces = []
    for d in range(4):
        rows = slice(128 * d, 128 * d + 128)
        got = jnp.dot(swapped[rows], decoder_other, preferred_element_type=f32).astype(bf16)
        mine = jnp.dot(activations[rows], decoder_own, preferred_element_type=f32)
        piece = (mine + to_core(got).astype(f32)).astype(bf16)
        pieces.append(to_major(piece, d) if d else piece)
    recon = sum(piece.astype(f32) for piece in pieces).astype(bf16)
    recon = exchange(turn(recon, (4 - minor) % 4).reshape(16, 8, HALF), team16)
    summed = jnp.sum(recon.astype(f32), axis=0)
    own_stream = jnp.where(low, stream[:8], stream[8:])
    grad_recon = (2.0 * (summed + bias_own - own_stream.astype(f32)) / TOKENS).astype(bf16)

    errors = exchange(jnp.broadcast_to(grad_recon, (16, 8, HALF)), team16)
    errors = turn(errors.reshape(128, HALF), minor)
    errors_own = gather(errors, to_major)
    errors_other = jnp.concatenate([to_core(piece) for piece in errors_own])
    errors_own = jnp.concatenate(errors_own)
    all_errors = whole(errors_own, errors_other)
    centred = whole(centred_own, centred_other)

    decoder_wide = decoder_weight.astype(f32)
    row_norms = jnp.sqrt(jnp.sum(decoder_wide * decoder_wide, axis=1) + norm_epsilon)
    grad_acts = jnp.einsum("td,ld->tl", errors_own, decoder_own, preferred_element_type=f32)
    grad_acts = grad_acts + swap_blocks(
        jnp.einsum("td,ld->tl", errors_other, decoder_other, preferred_element_type=f32)
    )
    grad_acts = grad_acts + sparsity_weight * row_norms / TOKENS
    grad_pre = (grad_acts * 2.0 * rectified).astype(bf16)
    grad_encoder = jnp.einsum("td,tl->dl", centred, grad_pre, preferred_element_type=f32)
    grad_encoder_bias = jnp.sum(grad_pre.astype(f32), axis=0)
    act_sum = jnp.sum(activations.astype(f32), axis=0)
    grad_decoder = jnp.einsum("tl,td->ld", activations, all_errors, preferred_element_type=f32)
    grad_decoder = (
        grad_decoder + sparsity_weight / TOKENS * (act_sum / row_norms)[:, None] * decoder_wide
    )
    return (grad_encoder.astype(bf16), grad_encoder_bias, grad_decoder.astype(bf16))


def solution(mesh):
    placed = (
        P("sae", "prod"),
        P("prod", None),
        P("sae", None),
        P(),
        P(None, ("prod", "sae")),
        P(("prod", "sae")),
        P(("prod", "sae"), None),
        P(),
    )
    return jax.shard_map(
        local,
        mesh=mesh,
        in_specs=placed,
        out_specs=(P(None, ("prod", "sae")), P(("prod", "sae")), P(("prod", "sae"), None)),
        check_vma=False,
    )
```

time: 155 us -> 171 us (1.10); the launches traced: 152 us -> 170 us
  waiting for transfers between devices: 74.3 us -> 54.4 us
  other arithmetic: 3.93 us -> 17.4 us
  blocking collectives: 0 us -> 12.5 us
  matrix products: 21.3 us -> 31.5 us
  local copies, waits for them, and re-layouts: 2.11 us -> 6.01 us
  starting transfers between devices: 49.9 us -> 47.3 us
    ppermute x29 -> x23, waiting for transfers between devices: 72.4 us -> 32.3 us  [move(): return lax.ppermute(value, AXES, route(step))]
    all_to_all x0 -> x2, waiting for transfers between devices: none -> 18.4 us  [exchange(): lax.all_to_all(value, AXES, 0, 0, axis_index_groups=team(members), tiled=...]
    ppermute x29 -> x23, starting transfers between devices: 48.4 us -> 34.6 us  [move(): return lax.ppermute(value, AXES, route(step))]
    all_to_all x0 -> x1, blocking collectives: none -> 12.5 us  [exchange(): lax.all_to_all(value, AXES, 0, 0, axis_index_groups=team(members), tiled=...]
    all_to_all x0 -> x2, starting transfers between devices: none -> 11.3 us  [exchange(): lax.all_to_all(value, AXES, 0, 0, axis_index_groups=team(members), tiled=...]
    dot_general x4 -> x13, matrix products: 11.8 us -> 22 us  [the longest x4 4.59 us: local(): mine = jnp.dot(activations[rows], decoder_own, preferred_element_type=f32)]
    select_n x2, other arithmetic: 0.01 us -> 4.09 us  [own_half(): return jnp.where(first, v[..., :HALF], v[..., HALF:])]
    unnamed x26 -> x52, local copies, waits for them, and re-layouts: 0.63 us -> 4.52 us
  transfers between devices with their start and end apart: 30 -> 26, of which waited for: 26 -> 13; matrix products, arithmetic and copies ran while one was open for 1% -> 12% of each run, Pallas kernels for 0% -> 0%
where the time goes in v2:
time: 171 us; the launch traced here: 170 us
  waiting for transfers between devices  54.4 us (32%)
  starting transfers between devices  47.3 us (28%)
  matrix products  31.5 us (18%)
  other arithmetic  17.4 us (10%)
  blocking collectives  12.5 us (7%)
  local copies, waits for them, and re-layouts  6.01 us (4%)
    ppermute x23, starting transfers between devices, move(): return lax.ppermute(value, AXES, route(step))  34.6 us
    ppermute x23, waiting for transfers between devices, move(): return lax.ppermute(value, AXES, route(step))  32.3 us
    all_to_all x2, waiting for transfers between devices, exchange(): lax.all_to_all(value, AXES, 0, 0, axis_index_groups=team(members), tiled=...  18.4 us
    all_to_all x1, blocking collectives, exchange(): lax.all_to_all(value, AXES, 0, 0, axis_index_groups=team(members), tiled=...  12.5 us
    all_to_all x2, starting transfers between devices, exchange(): lax.all_to_all(value, AXES, 0, 0, axis_index_groups=team(members), tiled=...  11.3 us
    dot_general x1, matrix products, local(): jnp.einsum('tl,td->ld', activations, all_errors, preferred_element_type=f32)  5.16 us
    select_n x2, other arithmetic, whole(): jnp.where(first, own, other)  4.7 us
    dot_general x4, matrix products, local(): mine = jnp.dot(activations[rows], decoder_own, preferred_element_type=f32)  4.59 us
  transfers between devices with their start and end apart: 26, of which 13 were waited for; matrix products, arithmetic and copies ran while one was open for 12% of the time, Pallas kernels for 0%

profile of v2, /device:TPU:1, one launch (start us, length us, event | category | flops | bytes accessed | tf_op | source)
XLA Modules:
  0.0 170.3 jit_solution(9144019781869137851)
XLA Ops:
  1.4 3.1 %fusion.46 = f32[16,4608]{1,0:T(8,128)S(1)} fusion(bf16[16,512]{1,0:T(8,128)(2,1)S(1)} %copy-done, bf16[512,4608]{1,0:T(8,128)(2,1)} %param.9), kind=kOutput, calls=%fused_computation.92 | convolution fusion | flops 75497472 | bytes 5029888 | tf_op jit(solution)/shard_map/dot_general | solution.py:116
  4.5 1.5 collective-permute-start
  7.0 1.5 collective-permute-start.1
  8.5 3.7 %collective-permute-done.1 = f32[16,2304]{1,0:T(8,128)S(1)} collective-permute-done((f32[16,2304]{1,0:T(8,128)S(1)}, f32[16,2304]{1,0:T(8,128)S(1)}, u32[]{:S(2)}, u32[]{:S(2)}) %collective-permute-start.1) | collective-permute-done | bytes 147488 | tf_op jit(solution)/shard_map/ppermute | solution.py:118
  16.1 6.7 %all-to-all-start = ((bf16[8,16,2304]{2,1,0:T(8,128)(2,1)}), bf16[8,16,2304]{2,1,0:T(8,128)(2,1)S(1)}, u32[]{:S(2)}, u32[]{:S(2)}) async-start(bf16[8,16,2304]{2,1,0:T(8,128)(2,1)} %broadcast_in_dim.7), calls=%async_computation | async-start | bytes 1179648 | tf_op jit(solution)/shard_map/all_to_all | solution.py:69
  22.8 9.0 %all-to-all-done = bf16[8,16,2304]{2,1,0:T(8,128)(2,1)S(1)} async-done(((bf16[8,16,2304]{2,1,0:T(8,128)(2,1)}), bf16[8,16,2304]{2,1,0:T(8,128)(2,1)S(1)}, u32[]{:S(2)}, u32[]{:S(2)}) %all-to-all-start) | async-done | bytes 589856 | tf_op jit(solution)/shard_map/all_to_all | solution.py:69
  32.0 3.8 %collective-permute-start.3 = (bf16[128,2304]{1,0:T(8,128)(2,1)S(1)}, bf16[128,2304]{1,0:T(8,128)(2,1)S(1)}, u32[]{:S(2)}, u32[]{:S(2)}) collective-permute-start(bf16[128,2304]{1,0:T(8,128)(2,1)S(1)} %bitcast.78), channel_id=1, source_target_pairs={{0,24},{32,38},{2,26},{34,32},{4,28},{36,34},{6,30},{38,36},{64,88... | collective-permute-start | bytes 1769480 | tf_op jit(solution)/shard_map/ppermute | solution.py:32
  35.9 4.5 %collective-permute-start.6 = (bf16[128,2304]{1,0:T(8,128)(2,1)S(1)}, bf16[128,2304]{1,0:T(8,128)(2,1)}, u32[]{:S(2)}, u32[]{:S(2)}) collective-permute-start(bf16[128,2304]{1,0:T(8,128)(2,1)S(1)} %bitcast.79), channel_id=1, source_target_pairs={{0,32},{32,0},{2,34},{34,2},{4,36},{36,4},{6,38},{38,6},{64,96},{9... | collective-permute-start | bytes 1769480 | tf_op jit(solution)/shard_map/ppermute | solution.py:32
  41.1 7.9 %collective-permute-done.3 = bf16[128,2304]{1,0:T(8,128)(2,1)S(1)} collective-permute-done((bf16[128,2304]{1,0:T(8,128)(2,1)S(1)}, bf16[128,2304]{1,0:T(8,128)(2,1)S(1)}, u32[]{:S(2)}, u32[]{:S(2)}) %collective-permute-start.3) | collective-permute-done | bytes 589856 | tf_op jit(solution)/shard_map/ppermute | solution.py:32
  49.0 5.1 %collective-permute-start.7 = (bf16[128,2304]{1,0:T(8,128)(2,1)S(1)}, bf16[128,2304]{1,0:T(8,128)(2,1)}, u32[]{:S(2)}, u32[]{:S(2)}) collective-permute-start(bf16[128,2304]{1,0:T(8,128)(2,1)S(1)} %collective-permute-done.3), channel_id=1, source_target_pairs={{0,32},{32,0},{2,34},{34,2},{4,36},{36,4},{6,38},{38,6},{64,96},{9... | collective-permute-start | bytes 1769480 | tf_op jit(solution)/shard_map/ppermute | solution.py:32
  54.1 4.1 %broadcast_select_fusion.1 = (bf16[512,2304]{1,0:T(8,128)(2,1)S(1)}, bf16[512,2304]{1,0:T(8,128)(2,1)}) fusion(pred[]{:T(512)S(6)} %eq.10, bf16[512,4608]{1,0:T(8,128)(2,1)} %param.14), kind=kLoop, calls=%fused_computation.27 | loop fusion | flops 2359296 | bytes 9437185 | tf_op jit(solution)/shard_map/jit(_where)/select_n | solution.py:106
  61.4 3.9 %fusion.9 = f32[512,512]{1,0:T(8,128)S(1)} fusion(bf16[512,2304]{1,0:T(8,128)(2,1)S(1)} %constant_dynamic-update-slice_fusion, bf16[4608,512]{1,0:T(8,128)(2,1)} %param.12, s32[]{:T(128)S(6)} %select_n.124), kind=kOutput, calls=%fused_computation.22 | convolution fusion | flops 1207959552 | bytes 5767172 | tf_op jit(solution)/shard_map/dot_general | solution.py:141
  65.5 4.0 %convert_reduce_fusion.1 = (f32[512]{0:T(512)S(1)}, bf16[512,512]{1,0:T(8,128)(2,1)S(1)}, f32[512,512]{1,0:T(8,128)}) fusion(f32[512]{0:T(512)S(1)} %copy-done.16, f32[4,4,32,512]{3,2,0,1:T(8,128)S(1)} %copy.12, bf16[4608,512]{1,0:T(8,128)(2,1)S(1)} %bitcast.102, s32[]{:T(128)S(6)} %select_n.123, bf16[128,2304]{1,0:T(8,128)(2,1)} %collective-permute-done.5, ...), kind=kOutput, calls=%fused_computation.48 | convolution fusion | flops 1219231232 | bytes 7344132 | tf_op jit(solution)/shard_map/dot_general | solution.py:139
  77.7 1.4 add_convert_fusion.3
  79.7 4.6 %collective-permute-done.16 = bf16[128,2304]{1,0:T(8,128)(2,1)} collective-permute-done((bf16[128,2304]{1,0:T(8,128)(2,1)}, bf16[128,2304]{1,0:T(8,128)(2,1)}, u32[]{:S(2)}, u32[]{:S(2)}) %collective-permute-start.16) | collective-permute-done | bytes 589856 | tf_op jit(solution)/shard_map/ppermute | solution.py:32
  84.3 3.1 %collective-permute-done.14 = bf16[128,2304]{1,0:T(8,128)(2,1)} collective-permute-done((bf16[128,2304]{1,0:T(8,128)(2,1)}, bf16[128,2304]{1,0:T(8,128)(2,1)}, u32[]{:S(2)}, u32[]{:S(2)}) %collective-permute-start.14) | collective-permute-done | bytes 589856 | tf_op jit(solution)/shard_map/ppermute | solution.py:32
  87.4 6.3 %collective-permute-done.12 = bf16[128,2304]{1,0:T(8,128)(2,1)} collective-permute-done((bf16[128,2304]{1,0:T(8,128)(2,1)}, bf16[128,2304]{1,0:T(8,128)(2,1)}, u32[]{:S(2)}, u32[]{:S(2)}) %collective-permute-start.12) | collective-permute-done | bytes 589856 | tf_op jit(solution)/shard_map/ppermute | solution.py:32
  93.6 2.0 %add_convert_fusion = bf16[128,2304]{1,0:T(8,128)(2,1)S(1)} fusion(bf16[128,2304]{1,0:T(8,128)(2,1)} %collective-permute-done.16, bf16[128,2304]{1,0:T(8,128)(2,1)} %collective-permute-done.14, bf16[128,2304]{1,0:T(8,128)(2,1)} %collective-permute-done.12, f32[128,2304]{1,0:T(8,128)S(1)} %fusion.34, bf16[128,2304]{1,0:T(8,128)(2,1)} %collective-permute-done.10), kind=kLoop, calls=%fused_computation.35 | loop fusion | flops 3244032 | bytes 4128768 | tf_op jit(solution)/shard_map/convert_element_type | solution.py:154
  96.7 4.6 %all-to-all-start.1 = ((bf16[16,8,2304]{2,1,0:T(8,128)(2,1)}), bf16[16,8,2304]{2,1,0:T(8,128)(2,1)S(1)}, u32[]{:S(2)}, u32[]{:S(2)}) async-start(bf16[16,8,2304]{2,1,0:T(8,128)(2,1)} %bitcast.91), calls=%async_computation.1 | async-start | bytes 1179648 | tf_op jit(solution)/shard_map/all_to_all | solution.py:69
  101.3 9.4 %all-to-all-done.1 = bf16[16,8,2304]{2,1,0:T(8,128)(2,1)S(1)} async-done(((bf16[16,8,2304]{2,1,0:T(8,128)(2,1)}), bf16[16,8,2304]{2,1,0:T(8,128)(2,1)S(1)}, u32[]{:S(2)}, u32[]{:S(2)}) %all-to-all-start.1) | async-done | bytes 589856 | tf_op jit(solution)/shard_map/all_to_all | solution.py:69
  111.6 12.5 %all_to_all.15 = bf16[16,8,2304]{2,1,0:T(8,128)(2,1)S(1)} all-to-all(bf16[16,8,2304]{2,1,0:T(8,128)(2,1)S(1)} %broadcast_in_dim.8), channel_id=1, replica_groups={{0,64,1,65,2,66,3,67,4,68,5,69,6,70,7,71},{8,72,9,73,10,74,11,75,12,76,..., dimensions={0} | all-to-all | bytes 1179648 | tf_op jit(solution)/shard_map/all_to_all | solution.py:69
  125.0 3.4 %fusion = f32[512]{0:T(512)S(1)} fusion(bf16[512,4608]{1,0:T(8,128)(2,1)} %param.14), kind=kLoop, calls=%fused_computation.2 | loop fusion | flops 7077376 | bytes 4720640 | tf_op jit(solution)/shard_map/reduce_sum | solution.py:169
  128.6 6.3 %collective-permute-start.20 = (bf16[128,2304]{1,0:T(8,128)(2,1)S(1)}, bf16[128,2304]{1,0:T(8,128)(2,1)S(1)}, u32[]{:S(2)}, u32[]{:S(2)}) collective-permute-start(bf16[128,2304]{1,0:T(8,128)(2,1)S(1)} %bitcast.85), channel_id=1, source_target_pairs={{0,32},{32,0},{2,34},{34,2},{4,36},{36,4},{6,38},{38,6},{64,96},{9... | collective-permute-start | bytes 1769480 | tf_op jit(solution)/shard_map/ppermute | solution.py:32
  136.3 4.0 %collective-permute-start.21 = (bf16[128,2304]{1,0:T(8,128)(2,1)S(1)}, bf16[128,2304]{1,0:T(8,128)(2,1)S(1)}, u32[]{:S(2)}, u32[]{:S(2)}) collective-permute-start(bf16[128,2304]{1,0:T(8,128)(2,1)S(1)} %collective-permute-done.17), channel_id=1, source_target_pairs={{0,32},{32,0},{2,34},{34,2},{4,36},{36,4},{6,38},{38,6},{64,96},{9... | collective-permute-start | bytes 1769480 | tf_op jit(solution)/shard_map/ppermute | solution.py:32
  140.3 3.6 %bitcast_select_fusion.3 = (bf16[512,2304]{1,0:T(8,128)(2,1)S(1)}, bf16[512,2304]{1,0:T(8,128)(2,1)S(1)}) fusion(bf16[4,4,32,2304]{3,2,0,1:T(8,128)(2,1)S(1)} %copy.11, pred[]{:T(512)S(6)} %eq.10, bf16[128,2304]{1,0:T(8,128)(2,1)} %collective-permute-done.5, bf16[128,2304]{1,0:T(8,128)(2,1)} %collective-permute-done.4, bf16[128,2304]{1,0:T(8,128)(2,1)S(1)} %copy-done.12, ...), kind=kLoop, calls=%fused_computation.21 | loop fusion | flops 11796480 | bytes 9437185 | tf_op jit(solution)/shard_map/jit(_where)/select_n | solution.py:136
  143.9 1.6 collective-permute-done.18
  146.5 5.3 %collective-permute-done.19 = bf16[128,2304]{1,0:T(8,128)(2,1)S(1)} collective-permute-done((bf16[128,2304]{1,0:T(8,128)(2,1)S(1)}, bf16[128,2304]{1,0:T(8,128)(2,1)S(1)}, u32[]{:S(2)}, u32[]{:S(2)}) %collective-permute-start.19) | collective-permute-done | bytes 589856 | tf_op jit(solution)/shard_map/ppermute | solution.py:32
  152.8 1.5 collective-permute-done.23
  154.4 1.4 fusion.47
  157.4 2.2 %convert_reduce_fusion.2 = (f32[512]{0:T(512)}, bf16[512,512]{1,0:T(8,128)(2,1)S(1)}) fusion(f32[512]{0:T(512)S(1)} %copy-done.17, f32[512,512]{1,0:T(8,128)S(1)} %copy-done.18, f32[4,4,32,512]{3,2,0,1:T(8,128)S(1)} %copy-done.9, f32[512]{0:T(512)S(1)} %get-tuple-element.20, f32[4,4,32,512]{3,2,0,1:T(8,128)S(1)} %copy.13, ...), kind=kOutput, calls=%fused_computation.49 | convolution fusion | flops 1220017664 | bytes 8394752 | tf_op jit(solution)/shard_map/td,ld->tl/dot_general | solution.py:170
  159.6 4.3 %convolution_convert_fusion = bf16[4608,512]{1,0:T(8,128)(2,1)} fusion(bf16[512,512]{1,0:T(8,128)(2,1)S(1)} %get-tuple-element.23, bf16[512,2304]{1,0:T(8,128)(2,1)S(1)} %get-tuple-element.12, bf16[512,2304]{1,0:T(8,128)(2,1)S(1)} %get-tuple-element.11), kind=kOutput, calls=%fused_computation.5 | convolution fusion | flops 2427715584 | bytes 9961472 | tf_op jit(solution)/shard_map/td,tl->dl/dot_general | solution.py:176
  165.1 5.2 %fusion.2 = bf16[512,4608]{1,0:T(8,128)(2,1)} fusion(bf16[512,4608]{1,0:T(8,128)(2,1)S(1)} %bitcast.75, bf16[512,512]{1,0:T(8,128)(2,1)S(1)} %copy-done.7, bf16[512,2304]{1,0:T(8,128)(2,1)S(1)} %get-tuple-element.10, bf16[512,2304]{1,0:T(8,128)(2,1)S(1)} %get-tuple-element.9, f32[512]{0:T(512)S(1)} %get-tuple-element.19), kind=kOutput, calls=%fused_computation.4 | convolution fusion | flops 2434793472 | bytes 14682112 | tf_op jit(solution)/shard_map/tl,td->ld/dot_general | solution.py:179
  (117 shorter events, 27.9 us)
Async XLA Ops:
  1.4 12.2 %copy-start.14 = (f32[4608]{0:T(1024)S(1)}, f32[4608]{0:T(1024)}, u32[]{:S(2)}) copy-start(f32[4608]{0:T(1024)} %param.15) | copy-start | bytes 55300
  1.4 12.2 %copy-start.15 = (f32[4608]{0:T(1024)S(1)}, f32[4608]{0:T(1024)}, u32[]{:S(2)}) copy-start(f32[4608]{0:T(1024)} %param.11) | copy-start | bytes 55300
  1.4 13.1 %copy-start.13 = (bf16[16,4608]{1,0:T(8,128)(2,1)S(1)}, bf16[16,4608]{1,0:T(8,128)(2,1)}, u32[]{:S(2)}) copy-start(bf16[16,4608]{1,0:T(8,128)(2,1)} %param.10) | copy-start | bytes 442372
  4.5 2.5 %collective-permute-start = (f32[16,2304]{1,0:T(8,128)S(1)}, f32[16,2304]{1,0:T(8,128)S(1)}, u32[]{:S(2)}, u32[]{:S(2)}) collective-permute-start(f32[16,2304]{1,0:T(8,128)S(1)} %slice_select_fusion), channel_id=1, source_target_pairs={{0,32},{32,0},{2,34},{34,2},{4,36},{36,4},{6,38},{38,6},{64,96},{9... | collective-permute-start | bytes 442376 | tf_op jit(solution)/shard_map/ppermute | solution.py:32
  7.0 5.1 %collective-permute-start.1 = (f32[16,2304]{1,0:T(8,128)S(1)}, f32[16,2304]{1,0:T(8,128)S(1)}, u32[]{:S(2)}, u32[]{:S(2)}) collective-permute-start(f32[16,2304]{1,0:T(8,128)S(1)} %select_add_fusion), channel_id=1, source_target_pairs={{0,64},{64,0},{32,96},{96,32},{1,65},{65,1},{33,97},{97,33},{2,66}... | collective-permute-start | bytes 442376 | tf_op jit(solution)/shard_map/ppermute | solution.py:118
  12.3 2.2 %collective-permute-start.2 = (f32[16,128]{0,1:T(8,128)S(1)}, f32[16,128]{0,1:T(8,128)S(1)}, u32[]{:S(2)}, u32[]{:S(2)}) collective-permute-start(f32[16,128]{0,1:T(8,128)S(1)} %broadcast_in_dim.6), channel_id=1, source_target_pairs={{0,32},{32,0},{2,34},{34,2},{4,36},{36,4},{6,38},{38,6},{64,96},{9... | collective-permute-start | bytes 24584 | tf_op jit(solution)/shard_map/ppermute | solution.py:32
  16.1 15.7 %all-to-all-start = ((bf16[8,16,2304]{2,1,0:T(8,128)(2,1)}), bf16[8,16,2304]{2,1,0:T(8,128)(2,1)S(1)}, u32[]{:S(2)}, u32[]{:S(2)}) async-start(bf16[8,16,2304]{2,1,0:T(8,128)(2,1)} %broadcast_in_dim.7), calls=%async_computation | async-start | bytes 1179648 | tf_op jit(solution)/shard_map/all_to_all | solution.py:69
  32.0 17.0 %collective-permute-start.3 = (bf16[128,2304]{1,0:T(8,128)(2,1)S(1)}, bf16[128,2304]{1,0:T(8,128)(2,1)S(1)}, u32[]{:S(2)}, u32[]{:S(2)}) collective-permute-start(bf16[128,2304]{1,0:T(8,128)(2,1)S(1)} %bitcast.78), channel_id=1, source_target_pairs={{0,24},{32,38},{2,26},{34,32},{4,28},{36,34},{6,30},{38,36},{64,88... | collective-permute-start | bytes 1769480 | tf_op jit(solution)/shard_map/ppermute | solution.py:32
  35.9 22.9 %collective-permute-start.6 = (bf16[128,2304]{1,0:T(8,128)(2,1)S(1)}, bf16[128,2304]{1,0:T(8,128)(2,1)}, u32[]{:S(2)}, u32[]{:S(2)}) collective-permute-start(bf16[128,2304]{1,0:T(8,128)(2,1)S(1)} %bitcast.79), channel_id=1, source_target_pairs={{0,32},{32,0},{2,34},{34,2},{4,36},{36,4},{6,38},{38,6},{64,96},{9... | collective-permute-start | bytes 1769480 | tf_op jit(solution)/shard_map/ppermute | solution.py:32
  40.4 17.9 %collective-permute-start.4 = (bf16[128,2304]{1,0:T(8,128)(2,1)S(1)}, bf16[128,2304]{1,0:T(8,128)(2,1)}, u32[]{:S(2)}, u32[]{:S(2)}) collective-permute-start(bf16[128,2304]{1,0:T(8,128)(2,1)S(1)} %bitcast.80), channel_id=1, source_target_pairs={{0,16},{32,36},{2,18},{34,38},{4,20},{36,32},{6,22},{38,34},{64,80... | collective-permute-start | bytes 1769480 | tf_op jit(solution)/shard_map/ppermute | solution.py:32
  40.8 17.6 %collective-permute-start.5 = (bf16[128,2304]{1,0:T(8,128)(2,1)S(1)}, bf16[128,2304]{1,0:T(8,128)(2,1)}, u32[]{:S(2)}, u32[]{:S(2)}) collective-permute-start(bf16[128,2304]{1,0:T(8,128)(2,1)S(1)} %bitcast.81), channel_id=1, source_target_pairs={{0,8},{32,34},{2,10},{34,36},{4,12},{36,38},{6,14},{38,32},{64,72}... | collective-permute-start | bytes 1769480 | tf_op jit(solution)/shard_map/ppermute | solution.py:32
  49.0 10.8 %collective-permute-start.7 = (bf16[128,2304]{1,0:T(8,128)(2,1)S(1)}, bf16[128,2304]{1,0:T(8,128)(2,1)}, u32[]{:S(2)}, u32[]{:S(2)}) collective-permute-start(bf16[128,2304]{1,0:T(8,128)(2,1)S(1)} %collective-permute-done.3), channel_id=1, source_target_pairs={{0,32},{32,0},{2,34},{34,2},{4,36},{36,4},{6,38},{38,6},{64,96},{9... | collective-permute-start | bytes 1769480 | tf_op jit(solution)/shard_map/ppermute | solution.py:32
  58.2 2.7 %collective-permute-start.8 = (bf16[128,2304]{1,0:T(8,128)(2,1)}, bf16[128,2304]{1,0:T(8,128)(2,1)S(1)}, u32[]{:S(2)}, u32[]{:S(2)}) collective-permute-start(bf16[128,2304]{1,0:T(8,128)(2,1)} %collective-permute-done.4), channel_id=1, source_target_pairs={{0,32},{32,0},{2,34},{34,2},{4,36},{36,4},{6,38},{38,6},{64,96},{9... | collective-permute-start | bytes 1769480 | tf_op jit(solution)/shard_map/ppermute | solution.py:32
  58.4 2.8 %collective-permute-start.9 = (bf16[128,2304]{1,0:T(8,128)(2,1)}, bf16[128,2304]{1,0:T(8,128)(2,1)S(1)}, u32[]{:S(2)}, u32[]{:S(2)}) collective-permute-start(bf16[128,2304]{1,0:T(8,128)(2,1)} %collective-permute-done.5), channel_id=1, source_target_pairs={{0,32},{32,0},{2,34},{34,2},{4,36},{36,4},{6,38},{38,6},{64,96},{9... | collective-permute-start | bytes 1769480 | tf_op jit(solution)/shard_map/ppermute | solution.py:32
  69.5 9.7 %copy-start.6 = (bf16[512,512]{1,0:T(8,128)(2,1)}, bf16[512,512]{1,0:T(8,128)(2,1)S(1)}, u32[]{:S(2)}) copy-start(bf16[512,512]{1,0:T(8,128)(2,1)S(1)} %get-tuple-element.4) | copy-start | bytes 1572868
  70.1 3.5 %collective-permute-start.15 = (bf16[128,2304]{1,0:T(8,128)(2,1)S(1)}, bf16[128,2304]{1,0:T(8,128)(2,1)S(1)}, u32[]{:S(2)}, u32[]{:S(2)}) collective-permute-start(bf16[128,2304]{1,0:T(8,128)(2,1)S(1)} %convolution_convert_fusion.1), channel_id=1, source_target_pairs={{0,32},{32,0},{2,34},{34,2},{4,36},{36,4},{6,38},{38,6},{64,96},{9... | collective-permute-start | bytes 1769480 | tf_op jit(solution)/shard_map/ppermute | solution.py:32
  70.9 4.2 %collective-permute-start.13 = (bf16[128,2304]{1,0:T(8,128)(2,1)S(1)}, bf16[128,2304]{1,0:T(8,128)(2,1)S(1)}, u32[]{:S(2)}, u32[]{:S(2)}) collective-permute-start(bf16[128,2304]{1,0:T(8,128)(2,1)S(1)} %convolution_convert_fusion.2), channel_id=1, source_target_pairs={{0,32},{32,0},{2,34},{34,2},{4,36},{36,4},{6,38},{38,6},{64,96},{9... | collective-permute-start | bytes 1769480 | tf_op jit(solution)/shard_map/ppermute | solution.py:32
  71.7 6.0 %collective-permute-start.11 = (bf16[128,2304]{1,0:T(8,128)(2,1)S(1)}, bf16[128,2304]{1,0:T(8,128)(2,1)S(1)}, u32[]{:S(2)}, u32[]{:S(2)}) collective-permute-start(bf16[128,2304]{1,0:T(8,128)(2,1)S(1)} %convolution_convert_fusion.3), channel_id=1, source_target_pairs={{0,32},{32,0},{2,34},{34,2},{4,36},{36,4},{6,38},{38,6},{64,96},{9... | collective-permute-start | bytes 1769480 | tf_op jit(solution)/shard_map/ppermute | solution.py:32
  73.3 6.4 %collective-permute-start.10 = (bf16[128,2304]{1,0:T(8,128)(2,1)}, bf16[128,2304]{1,0:T(8,128)(2,1)}, u32[]{:S(2)}, u32[]{:S(2)}) collective-permute-start(bf16[128,2304]{1,0:T(8,128)(2,1)} %convolution_convert_fusion.4), channel_id=1, source_target_pairs={{0,32},{32,0},{2,34},{34,2},{4,36},{36,4},{6,38},{38,6},{64,96},{9... | collective-permute-start | bytes 1769480 | tf_op jit(solution)/shard_map/ppermute | solution.py:32
  74.9 9.3 %collective-permute-start.16 = (bf16[128,2304]{1,0:T(8,128)(2,1)}, bf16[128,2304]{1,0:T(8,128)(2,1)}, u32[]{:S(2)}, u32[]{:S(2)}) collective-permute-start(bf16[128,2304]{1,0:T(8,128)(2,1)} %add_convert_fusion.1), channel_id=1, source_target_pairs={{0,24},{32,38},{2,26},{34,32},{4,28},{36,34},{6,30},{38,36},{64,88... | collective-permute-start | bytes 1769480 | tf_op jit(solution)/shard_map/ppermute | solution.py:32
  76.5 10.9 %collective-permute-start.14 = (bf16[128,2304]{1,0:T(8,128)(2,1)}, bf16[128,2304]{1,0:T(8,128)(2,1)}, u32[]{:S(2)}, u32[]{:S(2)}) collective-permute-start(bf16[128,2304]{1,0:T(8,128)(2,1)} %add_convert_fusion.2), channel_id=1, source_target_pairs={{0,16},{32,36},{2,18},{34,38},{4,20},{36,32},{6,22},{38,34},{64,80... | collective-permute-start | bytes 1769480 | tf_op jit(solution)/shard_map/ppermute | solution.py:32
  79.1 14.5 %collective-permute-start.12 = (bf16[128,2304]{1,0:T(8,128)(2,1)}, bf16[128,2304]{1,0:T(8,128)(2,1)}, u32[]{:S(2)}, u32[]{:S(2)}) collective-permute-start(bf16[128,2304]{1,0:T(8,128)(2,1)} %add_convert_fusion.3), channel_id=1, source_target_pairs={{0,8},{32,34},{2,10},{34,36},{4,12},{36,38},{6,14},{38,32},{64,72}... | collective-permute-start | bytes 1769480 | tf_op jit(solution)/shard_map/ppermute | solution.py:32
  96.7 14.0 %all-to-all-start.1 = ((bf16[16,8,2304]{2,1,0:T(8,128)(2,1)}), bf16[16,8,2304]{2,1,0:T(8,128)(2,1)S(1)}, u32[]{:S(2)}, u32[]{:S(2)}) async-start(bf16[16,8,2304]{2,1,0:T(8,128)(2,1)} %bitcast.91), calls=%async_computation.1 | async-start | bytes 1179648 | tf_op jit(solution)/shard_map/all_to_all | solution.py:69
  124.3 12.0 %collective-permute-start.17 = (bf16[128,2304]{1,0:T(8,128)(2,1)S(1)}, bf16[128,2304]{1,0:T(8,128)(2,1)S(1)}, u32[]{:S(2)}, u32[]{:S(2)}) collective-permute-start(bf16[128,2304]{1,0:T(8,128)(2,1)S(1)} %bitcast.84), channel_id=1, source_target_pairs={{0,24},{32,38},{2,26},{34,32},{4,28},{36,34},{6,30},{38,36},{64,88... | collective-permute-start | bytes 1769480 | tf_op jit(solution)/shard_map/ppermute | solution.py:32
  128.4 11.9 %copy-start.12 = (bf16[128,2304]{1,0:T(8,128)(2,1)S(1)}, bf16[128,2304]{1,0:T(8,128)(2,1)}, u32[]{:S(2)}) copy-start(bf16[128,2304]{1,0:T(8,128)(2,1)} %copy-done.10) | copy-start | bytes 1769476
  128.6 24.1 %collective-permute-start.20 = (bf16[128,2304]{1,0:T(8,128)(2,1)S(1)}, bf16[128,2304]{1,0:T(8,128)(2,1)S(1)}, u32[]{:S(2)}, u32[]{:S(2)}) collective-permute-start(bf16[128,2304]{1,0:T(8,128)(2,1)S(1)} %bitcast.85), channel_id=1, source_target_pairs={{0,32},{32,0},{2,34},{34,2},{4,36},{36,4},{6,38},{38,6},{64,96},{9... | collective-permute-start | bytes 1769480 | tf_op jit(solution)/shard_map/ppermute | solution.py:32
  134.9 10.6 %collective-permute-start.18 = (bf16[128,2304]{1,0:T(8,128)(2,1)S(1)}, bf16[128,2304]{1,0:T(8,128)(2,1)S(1)}, u32[]{:S(2)}, u32[]{:S(2)}) collective-permute-start(bf16[128,2304]{1,0:T(8,128)(2,1)S(1)} %bitcast.86), channel_id=1, source_target_pairs={{0,16},{32,36},{2,18},{34,38},{4,20},{36,32},{6,22},{38,34},{64,80... | collective-permute-start | bytes 1769480 | tf_op jit(solution)/shard_map/ppermute | solution.py:32
  135.9 15.8 %collective-permute-start.19 = (bf16[128,2304]{1,0:T(8,128)(2,1)S(1)}, bf16[128,2304]{1,0:T(8,128)(2,1)S(1)}, u32[]{:S(2)}, u32[]{:S(2)}) collective-permute-start(bf16[128,2304]{1,0:T(8,128)(2,1)S(1)} %bitcast.87), channel_id=1, source_target_pairs={{0,8},{32,34},{2,10},{34,36},{4,12},{36,38},{6,14},{38,32},{64,72}... | collective-permute-start | bytes 1769480 | tf_op jit(solution)/shard_map/ppermute | solution.py:32
  136.3 16.4 %collective-permute-start.21 = (bf16[128,2304]{1,0:T(8,128)(2,1)S(1)}, bf16[128,2304]{1,0:T(8,128)(2,1)S(1)}, u32[]{:S(2)}, u32[]{:S(2)}) collective-permute-start(bf16[128,2304]{1,0:T(8,128)(2,1)S(1)} %collective-permute-done.17), channel_id=1, source_target_pairs={{0,32},{32,0},{2,34},{34,2},{4,36},{36,4},{6,38},{38,6},{64,96},{9... | collective-permute-start | bytes 1769480 | tf_op jit(solution)/shard_map/ppermute | solution.py:32
  143.9 10.5 %copy-start.3 = (bf16[512,2304]{1,0:T(8,128)(2,1)S(1)}, bf16[512,2304]{1,0:T(8,128)(2,1)}, u32[]{:S(2)}) copy-start(bf16[512,2304]{1,0:T(8,128)(2,1)} %get-tuple-element.14) | copy-start | bytes 7077892
  145.5 7.3 %collective-permute-start.22 = (bf16[128,2304]{1,0:T(8,128)(2,1)S(1)}, bf16[128,2304]{1,0:T(8,128)(2,1)S(1)}, u32[]{:S(2)}, u32[]{:S(2)}) collective-permute-start(bf16[128,2304]{1,0:T(8,128)(2,1)S(1)} %collective-permute-done.18), channel_id=1, source_target_pairs={{0,32},{32,0},{2,34},{34,2},{4,36},{36,4},{6,38},{38,6},{64,96},{9... | collective-permute-start | bytes 1769480 | tf_op jit(solution)/shard_map/ppermute | solution.py:32
  151.7 2.6 %collective-permute-start.23 = (bf16[128,2304]{1,0:T(8,128)(2,1)S(1)}, bf16[128,2304]{1,0:T(8,128)(2,1)S(1)}, u32[]{:S(2)}, u32[]{:S(2)}) collective-permute-start(bf16[128,2304]{1,0:T(8,128)(2,1)S(1)} %collective-permute-done.19), channel_id=1, source_target_pairs={{0,32},{32,0},{2,34},{34,2},{4,36},{36,4},{6,38},{38,6},{64,96},{9... | collective-permute-start | bytes 1769480 | tf_op jit(solution)/shard_map/ppermute | solution.py:32
  (17 other events, 66.1 us)

commit v3 on v1

v3 whole, which is shorter than its diff:
```python
import functools

import jax
import jax.numpy as jnp
from jax import lax
from jax.experimental import pallas as pl
from jax.experimental.pallas import tpu as pltpu
from jax.sharding import PartitionSpec as P

sparsity_weight = 4.0
norm_epsilon = 1e-06
TOKENS = 512
D = 4608
HALF = D // 2
AXES = ("prod", "sae")
STEP = 768
VMEM = pltpu.VMEM
bf16 = jnp.bfloat16
f32 = jnp.float32


def place(x, y, z, c):
    return ((y % 2) * 2 + c) * 32 + (x * 4 + z) * 2 + y // 2


def route(step):
    pairs = []
    for x in range(4):
        for y in range(4):
            for z in range(4):
                for c in range(2):
                    tx, ty, tz, tc = step(x, y, z, c)
                    pairs.append((place(x, y, z, c), place(tx % 4, ty % 4, tz % 4, tc % 2)))
    return pairs


def move(value, step):
    return lax.ppermute(value, AXES, route(step))


def to_core(value):
    return move(value, lambda x, y, z, c: (x, y, z, 1 - c))


def to_major(value, d):
    return move(value, lambda x, y, z, c: (x + d, y, z, c) if c == 0 else (x, y, z + d, c))


def to_middle(value, d):
    return move(value, lambda x, y, z, c: (x, y + d, z, c))


def to_minor(value, d):
    return move(value, lambda x, y, z, c: (x, y, z + d, c) if c == 0 else (x + d, y, z, c))


def gather(value, to):
    return [value] + [to(value, -d) for d in (1, 2, 3)]


def swap_blocks(value):
    return value.reshape(4, 4, 32, value.shape[-1]).transpose(1, 0, 2, 3).reshape(value.shape)


def cut_kernel(axis, half_ref, after_ref, weight_ref, out_ref, sems):
    start, rows = half_ref[0] * HALF, out_ref.shape[0] // 4
    copies = []
    for i in range(4):
        if axis == 0:
            part = weight_ref.at[pl.ds(pl.multiple_of(start + i * rows, rows), rows), :]
        else:
            part = weight_ref.at[pl.ds(i * rows, rows), pl.ds(pl.multiple_of(start, HALF), HALF)]
        out = out_ref.at[pl.ds(i * rows, rows), :]
        copies.append(pltpu.make_async_copy(part, out, sems.at[i]))
        copies[-1].start()
    for copy in copies:
        copy.wait()


def cut(weight, axis, half, after):
    shape = (HALF, weight.shape[1]) if axis == 0 else (weight.shape[0], HALF)
    ins = [(half, pltpu.SMEM), (after, None), (weight, None)]
    kernel = functools.partial(cut_kernel, axis)
    scratch = [pltpu.SemaphoreType.DMA((4,))]
    return call(kernel, [(shape, bf16, VMEM)], ins, scratch, 4, 0, weight.size * 2)[0]


def call(kernel, outs, ins, scratch, mib, flops, data, **more):
    def spec(space):
        return pl.BlockSpec(memory_space=pl.ANY if space is None else space)

    return pl.pallas_call(
        kernel,
        out_shape=tuple(jax.ShapeDtypeStruct(shape, dtype) for shape, dtype, _ in outs),
        in_specs=[spec(space) for _, space in ins],
        out_specs=tuple(spec(space) for *_, space in outs),
        scratch_shapes=scratch,
        compiler_params=pltpu.CompilerParams(vmem_limit_bytes=mib * 2**20),
        cost_estimate=pl.CostEstimate(flops=flops, bytes_accessed=data, transcendentals=0),
        **more,
    )(*(value for value, _ in ins))


def flip_kernel(*refs):
    pieces, squares, (_, out, *square_outs) = refs[:4], refs[4:6], refs[6:]
    for k, piece in enumerate(pieces):

        def tile(j, carry, piece=piece, column=128 * k):
            rows = pl.ds(pl.multiple_of(j * 256, 256), 256)
            out[rows, column : column + 128] = piece[:, rows].T
            return carry

        lax.fori_loop(0, HALF // 256, tile, 0)
    for square, square_out in zip(squares, square_outs):
        for i in range(4):
            square_out[:, 128 * i : 128 * i + 128] = square[128 * i : 128 * i + 128, :].T


def flip(pieces, squares, after):
    ins = [(v, VMEM) for v in pieces + squares] + [(after, None)]
    outs = [((HALF, TOKENS), bf16, VMEM)] + [((TOKENS, TOKENS), bf16, VMEM)] * 2
    return call(flip_kernel, outs, ins, [], 8, 0, 6 * 2**20)


def rows_kernel(core, _, weight, act, own, other, factor, penalty, sems):
    copies = []
    for k, out in enumerate((own, other)):
        half = core[0] if k == 0 else 1 - core[0]
        for i in range(4):
            span = slice(128 * i, 128 * i + 128)
            columns = pl.ds(pl.multiple_of(half * HALF, HALF), HALF)
            copies.append(
                pltpu.make_async_copy(
                    weight.at[span, columns], out.at[span, :], sems.at[k, i]
                )
            )
            copies[-1].start()
    for copy in copies:
        copy.wait()
    squares = jnp.zeros((TOKENS, 128), f32)
    for out in (own, other):
        for j in range(HALF // 128):
            wide = out[:, 128 * j : 128 * j + 128].astype(f32)
            squares = squares + wide * wide
    norms = jnp.sqrt(jnp.sum(squares, axis=1, keepdims=True) + norm_epsilon)
    act_sum = jnp.sum(act[...].astype(f32), axis=1, keepdims=True)
    factor[...] = sparsity_weight / TOKENS * (act_sum / norms)
    norms = jnp.broadcast_to(sparsity_weight * norms / TOKENS, (TOKENS, 128))
    penalty[...] = norms.T[:1, :]


def decoder_rows(core, after, weight, act):
    ins = [(core, pltpu.SMEM), (after, None), (weight, None), (act, VMEM)]
    outs = [((TOKENS, HALF), bf16, VMEM)] * 2
    outs += [((TOKENS, 1), f32, VMEM), ((1, TOKENS), f32, VMEM)]
    scratch = [pltpu.SemaphoreType.DMA((2, 4))]
    return call(rows_kernel, outs, ins, scratch, 8, 0, 10 * 2**20)


def times_rows(a, b):
    return lax.dot_general(a, b, (((1,), (1,)), ((), ())), preferred_element_type=f32)


def join(pieces, out):
    for i, piece in enumerate(pieces):
        out[128 * i : 128 * i + 128, :] = piece[...]


def decoder_part(half, out, errors, weight, act, factor, stage, sems):
    copies = []
    for j in range(HALF // STEP):
        span = slice(j * STEP, j * STEP + STEP)
        part = jnp.dot(act[...], errors[:, span], preferred_element_type=f32)
        part = part + factor[...] * weight[:, span].astype(f32)
        stage[j] = part.astype(bf16)
        columns = pl.ds(pl.multiple_of(half * HALF + j * STEP, STEP), STEP)
        copies.append(pltpu.make_async_copy(stage.at[j], out.at[:, columns], sems.at[j]))
        copies[-1].start()
    return copies


def first_kernel(core, *refs):
    pieces, (weight, act, factor, grad_acts, out, errors, stage, sems) = refs[:4], refs[4:]
    join(pieces, errors)
    copies = decoder_part(core[0], out, errors, weight, act, factor, stage, sems)
    total = jnp.zeros((TOKENS, TOKENS), f32)
    for j in range(HALF // STEP):
        span = slice(j * STEP, j * STEP + STEP)
        total = total + times_rows(errors[:, span], weight[:, span])
    grad_acts[...] = total
    for copy in copies:
        copy.wait()


def first_gradients(core, errors, weight, act, factor):
    ins = [(core, pltpu.SMEM)] + [(v, VMEM) for v in [*errors, weight, act, factor]]
    outs = [((TOKENS, TOKENS), f32, VMEM), ((TOKENS, D), bf16, None)]
    scratch = [
        pltpu.VMEM((TOKENS, HALF), bf16),
        pltpu.VMEM((HALF // STEP, TOKENS, STEP), bf16),
        pltpu.SemaphoreType.DMA((HALF // STEP,)),
    ]
    flops = 4 * TOKENS * TOKENS * HALF
    return call(first_kernel, outs, ins, scratch, 24, flops, 8 * 2**20)


def last_kernel(core, _, own_acts, *refs):
    pieces, refs = refs[:4], refs[4:]
    (weight, act, factor, penalty, rectified, flipped_own, flipped_mate) = refs[:7]
    (out, out_encoder, out_bias) = refs[7:10]
    (errors, stage, turned, grads, grads_mate, encoder_stage, sems, encoder_sems) = refs[10:18]
    (streams, stream_sems) = refs[18:]
    loads = []
    for k, flipped in enumerate((flipped_own, flipped_mate)):
        for j in range(HALF // STEP):
            slot = k * (HALF // STEP) + j
            rows = slice(j * STEP, j * STEP + STEP)
            loads.append(
                pltpu.make_async_copy(flipped.at[rows, :], streams.at[slot], stream_sems.at[slot])
            )
            loads[-1].start()
    join(pieces, errors)
    total = jnp.zeros((TOKENS, TOKENS), f32)
    for j in range(HALF // STEP):
        span = slice(j * STEP, j * STEP + STEP)
        total = total + times_rows(errors[:, span], weight[:, span])
    turned[...] = total
    bias = jnp.zeros((1, TOKENS), f32)
    for major in range(4):
        for minor in range(4):
            here, there = (major * 4 + minor) * 32, (minor * 4 + major) * 32
            acts = own_acts[here : here + 32, :] + turned[there : there + 32, :] + penalty[...]
            rounded = (acts * 2.0 * rectified[here : here + 32, :]).astype(bf16)
            grads[here : here + 32, :] = rounded
            grads_mate[there : there + 32, :] = rounded
            bias = bias + jnp.sum(rounded.astype(f32), axis=0, keepdims=True)
    out_bias[...] = bias
    copies = []
    for k, grad in enumerate((grads, grads_mate)):
        half = core[0] if k == 0 else 1 - core[0]
        for j in range(HALF // STEP):
            slot = k * (HALF // STEP) + j
            loads[slot].wait()
            part = jnp.dot(streams[slot], grad[...], preferred_element_type=f32)
            encoder_stage[slot] = part.astype(bf16)
            rows = pl.ds(pl.multiple_of(half * HALF + j * STEP, STEP), STEP)
            copies.append(
                pltpu.make_async_copy(
                    encoder_stage.at[slot], out_encoder.at[rows, :], encoder_sems.at[slot]
                )
            )
            copies[-1].start()
    copies += decoder_part(1 - core[0], out, errors, weight, act, factor, stage, sems)
    for copy in copies:
        copy.wait()


def last_gradients(core, grad_decoder, grad_acts, errors, *rest):
    ins = [(core, pltpu.SMEM), (grad_decoder, None), (grad_acts, VMEM)]
    ins += [(v, VMEM) for v in [*errors, *rest[:-2]]] + [(v, None) for v in rest[-2:]]
    outs = [((TOKENS, D), bf16, None), ((D, TOKENS), bf16, None), ((1, TOKENS), f32, VMEM)]
    steps = HALF // STEP
    scratch = [
        pltpu.VMEM((TOKENS, HALF), bf16),
        pltpu.VMEM((steps, TOKENS, STEP), bf16),
        pltpu.VMEM((TOKENS, TOKENS), f32),
        pltpu.VMEM((TOKENS, TOKENS), bf16),
        pltpu.VMEM((TOKENS, TOKENS), bf16),
        pltpu.VMEM((2 * steps, STEP, TOKENS), bf16),
        pltpu.SemaphoreType.DMA((steps,)),
        pltpu.SemaphoreType.DMA((2 * steps,)),
        pltpu.VMEM((2 * steps, STEP, TOKENS), bf16),
        pltpu.SemaphoreType.DMA((2 * steps,)),
    ]
    flops = 8 * TOKENS * TOKENS * HALF
    return call(
        last_kernel, outs, ins, scratch, 32, flops, 16 * 2**20, input_output_aliases={1: 0}
    )


def dot(a, b):
    return jnp.dot(a, b, preferred_element_type=f32)


def local(
    head_outputs,
    out_weight,
    residual_input,
    post_gain,
    encoder_weight,
    encoder_bias,
    decoder_weight,
    decoder_bias,
):
    here = lax.axis_index("prod")
    low = here // 2 == 0
    first = here % 2 == 0

    def own_half(v):
        return jnp.where(first, v[..., :HALF], v[..., HALF:])

    def other_half(v):
        return jnp.where(first, v[..., HALF:], v[..., :HALF])

    core = (here % 2).reshape(1)
    partial_value = dot(head_outputs, out_weight)
    both = own_half(partial_value) + to_core(other_half(partial_value))
    projected = both + lax.ppermute(both, "prod", [(0, 2), (2, 0), (1, 3), (3, 1)])
    squares = jnp.broadcast_to(jnp.sum(projected * projected, axis=1, keepdims=True), (16, 128))
    squares = (squares + to_core(squares))[:, :1]
    gain = own_half(post_gain)
    normed = projected * lax.rsqrt(squares / D + norm_epsilon) * gain
    stream = (own_half(residual_input).astype(f32) + normed).astype(bf16)

    stream, encoder_send, decoder_send = lax.optimization_barrier(
        (stream, encoder_weight, decoder_weight)
    )
    encoder_mate = to_core(encoder_send)
    decoder_mate = to_core(decoder_send)
    bias_own = own_half(decoder_bias)
    stream = jnp.concatenate([stream, move(stream, lambda x, y, z, c: (x, 3 - y, z, c))])
    stream = jnp.where(low, stream, jnp.roll(stream, -8, axis=0))
    stream = jnp.concatenate(gather(stream, to_minor))
    own_stream = stream.reshape(4, 4, 8, HALF)[:, 0].reshape(32, HALF)
    centred = (stream.astype(f32) - bias_own).astype(bf16)
    centred, encoder_mate, decoder_mate = lax.optimization_barrier(
        (centred, encoder_mate, decoder_mate)
    )
    encoder_mate = cut(encoder_mate, 0, core, centred)
    decoder_mate = cut(decoder_mate, 1, core, centred)
    encoder_own = cut(encoder_weight, 0, core, centred)
    decoder_own = cut(decoder_weight, 1, core, centred)
    centred = gather(centred, to_major)

    for_mate = swap_blocks(jnp.concatenate([dot(piece, encoder_mate) for piece in centred]))
    for_mate, decoder_own, decoder_mate = lax.optimization_barrier(
        (for_mate, decoder_own, decoder_mate)
    )
    preact = jnp.concatenate([dot(piece, encoder_own) for piece in centred])
    preact = preact + to_core(for_mate) + encoder_bias
    rectified = jnp.maximum(preact, 0.0)
    activations = jnp.square(rectified).astype(bf16)
    swapped = swap_blocks(activations)
    mate_activations = to_core(swapped)

    pieces = []
    for d in range(4):
        rows = slice(128 * d, 128 * d + 128)
        piece = dot(activations[rows], decoder_own) + dot(mate_activations[rows], decoder_mate)
        pieces.append(to_major(piece.astype(bf16), d) if d else piece)
    recon = sum(piece.astype(f32) for piece in pieces).astype(bf16)
    flipped_own, flipped_act, flipped_swapped = flip(centred, [activations, swapped], activations)
    recon, flipped_own = lax.optimization_barrier((recon, flipped_own))
    flipped_mate = to_core(flipped_own)
    pieces = [recon.reshape(4, 4, 8, HALF)[:, d].reshape(32, HALF) for d in range(4)]
    pieces = [to_middle(piece, d) if d else piece for d, piece in enumerate(pieces)]
    recon = sum(piece.astype(f32) for piece in pieces).astype(bf16)
    summed = recon.astype(f32)
    for d in (1, 2, 3):
        summed = summed + jnp.roll(to_minor(recon, -d), 8 * d, axis=0).astype(f32)
    grad_recon = (2.0 * (summed + bias_own - own_stream.astype(f32)) / TOKENS).astype(bf16)

    errors = [piece.reshape(4, 1, 8, HALF) for piece in gather(grad_recon, to_middle)]
    errors = jnp.concatenate(errors, axis=1).reshape(128, HALF)
    errors, flipped_mate = lax.optimization_barrier((errors, flipped_mate))
    decoder_own, decoder_other, factor, penalty = decoder_rows(
        core, errors, decoder_weight, flipped_act
    )
    errors = gather(errors, to_major)
    errors[3], decoder_own, decoder_other, factor, penalty = lax.optimization_barrier(
        (errors[3], decoder_own, decoder_other, factor, penalty)
    )
    errors_mate = [to_core(piece) for piece in errors]

    grad_acts, grad_decoder = first_gradients(core, errors, decoder_own, flipped_act, factor)
    grad_decoder, grad_encoder, grad_bias = last_gradients(
        core, grad_decoder, grad_acts, errors_mate, decoder_other, flipped_swapped, factor,
        penalty, rectified, flipped_own, flipped_mate,
    )
    return (grad_encoder, grad_bias.reshape(TOKENS), grad_decoder)


def solution(mesh):
    placed = (
        P("sae", "prod"),
        P("prod", None),
        P("sae", None),
        P(),
        P(None, ("prod", "sae")),
        P(("prod", "sae")),
        P(("prod", "sae"), None),
        P(),
    )
    return jax.shard_map(
        local,
        mesh=mesh,
        in_specs=placed,
        out_specs=(P(None, ("prod", "sae")), P(("prod", "sae")), P(("prod", "sae"), None)),
        check_vma=False,
    )
```

time: 155 us -> 138 us (0.89); the launches traced: 152 us -> 138 us
  waiting for transfers between devices: 74.3 us -> 47.2 us
  Pallas kernels: 0 us -> 24.6 us
  matrix products: 21.3 us -> 11 us
  other arithmetic: 3.93 us -> 1.09 us
  starting transfers between devices: 49.9 us -> 51.5 us
    ppermute x29 -> x33, waiting for transfers between devices: 72.4 us -> 43.6 us  [move(): return lax.ppermute(value, AXES, route(step))]
    pallas_call x0 -> x8, Pallas kernels: none -> 24.6 us  [call(): pl.pallas_call(kernel, out_shape=tuple((jax.ShapeDtypeStruct(shape, dtype...]
    dot_general x6 -> x17, matrix products: 21.3 us -> 11 us  [dot(): return jnp.dot(a, b, preferred_element_type=f32)]
    ppermute x1, waiting for transfers between devices: 1.82 us -> 3.69 us  [local(): lax.ppermute(both, 'prod', [(0, 2), (2, 0), (1, 3), (3, 1)])]
    ppermute x29 -> x33, starting transfers between devices: 48.4 us -> 50.1 us  [move(): return lax.ppermute(value, AXES, route(step))]
  transfers between devices with their start and end apart: 30 -> 34, of which waited for: 26 -> 20; matrix products, arithmetic and copies ran while one was open for 1% -> 5% of each run, Pallas kernels for 0% -> 12%
where the time goes in v3:
time: 138 us
  starting transfers between devices  51.5 us (37%)
  waiting for transfers between devices  47.2 us (34%)
  Pallas kernels  24.6 us (18%)
  matrix products  11 us (8%)
    ppermute x33, starting transfers between devices, move(): return lax.ppermute(value, AXES, route(step))  50.1 us
    ppermute x33, waiting for transfers between devices, move(): return lax.ppermute(value, AXES, route(step))  43.6 us
    pallas_call x8, Pallas kernels, call(): pl.pallas_call(kernel, out_shape=tuple((jax.ShapeDtypeStruct(shape, dtype...  24.6 us
    dot_general x17, matrix products, dot(): return jnp.dot(a, b, preferred_element_type=f32)  11 us
    ppermute x1, waiting for transfers between devices, local(): lax.ppermute(both, 'prod', [(0, 2), (2, 0), (1, 3), (3, 1)])  3.69 us
  transfers between devices with their start and end apart: 34, of which 20 were waited for; matrix products, arithmetic and copies ran while one was open for 5% of the time, Pallas kernels for 12%

profile of v3, /device:TPU:1, one launch (start us, length us, event | category | flops | bytes accessed | tf_op | source)
XLA Modules:
  0.0 137.7 jit_solution(14852713446378891566)
XLA Ops:
  1.4 3.1 %fusion.32 = f32[16,4608]{1,0:T(8,128)S(1)} fusion(bf16[16,512]{1,0:T(8,128)(2,1)S(1)} %copy-done, bf16[512,4608]{1,0:T(8,128)(2,1)} %param.9), kind=kOutput, calls=%fused_computation.58 | convolution fusion | flops 75497472 | bytes 5029888 | tf_op jit(solution)/shard_map/dot_general | solution.py:282
  8.5 3.7 %collective-permute-done.1 = f32[16,2304]{1,0:T(8,128)S(1)} collective-permute-done((f32[16,2304]{1,0:T(8,128)S(1)}, f32[16,2304]{1,0:T(8,128)S(1)}, u32[]{:S(2)}, u32[]{:S(2)}) %collective-permute-start.1) | collective-permute-done | bytes 147488 | tf_op jit(solution)/shard_map/ppermute | solution.py:308
  15.2 2.8 %collective-permute-start.3 = (bf16[16,2304]{1,0:T(8,128)(2,1)S(1)}, bf16[16,2304]{1,0:T(8,128)(2,1)S(1)}, u32[]{:S(2)}, u32[]{:S(2)}) collective-permute-start(bf16[16,2304]{1,0:T(8,128)(2,1)S(1)} %add_convert_fusion), channel_id=1, source_target_pairs={{0,65},{32,97},{2,67},{34,99},{4,69},{36,101},{6,71},{38,103},{64,... | collective-permute-start | bytes 221192 | tf_op jit(solution)/shard_map/ppermute | solution.py:38
  18.0 2.2 %collective-permute-done.3 = bf16[16,2304]{1,0:T(8,128)(2,1)S(1)} collective-permute-done((bf16[16,2304]{1,0:T(8,128)(2,1)S(1)}, bf16[16,2304]{1,0:T(8,128)(2,1)S(1)}, u32[]{:S(2)}, u32[]{:S(2)}) %collective-permute-start.3) | collective-permute-done | bytes 73760 | tf_op jit(solution)/shard_map/ppermute | solution.py:38
  21.5 2.5 %collective-permute-start.5 = (bf16[32,2304]{1,0:T(8,128)(2,1)S(1)}, bf16[32,2304]{1,0:T(8,128)(2,1)S(1)}, u32[]{:S(2)}, u32[]{:S(2)}) collective-permute-start(bf16[32,2304]{1,0:T(8,128)(2,1)S(1)} %maximum_select_fusion), channel_id=1, source_target_pairs={{0,4},{32,48},{2,6},{34,50},{4,0},{36,52},{6,2},{38,54},{64,68},{9... | collective-permute-start | bytes 442376 | tf_op jit(solution)/shard_map/ppermute | solution.py:38
  25.6 2.5 %collective-permute-done.5 = bf16[32,2304]{1,0:T(8,128)(2,1)S(1)} collective-permute-done((bf16[32,2304]{1,0:T(8,128)(2,1)S(1)}, bf16[32,2304]{1,0:T(8,128)(2,1)S(1)}, u32[]{:S(2)}, u32[]{:S(2)}) %collective-permute-start.5) | collective-permute-done | bytes 147488 | tf_op jit(solution)/shard_map/ppermute | solution.py:38
  29.7 1.7 %collective-permute-start.11 = (bf16[128,2304]{1,0:T(8,128)(2,1)S(1)}, bf16[128,2304]{1,0:T(8,128)(2,1)S(1)}, u32[]{:S(2)}, u32[]{:S(2)}) collective-permute-start(bf16[128,2304]{1,0:T(8,128)(2,1)S(1)} %subtract_convert_fusion.after_ref.refs_0_), channel_id=1, source_target_pairs={{0,8},{32,34},{2,10},{34,36},{4,12},{36,38},{6,14},{38,32},{64,72}... | collective-permute-start | bytes 1769480 | tf_op jit(solution)/shard_map/ppermute | solution.py:38
  31.4 3.3 %collective-permute-start.10 = (bf16[128,2304]{1,0:T(8,128)(2,1)S(1)}, bf16[128,2304]{1,0:T(8,128)(2,1)S(1)}, u32[]{:S(2)}, u32[]{:S(2)}) collective-permute-start(bf16[128,2304]{1,0:T(8,128)(2,1)S(1)} %subtract_convert_fusion.after_ref.refs_0_), channel_id=1, source_target_pairs={{0,16},{32,36},{2,18},{34,38},{4,20},{36,32},{6,22},{38,34},{64,80... | collective-permute-start | bytes 1769480 | tf_op jit(solution)/shard_map/ppermute | solution.py:38
  35.4 1.6 %shard_map.103 = bf16[2304,512]{1,0:T(8,128)(2,1)S(1)} custom-call(s32[1]{0:T(128)} %bitcast.half_ref.core, bf16[128,2304]{1,0:T(8,128)(2,1)S(1)} %subtract_convert_fusion.after_ref.refs_0_, bf16[4608,512]{1,0:T(8,128)(2,1)} %weight_ref.2), custom_call_target="tpu_custom_call" | custom-call | bytes 4718592 | tf_op jit(solution)/shard_map/pallas_call | solution.py:92
  37.1 1.6 %shard_map.105 = bf16[512,2304]{1,0:T(8,128)(2,1)S(1)} custom-call(s32[1]{0:T(128)} %bitcast.half_ref.core, bf16[128,2304]{1,0:T(8,128)(2,1)S(1)} %subtract_convert_fusion.after_ref.refs_0_, bf16[512,4608]{1,0:T(8,128)(2,1)} %weight.1), custom_call_target="tpu_custom_call" | custom-call | bytes 4718592 | tf_op jit(solution)/shard_map/pallas_call | solution.py:92
  38.7 1.6 %shard_map.104 = bf16[2304,512]{1,0:T(8,128)(2,1)S(1)} custom-call(s32[1]{0:T(128)} %bitcast.half_ref.core, bf16[128,2304]{1,0:T(8,128)(2,1)S(1)} %subtract_convert_fusion.after_ref.refs_0_, bf16[4608,512]{1,0:T(8,128)(2,1)} %collective-permute-done.7.weight_ref), custom_call_target="tpu_custom_call" | custom-call | bytes 4718592 | tf_op jit(solution)/shard_map/pallas_call | solution.py:92
  40.4 1.6 %shard_map.106 = bf16[512,2304]{1,0:T(8,128)(2,1)S(1)} custom-call(s32[1]{0:T(128)} %bitcast.half_ref.core, bf16[128,2304]{1,0:T(8,128)(2,1)S(1)} %subtract_convert_fusion.after_ref.refs_0_, bf16[512,4608]{1,0:T(8,128)(2,1)} %collective-permute-done.8.weight_ref), custom_call_target="tpu_custom_call" | custom-call | bytes 4718592 | tf_op jit(solution)/shard_map/pallas_call | solution.py:92
  43.0 5.6 %collective-permute-done.10.refs_2_ = bf16[128,2304]{1,0:T(8,128)(2,1)S(1)} collective-permute-done((bf16[128,2304]{1,0:T(8,128)(2,1)S(1)}, bf16[128,2304]{1,0:T(8,128)(2,1)S(1)}, u32[]{:S(2)}, u32[]{:S(2)}) %collective-permute-start.10) | collective-permute-done | bytes 589856 | tf_op jit(solution)/shard_map/ppermute | solution.py:38
  49.7 2.1 %collective-permute-start.12 = (f32[512,512]{1,0:T(8,128)S(1)}, f32[512,512]{1,0:T(8,128)S(1)}, u32[]{:S(2)}, u32[]{:S(2)}) collective-permute-start(f32[512,512]{1,0:T(8,128)S(1)} %bitcast.73), channel_id=1, source_target_pairs={{0,32},{32,0},{2,34},{34,2},{4,36},{36,4},{6,38},{38,6},{64,96},{9... | collective-permute-start | bytes 3145736 | tf_op jit(solution)/shard_map/ppermute | solution.py:38
  56.9 2.0 %collective-permute-start.16 = (bf16[128,2304]{1,0:T(8,128)(2,1)S(1)}, bf16[128,2304]{1,0:T(8,128)(2,1)S(1)}, u32[]{:S(2)}, u32[]{:S(2)}) collective-permute-start(bf16[128,2304]{1,0:T(8,128)(2,1)S(1)} %fusion.5), channel_id=1, source_target_pairs={{0,24},{32,38},{2,26},{34,32},{4,28},{36,34},{6,30},{38,36},{64,88... | collective-permute-start | bytes 1769480 | tf_op jit(solution)/shard_map/ppermute | solution.py:38
  61.1 2.8 %shard_map.107 = (bf16[2304,512]{1,0:T(8,128)(2,1)S(1)}, bf16[512,512]{1,0:T(8,128)(2,1)S(1)}, bf16[512,512]{1,0:T(8,128)(2,1)S(1)}) custom-call(bf16[128,2304]{1,0:T(8,128)(2,1)S(1)} %subtract_convert_fusion.after_ref.refs_0_, bf16[128,2304]{1,0:T(8,128)(2,1)S(1)} %collective-permute-done.9.refs_1_, bf16[128,2304]{1,0:T(8,128)(2,1)S(1)} %collective-permute-done.10.refs_2_, ...), custom_call_target="tpu_custom_call" | custom-call | bytes 6291456 | tf_op jit(solution)/shard_map/pallas_call | solution.py:92
  64.4 7.7 %collective-permute-done.16 = bf16[128,2304]{1,0:T(8,128)(2,1)S(1)} collective-permute-done((bf16[128,2304]{1,0:T(8,128)(2,1)S(1)}, bf16[128,2304]{1,0:T(8,128)(2,1)S(1)}, u32[]{:S(2)}, u32[]{:S(2)}) %collective-permute-start.16) | collective-permute-done | bytes 589856 | tf_op jit(solution)/shard_map/ppermute | solution.py:38
  72.1 4.3 %collective-permute-done.14 = bf16[128,2304]{1,0:T(8,128)(2,1)S(1)} collective-permute-done((bf16[128,2304]{1,0:T(8,128)(2,1)S(1)}, bf16[128,2304]{1,0:T(8,128)(2,1)S(1)}, u32[]{:S(2)}, u32[]{:S(2)}) %collective-permute-start.14) | collective-permute-done | bytes 589856 | tf_op jit(solution)/shard_map/ppermute | solution.py:38
  78.2 1.8 %collective-permute-start.19 = (bf16[32,2304]{1,0:T(8,128)(2,1)S(1)}, bf16[32,2304]{1,0:T(8,128)(2,1)S(1)}, u32[]{:S(2)}, u32[]{:S(2)}) collective-permute-start(bf16[32,2304]{1,0:T(8,128)(2,1)S(1)} %get-tuple-element.68), channel_id=1, source_target_pairs={{0,65},{32,97},{2,67},{34,99},{4,69},{36,101},{6,71},{38,103},{64,... | collective-permute-start | bytes 442376 | tf_op jit(solution)/shard_map/ppermute | solution.py:38
  81.3 1.7 %collective-permute-start.26 = (bf16[2304,512]{1,0:T(8,128)(2,1)S(1)}, bf16[2304,512]{1,0:T(8,128)(2,1)S(1)}, u32[]{:S(2)}, u32[]{:S(2)}) collective-permute-start(bf16[2304,512]{1,0:T(8,128)(2,1)S(1)} %get-tuple-element.44.refs_9_), channel_id=1, source_target_pairs={{0,32},{32,0},{2,34},{34,2},{4,36},{36,4},{6,38},{38,6},{64,96},{9... | collective-permute-start | bytes 7077896 | tf_op jit(solution)/shard_map/ppermute | solution.py:38
  83.0 4.4 %collective-permute-done.18 = bf16[32,2304]{1,0:T(8,128)(2,1)S(1)} collective-permute-done((bf16[32,2304]{1,0:T(8,128)(2,1)S(1)}, bf16[32,2304]{1,0:T(8,128)(2,1)S(1)}, u32[]{:S(2)}, u32[]{:S(2)}) %collective-permute-start.18) | collective-permute-done | bytes 147488 | tf_op jit(solution)/shard_map/ppermute | solution.py:38
  89.0 1.8 %collective-permute-start.21 = (bf16[32,2304]{1,0:T(8,128)(2,1)S(1)}, bf16[32,2304]{1,0:T(8,128)(2,1)S(1)}, u32[]{:S(2)}, u32[]{:S(2)}) collective-permute-start(bf16[32,2304]{1,0:T(8,128)(2,1)S(1)} %fusion.13), channel_id=1, source_target_pairs={{0,4},{32,48},{2,6},{34,50},{4,0},{36,52},{6,2},{38,54},{64,68},{9... | collective-permute-start | bytes 442376 | tf_op jit(solution)/shard_map/ppermute | solution.py:38
  92.7 2.4 %collective-permute-done.20 = bf16[32,2304]{1,0:T(8,128)(2,1)S(1)} collective-permute-done((bf16[32,2304]{1,0:T(8,128)(2,1)S(1)}, bf16[32,2304]{1,0:T(8,128)(2,1)S(1)}, u32[]{:S(2)}, u32[]{:S(2)}) %collective-permute-start.20) | collective-permute-done | bytes 147488 | tf_op jit(solution)/shard_map/ppermute | solution.py:38
  96.0 1.8 %collective-permute-start.24 = (bf16[32,2304]{1,0:T(8,128)(2,1)S(1)}, bf16[32,2304]{1,0:T(8,128)(2,1)S(1)}, u32[]{:S(2)}, u32[]{:S(2)}) collective-permute-start(bf16[32,2304]{1,0:T(8,128)(2,1)S(1)} %fusion.10), channel_id=1, source_target_pairs={{0,1},{32,33},{2,3},{34,35},{4,5},{36,37},{6,7},{38,39},{64,65},{9... | collective-permute-start | bytes 442376 | tf_op jit(solution)/shard_map/ppermute | solution.py:38
  98.5 3.8 %collective-permute-done.25 = bf16[32,2304]{1,0:T(8,128)(2,1)S(1)} collective-permute-done((bf16[32,2304]{1,0:T(8,128)(2,1)S(1)}, bf16[32,2304]{1,0:T(8,128)(2,1)S(1)}, u32[]{:S(2)}, u32[]{:S(2)}) %collective-permute-start.25) | collective-permute-done | bytes 147488 | tf_op jit(solution)/shard_map/ppermute | solution.py:38
  103.6 2.4 %collective-permute-start.27 = (bf16[128,2304]{1,0:T(8,128)(2,1)S(1)}, bf16[128,2304]{1,0:T(8,128)(2,1)S(1)}, u32[]{:S(2)}, u32[]{:S(2)}) collective-permute-start(bf16[128,2304]{1,0:T(8,128)(2,1)S(1)} %bitcast.64), channel_id=1, source_target_pairs={{0,24},{32,38},{2,26},{34,32},{4,28},{36,34},{6,30},{38,36},{64,88... | collective-permute-start | bytes 1769480 | tf_op jit(solution)/shard_map/ppermute | solution.py:38
  106.0 6.0 %collective-permute-start.30 = (bf16[128,2304]{1,0:T(8,128)(2,1)S(1)}, bf16[128,2304]{1,0:T(8,128)(2,1)S(1)}, u32[]{:S(2)}, u32[]{:S(2)}) collective-permute-start(bf16[128,2304]{1,0:T(8,128)(2,1)S(1)} %bitcast.65), channel_id=1, source_target_pairs={{0,32},{32,0},{2,34},{34,2},{4,36},{36,4},{6,38},{38,6},{64,96},{9... | collective-permute-start | bytes 1769480 | tf_op jit(solution)/shard_map/ppermute | solution.py:38
  111.9 3.5 %shard_map.108 = (bf16[512,2304]{1,0:T(8,128)(2,1)S(1)}, bf16[512,2304]{1,0:T(8,128)(2,1)S(1)}, f32[512,1]{1,0:T(8,128)S(1)}, f32[1,512]{1,0:T(1,128)S(1)}) custom-call(s32[1]{0:T(128)} %bitcast.half_ref.core, bf16[128,2304]{1,0:T(8,128)(2,1)S(1)} %bitcast.66, bf16[512,4608]{1,0:T(8,128)(2,1)} %weight.1, bf16[512,512]{1,0:T(8,128)(2,1)S(1)} %get-tuple-element.46.act.refs_5_), custom_call_target="tpu_custom_call" | custom-call | bytes 10485760 | tf_op jit(solution)/shard_map/pallas_call | solution.py:92
  115.5 4.4 %collective-permute-done.29.refs_3_ = bf16[128,2304]{1,0:T(8,128)(2,1)S(1)} collective-permute-done((bf16[128,2304]{1,0:T(8,128)(2,1)S(1)}, bf16[128,2304]{1,0:T(8,128)(2,1)S(1)}, u32[]{:S(2)}, u32[]{:S(2)}) %collective-permute-start.29) | collective-permute-done | bytes 589856 | tf_op jit(solution)/shard_map/ppermute | solution.py:38
  119.9 5.3 %collective-permute-start.32 = (bf16[128,2304]{1,0:T(8,128)(2,1)S(1)}, bf16[128,2304]{1,0:T(8,128)(2,1)S(1)}, u32[]{:S(2)}, u32[]{:S(2)}) collective-permute-start(bf16[128,2304]{1,0:T(8,128)(2,1)S(1)} %collective-permute-done.28.refs_2_), channel_id=1, source_target_pairs={{0,32},{32,0},{2,34},{34,2},{4,36},{36,4},{6,38},{38,6},{64,96},{9... | collective-permute-start | bytes 1769480 | tf_op jit(solution)/shard_map/ppermute | solution.py:38
  125.7 3.2 %shard_map.109 = (f32[512,512]{1,0:T(8,128)S(1)}, bf16[512,4608]{1,0:T(8,128)(2,1)}) custom-call(s32[1]{0:T(128)} %bitcast.half_ref.core, bf16[128,2304]{1,0:T(8,128)(2,1)S(1)} %bitcast.67, bf16[128,2304]{1,0:T(8,128)(2,1)S(1)} %collective-permute-done.27.refs_1_, bf16[128,2304]{1,0:T(8,128)(2,1)S(1)} %collective-permute-done.28.refs_2_, ...), custom_call_target="tpu_custom_call" | custom-call | flops 2415919104 | bytes 8388608 | tf_op jit(solution)/shard_map/pallas_call | solution.py:92
  129.0 8.5 %shard_map.110 = (bf16[512,4608]{1,0:T(8,128)(2,1)}, bf16[4608,512]{1,0:T(8,128)(2,1)}, f32[1,512]{1,0:T(1,128)}) custom-call(s32[1]{0:T(128)} %bitcast.half_ref.core, bf16[512,4608]{1,0:T(8,128)(2,1)} %get-tuple-element.54._, f32[512,512]{1,0:T(8,128)S(1)} %get-tuple-element.55.own_acts, ...), custom_call_target="tpu_custom_call", output_to_operand_aliasing={{0}: (1, {})} | custom-call | flops 4831838208 | bytes 16777216 | tf_op jit(solution)/shard_map/pallas_call | solution.py:92
  (101 shorter events, 32.7 us)
Async XLA Ops:
  4.5 2.5 %collective-permute-start = (f32[16,2304]{1,0:T(8,128)S(1)}, f32[16,2304]{1,0:T(8,128)S(1)}, u32[]{:S(2)}, u32[]{:S(2)}) collective-permute-start(f32[16,2304]{1,0:T(8,128)S(1)} %slice_select_fusion), channel_id=1, source_target_pairs={{0,32},{32,0},{2,34},{34,2},{4,36},{36,4},{6,38},{38,6},{64,96},{9... | collective-permute-start | bytes 442376 | tf_op jit(solution)/shard_map/ppermute | solution.py:38
  7.0 5.1 %collective-permute-start.1 = (f32[16,2304]{1,0:T(8,128)S(1)}, f32[16,2304]{1,0:T(8,128)S(1)}, u32[]{:S(2)}, u32[]{:S(2)}) collective-permute-start(f32[16,2304]{1,0:T(8,128)S(1)} %select_add_fusion), channel_id=1, source_target_pairs={{0,64},{64,0},{32,96},{96,32},{1,65},{65,1},{33,97},{97,33},{2,66}... | collective-permute-start | bytes 442376 | tf_op jit(solution)/shard_map/ppermute | solution.py:308
  14.6 13.6 %collective-permute-start.7 = (bf16[4608,512]{1,0:T(8,128)(2,1)}, bf16[4608,512]{1,0:T(8,128)(2,1)}, u32[]{:S(2)}, u32[]{:S(2)}) collective-permute-start(bf16[4608,512]{1,0:T(8,128)(2,1)} %weight_ref.2), channel_id=1, source_target_pairs={{0,32},{32,0},{2,34},{34,2},{4,36},{36,4},{6,38},{38,6},{64,96},{9... | collective-permute-start | bytes 14155784 | tf_op jit(solution)/shard_map/ppermute | solution.py:38
  15.0 14.6 %collective-permute-start.8 = (bf16[512,4608]{1,0:T(8,128)(2,1)}, bf16[512,4608]{1,0:T(8,128)(2,1)}, u32[]{:S(2)}, u32[]{:S(2)}) collective-permute-start(bf16[512,4608]{1,0:T(8,128)(2,1)} %weight.1), channel_id=1, source_target_pairs={{0,32},{32,0},{2,34},{34,2},{4,36},{36,4},{6,38},{38,6},{64,96},{9... | collective-permute-start | bytes 14155784 | tf_op jit(solution)/shard_map/ppermute | solution.py:38
  15.2 5.0 %collective-permute-start.3 = (bf16[16,2304]{1,0:T(8,128)(2,1)S(1)}, bf16[16,2304]{1,0:T(8,128)(2,1)S(1)}, u32[]{:S(2)}, u32[]{:S(2)}) collective-permute-start(bf16[16,2304]{1,0:T(8,128)(2,1)S(1)} %add_convert_fusion), channel_id=1, source_target_pairs={{0,65},{32,97},{2,67},{34,99},{4,69},{36,101},{6,71},{38,103},{64,... | collective-permute-start | bytes 221192 | tf_op jit(solution)/shard_map/ppermute | solution.py:38
  20.3 5.3 %collective-permute-start.6 = (bf16[32,2304]{1,0:T(8,128)(2,1)S(1)}, bf16[32,2304]{1,0:T(8,128)(2,1)S(1)}, u32[]{:S(2)}, u32[]{:S(2)}) collective-permute-start(bf16[32,2304]{1,0:T(8,128)(2,1)S(1)} %maximum_select_fusion), channel_id=1, source_target_pairs={{0,2},{32,40},{2,4},{34,42},{4,6},{36,44},{6,0},{38,46},{64,66},{9... | collective-permute-start | bytes 442376 | tf_op jit(solution)/shard_map/ppermute | solution.py:38
  21.5 6.6 %collective-permute-start.5 = (bf16[32,2304]{1,0:T(8,128)(2,1)S(1)}, bf16[32,2304]{1,0:T(8,128)(2,1)S(1)}, u32[]{:S(2)}, u32[]{:S(2)}) collective-permute-start(bf16[32,2304]{1,0:T(8,128)(2,1)S(1)} %maximum_select_fusion), channel_id=1, source_target_pairs={{0,4},{32,48},{2,6},{34,50},{4,0},{36,52},{6,2},{38,54},{64,68},{9... | collective-permute-start | bytes 442376 | tf_op jit(solution)/shard_map/ppermute | solution.py:38
  23.9 4.2 %collective-permute-start.4 = (bf16[32,2304]{1,0:T(8,128)(2,1)S(1)}, bf16[32,2304]{1,0:T(8,128)(2,1)S(1)}, u32[]{:S(2)}, u32[]{:S(2)}) collective-permute-start(bf16[32,2304]{1,0:T(8,128)(2,1)S(1)} %maximum_select_fusion), channel_id=1, source_target_pairs={{0,6},{32,56},{2,0},{34,58},{4,2},{36,60},{6,4},{38,62},{64,70},{9... | collective-permute-start | bytes 442376 | tf_op jit(solution)/shard_map/ppermute | solution.py:38
  29.7 12.8 %collective-permute-start.11 = (bf16[128,2304]{1,0:T(8,128)(2,1)S(1)}, bf16[128,2304]{1,0:T(8,128)(2,1)S(1)}, u32[]{:S(2)}, u32[]{:S(2)}) collective-permute-start(bf16[128,2304]{1,0:T(8,128)(2,1)S(1)} %subtract_convert_fusion.after_ref.refs_0_), channel_id=1, source_target_pairs={{0,8},{32,34},{2,10},{34,36},{4,12},{36,38},{6,14},{38,32},{64,72}... | collective-permute-start | bytes 1769480 | tf_op jit(solution)/shard_map/ppermute | solution.py:38
  31.4 17.2 %collective-permute-start.10 = (bf16[128,2304]{1,0:T(8,128)(2,1)S(1)}, bf16[128,2304]{1,0:T(8,128)(2,1)S(1)}, u32[]{:S(2)}, u32[]{:S(2)}) collective-permute-start(bf16[128,2304]{1,0:T(8,128)(2,1)S(1)} %subtract_convert_fusion.after_ref.refs_0_), channel_id=1, source_target_pairs={{0,16},{32,36},{2,18},{34,38},{4,20},{36,32},{6,22},{38,34},{64,80... | collective-permute-start | bytes 1769480 | tf_op jit(solution)/shard_map/ppermute | solution.py:38
  34.7 14.4 %collective-permute-start.9 = (bf16[128,2304]{1,0:T(8,128)(2,1)S(1)}, bf16[128,2304]{1,0:T(8,128)(2,1)S(1)}, u32[]{:S(2)}, u32[]{:S(2)}) collective-permute-start(bf16[128,2304]{1,0:T(8,128)(2,1)S(1)} %subtract_convert_fusion.after_ref.refs_0_), channel_id=1, source_target_pairs={{0,24},{32,38},{2,26},{34,32},{4,28},{36,34},{6,30},{38,36},{64,88... | collective-permute-start | bytes 1769480 | tf_op jit(solution)/shard_map/ppermute | solution.py:38
  49.7 4.4 %collective-permute-start.12 = (f32[512,512]{1,0:T(8,128)S(1)}, f32[512,512]{1,0:T(8,128)S(1)}, u32[]{:S(2)}, u32[]{:S(2)}) collective-permute-start(f32[512,512]{1,0:T(8,128)S(1)} %bitcast.73), channel_id=1, source_target_pairs={{0,32},{32,0},{2,34},{34,2},{4,36},{36,4},{6,38},{38,6},{64,96},{9... | collective-permute-start | bytes 3145736 | tf_op jit(solution)/shard_map/ppermute | solution.py:38
  56.9 15.2 %collective-permute-start.16 = (bf16[128,2304]{1,0:T(8,128)(2,1)S(1)}, bf16[128,2304]{1,0:T(8,128)(2,1)S(1)}, u32[]{:S(2)}, u32[]{:S(2)}) collective-permute-start(bf16[128,2304]{1,0:T(8,128)(2,1)S(1)} %fusion.5), channel_id=1, source_target_pairs={{0,24},{32,38},{2,26},{34,32},{4,28},{36,34},{6,30},{38,36},{64,88... | collective-permute-start | bytes 1769480 | tf_op jit(solution)/shard_map/ppermute | solution.py:38
  59.5 12.6 %collective-permute-start.15 = (bf16[128,2304]{1,0:T(8,128)(2,1)S(1)}, bf16[128,2304]{1,0:T(8,128)(2,1)S(1)}, u32[]{:S(2)}, u32[]{:S(2)}) collective-permute-start(bf16[128,2304]{1,0:T(8,128)(2,1)S(1)} %fusion.4), channel_id=1, source_target_pairs={{0,16},{32,36},{2,18},{34,38},{4,20},{36,32},{6,22},{38,34},{64,80... | collective-permute-start | bytes 1769480 | tf_op jit(solution)/shard_map/ppermute | solution.py:38
  60.7 15.7 %collective-permute-start.14 = (bf16[128,2304]{1,0:T(8,128)(2,1)S(1)}, bf16[128,2304]{1,0:T(8,128)(2,1)S(1)}, u32[]{:S(2)}, u32[]{:S(2)}) collective-permute-start(bf16[128,2304]{1,0:T(8,128)(2,1)S(1)} %fusion.3), channel_id=1, source_target_pairs={{0,8},{32,34},{2,10},{34,36},{4,12},{36,38},{6,14},{38,32},{64,72}... | collective-permute-start | bytes 1769480 | tf_op jit(solution)/shard_map/ppermute | solution.py:38
  77.1 5.9 %collective-permute-start.17 = (bf16[32,2304]{1,0:T(8,128)(2,1)S(1)}, bf16[32,2304]{1,0:T(8,128)(2,1)S(1)}, u32[]{:S(2)}, u32[]{:S(2)}) collective-permute-start(bf16[32,2304]{1,0:T(8,128)(2,1)S(1)} %get-tuple-element.67), channel_id=1, source_target_pairs={{0,64},{32,96},{2,66},{34,98},{4,68},{36,100},{6,70},{38,102},{64,... | collective-permute-start | bytes 442376 | tf_op jit(solution)/shard_map/ppermute | solution.py:38
  78.2 4.8 %collective-permute-start.19 = (bf16[32,2304]{1,0:T(8,128)(2,1)S(1)}, bf16[32,2304]{1,0:T(8,128)(2,1)S(1)}, u32[]{:S(2)}, u32[]{:S(2)}) collective-permute-start(bf16[32,2304]{1,0:T(8,128)(2,1)S(1)} %get-tuple-element.68), channel_id=1, source_target_pairs={{0,65},{32,97},{2,67},{34,99},{4,69},{36,101},{6,71},{38,103},{64,... | collective-permute-start | bytes 442376 | tf_op jit(solution)/shard_map/ppermute | solution.py:38
  80.0 7.4 %collective-permute-start.18 = (bf16[32,2304]{1,0:T(8,128)(2,1)S(1)}, bf16[32,2304]{1,0:T(8,128)(2,1)S(1)}, u32[]{:S(2)}, u32[]{:S(2)}) collective-permute-start(bf16[32,2304]{1,0:T(8,128)(2,1)S(1)} %get-tuple-element.69), channel_id=1, source_target_pairs={{0,1},{32,33},{2,3},{34,35},{4,5},{36,37},{6,7},{38,39},{64,65},{9... | collective-permute-start | bytes 442376 | tf_op jit(solution)/shard_map/ppermute | solution.py:38
  81.3 21.9 %collective-permute-start.26 = (bf16[2304,512]{1,0:T(8,128)(2,1)S(1)}, bf16[2304,512]{1,0:T(8,128)(2,1)S(1)}, u32[]{:S(2)}, u32[]{:S(2)}) collective-permute-start(bf16[2304,512]{1,0:T(8,128)(2,1)S(1)} %get-tuple-element.44.refs_9_), channel_id=1, source_target_pairs={{0,32},{32,0},{2,34},{34,2},{4,36},{36,4},{6,38},{38,6},{64,96},{9... | collective-permute-start | bytes 7077896 | tf_op jit(solution)/shard_map/ppermute | solution.py:38
  87.4 5.3 %collective-permute-start.22 = (bf16[32,2304]{1,0:T(8,128)(2,1)S(1)}, bf16[32,2304]{1,0:T(8,128)(2,1)S(1)}, u32[]{:S(2)}, u32[]{:S(2)}) collective-permute-start(bf16[32,2304]{1,0:T(8,128)(2,1)S(1)} %fusion.13), channel_id=1, source_target_pairs={{0,2},{32,40},{2,4},{34,42},{4,6},{36,44},{6,0},{38,46},{64,66},{9... | collective-permute-start | bytes 442376 | tf_op jit(solution)/shard_map/ppermute | solution.py:38
  89.0 6.2 %collective-permute-start.21 = (bf16[32,2304]{1,0:T(8,128)(2,1)S(1)}, bf16[32,2304]{1,0:T(8,128)(2,1)S(1)}, u32[]{:S(2)}, u32[]{:S(2)}) collective-permute-start(bf16[32,2304]{1,0:T(8,128)(2,1)S(1)} %fusion.13), channel_id=1, source_target_pairs={{0,4},{32,48},{2,6},{34,50},{4,0},{36,52},{6,2},{38,54},{64,68},{9... | collective-permute-start | bytes 442376 | tf_op jit(solution)/shard_map/ppermute | solution.py:38
  90.9 4.3 %collective-permute-start.20 = (bf16[32,2304]{1,0:T(8,128)(2,1)S(1)}, bf16[32,2304]{1,0:T(8,128)(2,1)S(1)}, u32[]{:S(2)}, u32[]{:S(2)}) collective-permute-start(bf16[32,2304]{1,0:T(8,128)(2,1)S(1)} %fusion.13), channel_id=1, source_target_pairs={{0,6},{32,56},{2,0},{34,58},{4,2},{36,60},{6,4},{38,62},{64,70},{9... | collective-permute-start | bytes 442376 | tf_op jit(solution)/shard_map/ppermute | solution.py:38
  95.4 6.9 %collective-permute-start.25 = (bf16[32,2304]{1,0:T(8,128)(2,1)S(1)}, bf16[32,2304]{1,0:T(8,128)(2,1)S(1)}, u32[]{:S(2)}, u32[]{:S(2)}) collective-permute-start(bf16[32,2304]{1,0:T(8,128)(2,1)S(1)} %fusion.10), channel_id=1, source_target_pairs={{0,64},{32,96},{2,66},{34,98},{4,68},{36,100},{6,70},{38,102},{64,... | collective-permute-start | bytes 442376 | tf_op jit(solution)/shard_map/ppermute | solution.py:38
  96.0 6.2 %collective-permute-start.24 = (bf16[32,2304]{1,0:T(8,128)(2,1)S(1)}, bf16[32,2304]{1,0:T(8,128)(2,1)S(1)}, u32[]{:S(2)}, u32[]{:S(2)}) collective-permute-start(bf16[32,2304]{1,0:T(8,128)(2,1)S(1)} %fusion.10), channel_id=1, source_target_pairs={{0,1},{32,33},{2,3},{34,35},{4,5},{36,37},{6,7},{38,39},{64,65},{9... | collective-permute-start | bytes 442376 | tf_op jit(solution)/shard_map/ppermute | solution.py:38
  97.8 5.4 %collective-permute-start.23 = (bf16[32,2304]{1,0:T(8,128)(2,1)S(1)}, bf16[32,2304]{1,0:T(8,128)(2,1)S(1)}, u32[]{:S(2)}, u32[]{:S(2)}) collective-permute-start(bf16[32,2304]{1,0:T(8,128)(2,1)S(1)} %fusion.10), channel_id=1, source_target_pairs={{0,65},{32,97},{2,67},{34,99},{4,69},{36,101},{6,71},{38,103},{64,... | collective-permute-start | bytes 442376 | tf_op jit(solution)/shard_map/ppermute | solution.py:38
  103.2 16.6 %collective-permute-start.29 = (bf16[128,2304]{1,0:T(8,128)(2,1)S(1)}, bf16[128,2304]{1,0:T(8,128)(2,1)S(1)}, u32[]{:S(2)}, u32[]{:S(2)}) collective-permute-start(bf16[128,2304]{1,0:T(8,128)(2,1)S(1)} %bitcast.62), channel_id=1, source_target_pairs={{0,8},{32,34},{2,10},{34,36},{4,12},{36,38},{6,14},{38,32},{64,72}... | collective-permute-start | bytes 1769480 | tf_op jit(solution)/shard_map/ppermute | solution.py:38
  103.3 16.5 %collective-permute-start.28 = (bf16[128,2304]{1,0:T(8,128)(2,1)S(1)}, bf16[128,2304]{1,0:T(8,128)(2,1)S(1)}, u32[]{:S(2)}, u32[]{:S(2)}) collective-permute-start(bf16[128,2304]{1,0:T(8,128)(2,1)S(1)} %bitcast.63), channel_id=1, source_target_pairs={{0,16},{32,36},{2,18},{34,38},{4,20},{36,32},{6,22},{38,34},{64,80... | collective-permute-start | bytes 1769480 | tf_op jit(solution)/shard_map/ppermute | solution.py:38
  103.6 21.5 %collective-permute-start.27 = (bf16[128,2304]{1,0:T(8,128)(2,1)S(1)}, bf16[128,2304]{1,0:T(8,128)(2,1)S(1)}, u32[]{:S(2)}, u32[]{:S(2)}) collective-permute-start(bf16[128,2304]{1,0:T(8,128)(2,1)S(1)} %bitcast.64), channel_id=1, source_target_pairs={{0,24},{32,38},{2,26},{34,32},{4,28},{36,34},{6,30},{38,36},{64,88... | collective-permute-start | bytes 1769480 | tf_op jit(solution)/shard_map/ppermute | solution.py:38
  106.0 23.0 %collective-permute-start.30 = (bf16[128,2304]{1,0:T(8,128)(2,1)S(1)}, bf16[128,2304]{1,0:T(8,128)(2,1)S(1)}, u32[]{:S(2)}, u32[]{:S(2)}) collective-permute-start(bf16[128,2304]{1,0:T(8,128)(2,1)S(1)} %bitcast.65), channel_id=1, source_target_pairs={{0,32},{32,0},{2,34},{34,2},{4,36},{36,4},{6,38},{38,6},{64,96},{9... | collective-permute-start | bytes 1769480 | tf_op jit(solution)/shard_map/ppermute | solution.py:38
  119.9 9.1 %collective-permute-start.32 = (bf16[128,2304]{1,0:T(8,128)(2,1)S(1)}, bf16[128,2304]{1,0:T(8,128)(2,1)S(1)}, u32[]{:S(2)}, u32[]{:S(2)}) collective-permute-start(bf16[128,2304]{1,0:T(8,128)(2,1)S(1)} %collective-permute-done.28.refs_2_), channel_id=1, source_target_pairs={{0,32},{32,0},{2,34},{34,2},{4,36},{36,4},{6,38},{38,6},{64,96},{9... | collective-permute-start | bytes 1769480 | tf_op jit(solution)/shard_map/ppermute | solution.py:38
  125.1 3.8 %collective-permute-start.31 = (bf16[128,2304]{1,0:T(8,128)(2,1)S(1)}, bf16[128,2304]{1,0:T(8,128)(2,1)S(1)}, u32[]{:S(2)}, u32[]{:S(2)}) collective-permute-start(bf16[128,2304]{1,0:T(8,128)(2,1)S(1)} %collective-permute-done.27.refs_1_), channel_id=1, source_target_pairs={{0,32},{32,0},{2,34},{34,2},{4,36},{36,4},{6,38},{38,6},{64,96},{9... | collective-permute-start | bytes 1769480 | tf_op jit(solution)/shard_map/ppermute | solution.py:38
  125.7 3.3 %collective-permute-start.33 = (bf16[128,2304]{1,0:T(8,128)(2,1)S(1)}, bf16[128,2304]{1,0:T(8,128)(2,1)S(1)}, u32[]{:S(2)}, u32[]{:S(2)}) collective-permute-start(bf16[128,2304]{1,0:T(8,128)(2,1)S(1)} %collective-permute-done.29.refs_3_), channel_id=1, source_target_pairs={{0,32},{32,0},{2,34},{34,2},{4,36},{36,4},{6,38},{38,6},{64,96},{9... | collective-permute-start | bytes 1769480 | tf_op jit(solution)/shard_map/ppermute | solution.py:38
  (8 other events, 60.3 us)

commit v4 on v3

--- a/solution.py
+++ b/solution.py
@@ -46,16 +46,27 @@
     return move(value, lambda x, y, z, c: (x + d, y, z, c) if c == 0 else (x, y, z + d, c))
 
 
-def to_middle(value, d):
-    return move(value, lambda x, y, z, c: (x, y + d, z, c))
+def to_y(value, mask):
+    return move(value, lambda x, y, z, c: (x, y ^ mask, z, c))
 
 
 def to_minor(value, d):
     return move(value, lambda x, y, z, c: (x, y, z + d, c) if c == 0 else (x + d, y, z, c))
 
 
-def gather(value, to):
-    return [value] + [to(value, -d) for d in (1, 2, 3)]
+MASKS = (0, 1, 3, 2)
+
+
+def gather_y(value):
+    pieces = [value] + [to_y(value, mask) for mask in MASKS[1:]]
+    pieces = [piece.reshape(4, 1, 8, HALF) for piece in pieces]
+    return jnp.concatenate(pieces, axis=1).reshape(128, HALF)
+
+
+def scatter_y(value):
+    pieces = [value.reshape(4, 4, 8, HALF)[:, k].reshape(32, HALF) for k in range(4)]
+    pieces = pieces[:1] + [to_y(piece, mask) for piece, mask in zip(pieces[1:], MASKS[1:])]
+    return sum(piece.astype(f32) for piece in pieces)
 
 
 def swap_blocks(value):
@@ -122,25 +133,22 @@
     return call(flip_kernel, outs, ins, [], 8, 0, 6 * 2**20)
 
 
-def rows_kernel(core, _, weight, act, own, other, factor, penalty, sems):
+def rows_kernel(core, _, weight, own, act, other, factor, penalty, sems):
+    columns = pl.ds(pl.multiple_of((1 - core[0]) * HALF, HALF), HALF)
     copies = []
-    for k, out in enumerate((own, other)):
-        half = core[0] if k == 0 else 1 - core[0]
-        for i in range(4):
-            span = slice(128 * i, 128 * i + 128)
-            columns = pl.ds(pl.multiple_of(half * HALF, HALF), HALF)
-            copies.append(
-                pltpu.make_async_copy(
-                    weight.at[span, columns], out.at[span, :], sems.at[k, i]
-                )
-            )
-            copies[-1].start()
-    for copy in copies:
-        copy.wait()
+    for i in range(4):
+        span = slice(128 * i, 128 * i + 128)
+        copies.append(
+            pltpu.make_async_copy(weight.at[span, columns], other.at[span, :], sems.at[i])
+        )
+        copies[-1].start()
     squares = jnp.zeros((TOKENS, 128), f32)
-    for out in (own, other):
+    for part in (own, other):
+        if part is other:
+            for copy in copies:
+                copy.wait()
         for j in range(HALF // 128):
-            wide = out[:, 128 * j : 128 * j + 128].astype(f32)
+            wide = part[:, 128 * j : 128 * j + 128].astype(f32)
             squares = squares + wide * wide
     norms = jnp.sqrt(jnp.sum(squares, axis=1, keepdims=True) + norm_epsilon)
     act_sum = jnp.sum(act[...].astype(f32), axis=1, keepdims=True)
@@ -149,12 +157,12 @@
     penalty[...] = norms.T[:1, :]
 
 
-def decoder_rows(core, after, weight, act):
-    ins = [(core, pltpu.SMEM), (after, None), (weight, None), (act, VMEM)]
-    outs = [((TOKENS, HALF), bf16, VMEM)] * 2
+def decoder_rows(core, after, weight, own, act):
+    ins = [(core, pltpu.SMEM), (after, None), (weight, None), (own, VMEM), (act, VMEM)]
+    outs = [((TOKENS, HALF), bf16, VMEM)]
     outs += [((TOKENS, 1), f32, VMEM), ((1, TOKENS), f32, VMEM)]
-    scratch = [pltpu.SemaphoreType.DMA((2, 4))]
-    return call(rows_kernel, outs, ins, scratch, 8, 0, 10 * 2**20)
+    scratch = [pltpu.SemaphoreType.DMA((4,))]
+    return call(rows_kernel, outs, ins, scratch, 8, 0, 6 * 2**20)
 
 
 def times_rows(a, b):
@@ -311,6 +319,7 @@
     gain = own_half(post_gain)
     normed = projected * lax.rsqrt(squares / D + norm_epsilon) * gain
     stream = (own_half(residual_input).astype(f32) + normed).astype(bf16)
+    stream = jnp.where(low, stream, jnp.roll(stream, 8, axis=0))
 
     stream, encoder_send, decoder_send = lax.optimization_barrier(
         (stream, encoder_weight, decoder_weight)
@@ -318,9 +327,8 @@
     encoder_mate = to_core(encoder_send)
     decoder_mate = to_core(decoder_send)
     bias_own = own_half(decoder_bias)
-    stream = jnp.concatenate([stream, move(stream, lambda x, y, z, c: (x, 3 - y, z, c))])
-    stream = jnp.where(low, stream, jnp.roll(stream, -8, axis=0))
-    stream = jnp.concatenate(gather(stream, to_minor))
+    stream = jnp.concatenate([stream, to_y(stream, 3)])
+    stream = jnp.concatenate([stream] + [to_minor(stream, -d) for d in (1, 2, 3)])
     own_stream = stream.reshape(4, 4, 8, HALF)[:, 0].reshape(32, HALF)
     centred = (stream.astype(f32) - bias_own).astype(bf16)
     centred, encoder_mate, decoder_mate = lax.optimization_barrier(
@@ -330,7 +338,7 @@
     decoder_mate = cut(decoder_mate, 1, core, centred)
     encoder_own = cut(encoder_weight, 0, core, centred)
     decoder_own = cut(decoder_weight, 1, core, centred)
-    centred = gather(centred, to_major)
+    centred = [centred] + [to_major(centred, -d) for d in (1, 2, 3)]
 
     for_mate = swap_blocks(jnp.concatenate([dot(piece, encoder_mate) for piece in centred]))
     for_mate, decoder_own, decoder_mate = lax.optimization_barrier(
@@ -343,33 +351,38 @@
     swapped = swap_blocks(activations)
     mate_activations = to_core(swapped)
 
-    pieces = []
+    pieces = {}
     for d in range(4):
         rows = slice(128 * d, 128 * d + 128)
-        piece = dot(activations[rows], decoder_own) + dot(mate_activations[rows], decoder_mate)
-        pieces.append(to_major(piece.astype(bf16), d) if d else piece)
-    recon = sum(piece.astype(f32) for piece in pieces).astype(bf16)
-    flipped_own, flipped_act, flipped_swapped = flip(centred, [activations, swapped], activations)
-    recon, flipped_own = lax.optimization_barrier((recon, flipped_own))
+        own = dot(activations[rows], decoder_own)
+        pieces[d] = (own + dot(mate_activations[rows], decoder_mate)).astype(bf16)
+    far = pieces[2].reshape(4, 4, 8, HALF)
+    keep = jnp.where(first, far[:, :2], far[:, ::2])
+    send = jnp.where(first, far[:, 2:], far[:, 1::2])
+    send = move(send, lambda x, y, z, c: (x, y ^ (3 if c == 0 else 1), z, c))
+    far = (keep.astype(f32) + send.astype(f32)).astype(bf16)
+    send = move(far[:, 1], lambda x, y, z, c: (x, y ^ (1 if c == 0 else 3), z, c))
+    far = (far[:, 0].astype(f32) + send.astype(f32)).astype(bf16).reshape(32, HALF)
+    recon = [pieces[0], to_major(pieces[1], 1), to_major(pieces[3], 3)]
+    recon = sum(piece.astype(f32) for piece in recon).astype(bf16)
+    flipped_own, flipped_act, flipped_swapped = flip(centred, [activations, swapped], pieces[0])
+    decoder_other, factor, penalty = decoder_rows(
+        core, pieces[0], decoder_weight, decoder_own, flipped_act
+    )
+    recon, flipped_own, decoder_other, factor, penalty = lax.optimization_barrier(
+        (recon, flipped_own, decoder_other, factor, penalty)
+    )
     flipped_mate = to_core(flipped_own)
-    pieces = [recon.reshape(4, 4, 8, HALF)[:, d].reshape(32, HALF) for d in range(4)]
-    pieces = [to_middle(piece, d) if d else piece for d, piece in enumerate(pieces)]
-    recon = sum(piece.astype(f32) for piece in pieces).astype(bf16)
+    recon = (scatter_y(recon) + to_major(far, 2).astype(f32)).astype(bf16)
     summed = recon.astype(f32)
     for d in (1, 2, 3):
         summed = summed + jnp.roll(to_minor(recon, -d), 8 * d, axis=0).astype(f32)
     grad_recon = (2.0 * (summed + bias_own - own_stream.astype(f32)) / TOKENS).astype(bf16)
 
-    errors = [piece.reshape(4, 1, 8, HALF) for piece in gather(grad_recon, to_middle)]
-    errors = jnp.concatenate(errors, axis=1).reshape(128, HALF)
+    far = to_major(grad_recon, 2)
+    errors = gather_y(grad_recon)
     errors, flipped_mate = lax.optimization_barrier((errors, flipped_mate))
-    decoder_own, decoder_other, factor, penalty = decoder_rows(
-        core, errors, decoder_weight, flipped_act
-    )
-    errors = gather(errors, to_major)
-    errors[3], decoder_own, decoder_other, factor, penalty = lax.optimization_barrier(
-        (errors[3], decoder_own, decoder_other, factor, penalty)
-    )
+    errors = [errors, to_major(errors, -1), gather_y(far), to_major(errors, -3)]
     errors_mate = [to_core(piece) for piece in errors]
 
     grad_acts, grad_decoder = first_gradients(core, errors, decoder_own, flipped_act, factor)

time: 138 us -> 131 us (0.949)
  waiting for transfers between devices: 47.2 us -> 32.3 us
  starting transfers between devices: 51.5 us -> 63.3 us
  Pallas kernels: 24.6 us -> 17.7 us
  local copies, waits for them, and re-layouts: 0.95 us -> 3.84 us
    ppermute x33 -> x38, waiting for transfers between devices: 43.6 us -> 28.6 us  [move(): return lax.ppermute(value, AXES, route(step))]
    ppermute x33 -> x38, starting transfers between devices: 50.1 us -> 61.9 us  [move(): return lax.ppermute(value, AXES, route(step))]
    pallas_call x8, Pallas kernels: 24.6 us -> 17.7 us  [call(): pl.pallas_call(kernel, out_shape=tuple((jax.ShapeDtypeStruct(shape, dtype...]
    unnamed x13 -> x21, local copies, waits for them, and re-layouts: 0.73 us -> 3.6 us
  transfers between devices with their start and end apart: 34 -> 39, of which waited for: 20 -> 19; matrix products, arithmetic and copies ran while one was open for 5% -> 5% of each run, Pallas kernels for 12% -> 7%
where the time goes in v4:
time: 131 us
  starting transfers between devices  63.3 us (48%)
  waiting for transfers between devices  32.3 us (25%)
  Pallas kernels  17.7 us (14%)
  matrix products  10.9 us (8%)
  local copies, waits for them, and re-layouts  3.84 us (3%)
  other arithmetic  1.51 us (1%)
  between operations  1.32 us (1%)
    ppermute x38, starting transfers between devices, move(): return lax.ppermute(value, AXES, route(step))  61.9 us
    ppermute x38, waiting for transfers between devices, move(): return lax.ppermute(value, AXES, route(step))  28.6 us
    pallas_call x8, Pallas kernels, call(): pl.pallas_call(kernel, out_shape=tuple((jax.ShapeDtypeStruct(shape, dtype...  17.7 us
    dot_general x17, matrix products, dot(): return jnp.dot(a, b, preferred_element_type=f32)  10.9 us
    ppermute x1, waiting for transfers between devices, local(): lax.ppermute(both, 'prod', [(0, 2), (2, 0), (1, 3), (3, 1)])  3.69 us
    unnamed x21, local copies, waits for them, and re-layouts  3.6 us
  transfers between devices with their start and end apart: 39, of which 19 were waited for; matrix products, arithmetic and copies ran while one was open for 5% of the time, Pallas kernels for 7%

profile of v4, /device:TPU:1, one launch (start us, length us, event | category | flops | bytes accessed | tf_op | source)
XLA Modules:
  0.0 130.8 jit_solution(6872339936915921019)
XLA Ops:
  1.4 3.1 %fusion.33 = f32[16,4608]{1,0:T(8,128)S(1)} fusion(bf16[16,512]{1,0:T(8,128)(2,1)S(1)} %copy-done, bf16[512,4608]{1,0:T(8,128)(2,1)} %param.9), kind=kOutput, calls=%fused_computation.71 | convolution fusion | flops 75497472 | bytes 5029888 | tf_op jit(solution)/shard_map/dot_general | solution.py:290
  4.5 1.5 %collective-permute-start = (f32[16,2304]{1,0:T(8,128)S(1)}, f32[16,2304]{1,0:T(8,128)S(1)}, u32[]{:S(2)}, u32[]{:S(2)}) collective-permute-start(f32[16,2304]{1,0:T(8,128)S(1)} %slice_select_fusion.2), channel_id=1, source_target_pairs={{0,32},{32,0},{2,34},{34,2},{4,36},{36,4},{6,38},{38,6},{64,96},{9... | collective-permute-start | bytes 442376 | tf_op jit(solution)/shard_map/ppermute | solution.py:38
  8.5 3.7 %collective-permute-done.1 = f32[16,2304]{1,0:T(8,128)S(1)} collective-permute-done((f32[16,2304]{1,0:T(8,128)S(1)}, f32[16,2304]{1,0:T(8,128)S(1)}, u32[]{:S(2)}, u32[]{:S(2)}) %collective-permute-start.1) | collective-permute-done | bytes 147488 | tf_op jit(solution)/shard_map/ppermute | solution.py:316
  15.2 2.8 %collective-permute-start.3 = (bf16[16,2304]{1,0:T(8,128)(2,1)S(1)}, bf16[16,2304]{1,0:T(8,128)(2,1)S(1)}, u32[]{:S(2)}, u32[]{:S(2)}) collective-permute-start(bf16[16,2304]{1,0:T(8,128)(2,1)S(1)} %maximum_select_fusion), channel_id=1, source_target_pairs={{0,65},{32,97},{2,67},{34,99},{4,69},{36,101},{6,71},{38,103},{64,... | collective-permute-start | bytes 221192 | tf_op jit(solution)/shard_map/ppermute | solution.py:38
  18.1 2.2 %collective-permute-done.3 = bf16[16,2304]{1,0:T(8,128)(2,1)S(1)} collective-permute-done((bf16[16,2304]{1,0:T(8,128)(2,1)S(1)}, bf16[16,2304]{1,0:T(8,128)(2,1)S(1)}, u32[]{:S(2)}, u32[]{:S(2)}) %collective-permute-start.3) | collective-permute-done | bytes 73760 | tf_op jit(solution)/shard_map/ppermute | solution.py:38
  20.3 2.4 %collective-permute-start.4 = (bf16[32,2304]{1,0:T(8,128)(2,1)S(1)}, bf16[32,2304]{1,0:T(8,128)(2,1)S(1)}, u32[]{:S(2)}, u32[]{:S(2)}) collective-permute-start(bf16[32,2304]{1,0:T(8,128)(2,1)S(1)} %get-tuple-element.66), channel_id=1, source_target_pairs={{0,6},{32,56},{2,0},{34,58},{4,2},{36,60},{6,4},{38,62},{64,70},{9... | collective-permute-start | bytes 442376 | tf_op jit(solution)/shard_map/ppermute | solution.py:38
  22.8 1.7 %collective-permute-start.5 = (bf16[32,2304]{1,0:T(8,128)(2,1)S(1)}, bf16[32,2304]{1,0:T(8,128)(2,1)S(1)}, u32[]{:S(2)}, u32[]{:S(2)}) collective-permute-start(bf16[32,2304]{1,0:T(8,128)(2,1)S(1)} %get-tuple-element.66), channel_id=1, source_target_pairs={{0,4},{32,48},{2,6},{34,50},{4,0},{36,52},{6,2},{38,54},{64,68},{9... | collective-permute-start | bytes 442376 | tf_op jit(solution)/shard_map/ppermute | solution.py:38
  24.8 3.9 %collective-permute-done.5 = bf16[32,2304]{1,0:T(8,128)(2,1)S(1)} collective-permute-done((bf16[32,2304]{1,0:T(8,128)(2,1)S(1)}, bf16[32,2304]{1,0:T(8,128)(2,1)S(1)}, u32[]{:S(2)}, u32[]{:S(2)}) %collective-permute-start.5) | collective-permute-done | bytes 147488 | tf_op jit(solution)/shard_map/ppermute | solution.py:38
  30.0 1.5 %collective-permute-start.11 = (bf16[128,2304]{1,0:T(8,128)(2,1)S(1)}, bf16[128,2304]{1,0:T(8,128)(2,1)S(1)}, u32[]{:S(2)}, u32[]{:S(2)}) collective-permute-start(bf16[128,2304]{1,0:T(8,128)(2,1)S(1)} %subtract_convert_fusion.after_ref.refs_0_), channel_id=1, source_target_pairs={{0,8},{32,34},{2,10},{34,36},{4,12},{36,38},{6,14},{38,32},{64,72}... | collective-permute-start | bytes 1769480 | tf_op jit(solution)/shard_map/ppermute | solution.py:38
  31.6 3.5 %collective-permute-start.10 = (bf16[128,2304]{1,0:T(8,128)(2,1)S(1)}, bf16[128,2304]{1,0:T(8,128)(2,1)S(1)}, u32[]{:S(2)}, u32[]{:S(2)}) collective-permute-start(bf16[128,2304]{1,0:T(8,128)(2,1)S(1)} %subtract_convert_fusion.after_ref.refs_0_), channel_id=1, source_target_pairs={{0,16},{32,36},{2,18},{34,38},{4,20},{36,32},{6,22},{38,34},{64,80... | collective-permute-start | bytes 1769480 | tf_op jit(solution)/shard_map/ppermute | solution.py:38
  35.6 2.3 %copy-done.2 = bf16[4608,512]{1,0:T(8,128)(2,1)S(1)} copy-done((bf16[4608,512]{1,0:T(8,128)(2,1)S(1)}, bf16[4608,512]{1,0:T(8,128)(2,1)}, u32[]{:S(2)}) %copy-start.2) | copy-done | bytes 4718616
  41.9 7.0 %collective-permute-done.10.refs_2_ = bf16[128,2304]{1,0:T(8,128)(2,1)S(1)} collective-permute-done((bf16[128,2304]{1,0:T(8,128)(2,1)S(1)}, bf16[128,2304]{1,0:T(8,128)(2,1)S(1)}, u32[]{:S(2)}, u32[]{:S(2)}) %collective-permute-start.10) | collective-permute-done | bytes 589856 | tf_op jit(solution)/shard_map/ppermute | solution.py:38
  50.1 3.2 %collective-permute-start.12 = (f32[512,512]{1,0:T(8,128)S(1)}, f32[512,512]{1,0:T(8,128)S(1)}, u32[]{:S(2)}, u32[]{:S(2)}) collective-permute-start(f32[512,512]{1,0:T(8,128)S(1)} %bitcast.95), channel_id=1, source_target_pairs={{0,32},{32,0},{2,34},{34,2},{4,36},{36,4},{6,38},{38,6},{64,96},{9... | collective-permute-start | bytes 3145736 | tf_op jit(solution)/shard_map/ppermute | solution.py:38
  60.0 2.0 %collective-permute-start.15 = (bf16[128,2304]{1,0:T(8,128)(2,1)S(1)}, bf16[128,2304]{1,0:T(8,128)(2,1)S(1)}, u32[]{:S(2)}, u32[]{:S(2)}) collective-permute-start(bf16[128,2304]{1,0:T(8,128)(2,1)S(1)} %fusion.2), channel_id=1, source_target_pairs={{0,24},{32,38},{2,26},{34,32},{4,28},{36,34},{6,30},{38,36},{64,88... | collective-permute-start | bytes 1769480 | tf_op jit(solution)/shard_map/ppermute | solution.py:38
  62.6 2.7 %collective-permute-done.19 = bf16[4,2,8,2304]{3,2,1,0:T(8,128)(2,1)S(1)} collective-permute-done((bf16[4,2,8,2304]{3,2,1,0:T(8,128)(2,1)S(1)}, bf16[4,2,8,2304]{3,2,1,0:T(8,128)(2,1)S(1)}, u32[]{:S(2)}, u32[]{:S(2)}) %collective-permute-start.19) | collective-permute-done | bytes 294944 | tf_op jit(solution)/shard_map/ppermute | solution.py:38
  65.5 2.8 %collective-permute-start.20 = (bf16[4,8,2304]{2,1,0:T(8,128)(2,1)S(1)}, bf16[4,8,2304]{2,1,0:T(8,128)(2,1)S(1)}, u32[]{:S(2)}, u32[]{:S(2)}) collective-permute-start(bf16[4,8,2304]{2,1,0:T(8,128)(2,1)S(1)} %slice_bitcast_fusion.1), channel_id=1, source_target_pairs={{0,64},{32,97},{2,66},{34,99},{4,68},{36,101},{6,70},{38,103},{64,... | collective-permute-start | bytes 442376 | tf_op jit(solution)/shard_map/ppermute | solution.py:38
  68.7 2.9 %shard_map.107 = (bf16[2304,512]{1,0:T(8,128)(2,1)S(1)}, bf16[512,512]{1,0:T(8,128)(2,1)S(1)}, bf16[512,512]{1,0:T(8,128)(2,1)S(1)}) custom-call(bf16[128,2304]{1,0:T(8,128)(2,1)S(1)} %subtract_convert_fusion.after_ref.refs_0_, bf16[128,2304]{1,0:T(8,128)(2,1)S(1)} %collective-permute-done.9.refs_1_, bf16[128,2304]{1,0:T(8,128)(2,1)S(1)} %collective-permute-done.10.refs_2_, ...), custom_call_target="tpu_custom_call" | custom-call | bytes 6291456 | tf_op jit(solution)/shard_map/pallas_call | solution.py:103
  71.6 1.7 %shard_map.108 = (bf16[512,2304]{1,0:T(8,128)(2,1)S(1)}, f32[512,1]{1,0:T(8,128)S(1)}, f32[1,512]{1,0:T(1,128)S(1)}) custom-call(s32[1]{0:T(128)} %bitcast.half_ref.core, bf16[128,2304]{1,0:T(8,128)(2,1)S(1)} %fusion.refs_6_._, bf16[512,4608]{1,0:T(8,128)(2,1)S(1)} %bitcast.79, bf16[512,2304]{1,0:T(8,128)(2,1)S(1)} %shard_map.105.own.refs_4_, ...), custom_call_target="tpu_custom_call" | custom-call | bytes 6291456 | tf_op jit(solution)/shard_map/pallas_call | solution.py:103
  74.6 2.4 %collective-permute-start.18 = (bf16[32,2304]{1,0:T(8,128)(2,1)S(1)}, bf16[32,2304]{1,0:T(8,128)(2,1)S(1)}, u32[]{:S(2)}, u32[]{:S(2)}) collective-permute-start(bf16[32,2304]{1,0:T(8,128)(2,1)S(1)} %get-tuple-element.62), channel_id=1, source_target_pairs={{0,1},{32,33},{2,3},{34,35},{4,5},{36,37},{6,7},{38,39},{64,65},{9... | collective-permute-start | bytes 442376 | tf_op jit(solution)/shard_map/ppermute | solution.py:38
  78.0 4.4 %collective-permute-start.28 = (bf16[2304,512]{1,0:T(8,128)(2,1)S(1)}, bf16[2304,512]{1,0:T(8,128)(2,1)S(1)}, u32[]{:S(2)}, u32[]{:S(2)}) collective-permute-start(bf16[2304,512]{1,0:T(8,128)(2,1)S(1)} %get-tuple-element.45.refs_9_), channel_id=1, source_target_pairs={{0,32},{32,0},{2,34},{34,2},{4,36},{36,4},{6,38},{38,6},{64,96},{9... | collective-permute-start | bytes 7077896 | tf_op jit(solution)/shard_map/ppermute | solution.py:38
  82.8 1.7 %collective-permute-start.24 = (bf16[32,2304]{1,0:T(8,128)(2,1)S(1)}, bf16[32,2304]{1,0:T(8,128)(2,1)S(1)}, u32[]{:S(2)}, u32[]{:S(2)}) collective-permute-start(bf16[32,2304]{1,0:T(8,128)(2,1)S(1)} %fusion.12), channel_id=1, source_target_pairs={{0,2},{32,40},{2,4},{34,42},{4,6},{36,44},{6,0},{38,46},{64,66},{9... | collective-permute-start | bytes 442376 | tf_op jit(solution)/shard_map/ppermute | solution.py:38
  85.5 2.8 %collective-permute-start.23 = (bf16[32,2304]{1,0:T(8,128)(2,1)S(1)}, bf16[32,2304]{1,0:T(8,128)(2,1)S(1)}, u32[]{:S(2)}, u32[]{:S(2)}) collective-permute-start(bf16[32,2304]{1,0:T(8,128)(2,1)S(1)} %fusion.12), channel_id=1, source_target_pairs={{0,4},{32,48},{2,6},{34,50},{4,0},{36,52},{6,2},{38,54},{64,68},{9... | collective-permute-start | bytes 442376 | tf_op jit(solution)/shard_map/ppermute | solution.py:38
  89.1 1.9 %collective-permute-done.23 = bf16[32,2304]{1,0:T(8,128)(2,1)S(1)} collective-permute-done((bf16[32,2304]{1,0:T(8,128)(2,1)S(1)}, bf16[32,2304]{1,0:T(8,128)(2,1)S(1)}, u32[]{:S(2)}, u32[]{:S(2)}) %collective-permute-start.23) | collective-permute-done | bytes 147488 | tf_op jit(solution)/shard_map/ppermute | solution.py:38
  92.3 1.8 %collective-permute-start.26 = (bf16[32,2304]{1,0:T(8,128)(2,1)S(1)}, bf16[32,2304]{1,0:T(8,128)(2,1)S(1)}, u32[]{:S(2)}, u32[]{:S(2)}) collective-permute-start(bf16[32,2304]{1,0:T(8,128)(2,1)S(1)} %fusion.7), channel_id=1, source_target_pairs={{0,65},{32,97},{2,67},{34,99},{4,69},{36,101},{6,71},{38,103},{64,... | collective-permute-start | bytes 442376 | tf_op jit(solution)/shard_map/ppermute | solution.py:38
  94.3 4.6 %collective-permute-start.30 = (bf16[32,2304]{1,0:T(8,128)(2,1)S(1)}, bf16[32,2304]{1,0:T(8,128)(2,1)S(1)}, u32[]{:S(2)}, u32[]{:S(2)}) collective-permute-start(bf16[32,2304]{1,0:T(8,128)(2,1)S(1)} %fusion.7), channel_id=1, source_target_pairs={{0,16},{32,36},{2,18},{34,38},{4,20},{36,32},{6,22},{38,34},{64,80... | collective-permute-start | bytes 442376 | tf_op jit(solution)/shard_map/ppermute | solution.py:38
  99.1 4.5 %collective-permute-start.34 = (bf16[128,2304]{1,0:T(8,128)(2,1)S(1)}, bf16[128,2304]{1,0:T(8,128)(2,1)S(1)}, u32[]{:S(2)}, u32[]{:S(2)}) collective-permute-start(bf16[128,2304]{1,0:T(8,128)(2,1)S(1)} %bitcast.83), channel_id=1, source_target_pairs={{0,8},{32,34},{2,10},{34,36},{4,12},{36,38},{6,14},{38,32},{64,72}... | collective-permute-start | bytes 1769480 | tf_op jit(solution)/shard_map/ppermute | solution.py:38
  103.5 2.1 %collective-permute-start.33 = (bf16[32,2304]{1,0:T(8,128)(2,1)S(1)}, bf16[32,2304]{1,0:T(8,128)(2,1)S(1)}, u32[]{:S(2)}, u32[]{:S(2)}) collective-permute-start(bf16[32,2304]{1,0:T(8,128)(2,1)S(1)} %collective-permute-done.30), channel_id=1, source_target_pairs={{0,1},{32,33},{2,3},{34,35},{4,5},{36,37},{6,7},{38,39},{64,65},{9... | collective-permute-start | bytes 442376 | tf_op jit(solution)/shard_map/ppermute | solution.py:38
  106.8 2.2 %collective-permute-done.33 = bf16[32,2304]{1,0:T(8,128)(2,1)S(1)} collective-permute-done((bf16[32,2304]{1,0:T(8,128)(2,1)S(1)}, bf16[32,2304]{1,0:T(8,128)(2,1)S(1)}, u32[]{:S(2)}, u32[]{:S(2)}) %collective-permute-start.33) | collective-permute-done | bytes 147488 | tf_op jit(solution)/shard_map/ppermute | solution.py:38
  109.0 2.1 %collective-permute-done.32 = bf16[32,2304]{1,0:T(8,128)(2,1)S(1)} collective-permute-done((bf16[32,2304]{1,0:T(8,128)(2,1)S(1)}, bf16[32,2304]{1,0:T(8,128)(2,1)S(1)}, u32[]{:S(2)}, u32[]{:S(2)}) %collective-permute-start.32) | collective-permute-done | bytes 147488 | tf_op jit(solution)/shard_map/ppermute | solution.py:38
  111.4 6.7 %collective-permute-start.37 = (bf16[128,2304]{1,0:T(8,128)(2,1)S(1)}, bf16[128,2304]{1,0:T(8,128)(2,1)S(1)}, u32[]{:S(2)}, u32[]{:S(2)}) collective-permute-start(bf16[128,2304]{1,0:T(8,128)(2,1)S(1)} %bitcast.87), channel_id=1, source_target_pairs={{0,32},{32,0},{2,34},{34,2},{4,36},{36,4},{6,38},{38,6},{64,96},{9... | collective-permute-start | bytes 1769480 | tf_op jit(solution)/shard_map/ppermute | solution.py:38
  118.8 3.2 %shard_map.109 = (f32[512,512]{1,0:T(8,128)S(1)}, bf16[512,4608]{1,0:T(8,128)(2,1)}) custom-call(s32[1]{0:T(128)} %bitcast.half_ref.core, bf16[128,2304]{1,0:T(8,128)(2,1)S(1)} %bitcast.86, bf16[128,2304]{1,0:T(8,128)(2,1)S(1)} %collective-permute-done.29.refs_1_, bf16[128,2304]{1,0:T(8,128)(2,1)S(1)} %bitcast.88, ...), custom_call_target="tpu_custom_call" | custom-call | flops 2415919104 | bytes 8388608 | tf_op jit(solution)/shard_map/pallas_call | solution.py:103
  122.2 8.5 %shard_map.110 = (bf16[512,4608]{1,0:T(8,128)(2,1)}, bf16[4608,512]{1,0:T(8,128)(2,1)}, f32[1,512]{1,0:T(1,128)}) custom-call(s32[1]{0:T(128)} %bitcast.half_ref.core, bf16[512,4608]{1,0:T(8,128)(2,1)} %get-tuple-element.48._, f32[512,512]{1,0:T(8,128)S(1)} %get-tuple-element.49.own_acts, ...), custom_call_target="tpu_custom_call", output_to_operand_aliasing={{0}: (1, {})} | custom-call | flops 4831838208 | bytes 16777216 | tf_op jit(solution)/shard_map/pallas_call | solution.py:103
  (125 shorter events, 29.8 us)
Async XLA Ops:
  7.0 5.1 %collective-permute-start.1 = (f32[16,2304]{1,0:T(8,128)S(1)}, f32[16,2304]{1,0:T(8,128)S(1)}, u32[]{:S(2)}, u32[]{:S(2)}) collective-permute-start(f32[16,2304]{1,0:T(8,128)S(1)} %select_add_fusion), channel_id=1, source_target_pairs={{0,64},{64,0},{32,96},{96,32},{1,65},{65,1},{33,97},{97,33},{2,66}... | collective-permute-start | bytes 442376 | tf_op jit(solution)/shard_map/ppermute | solution.py:316
  14.6 15.4 %collective-permute-start.7 = (bf16[4608,512]{1,0:T(8,128)(2,1)}, bf16[4608,512]{1,0:T(8,128)(2,1)S(1)}, u32[]{:S(2)}, u32[]{:S(2)}) collective-permute-start(bf16[4608,512]{1,0:T(8,128)(2,1)} %weight_ref.2), channel_id=1, source_target_pairs={{0,32},{32,0},{2,34},{34,2},{4,36},{36,4},{6,38},{38,6},{64,96},{9... | collective-permute-start | bytes 14155784 | tf_op jit(solution)/shard_map/ppermute | solution.py:38
  15.1 14.9 %collective-permute-start.8 = (bf16[512,4608]{1,0:T(8,128)(2,1)}, bf16[512,4608]{1,0:T(8,128)(2,1)S(1)}, u32[]{:S(2)}, u32[]{:S(2)}) collective-permute-start(bf16[512,4608]{1,0:T(8,128)(2,1)} %weight.1), channel_id=1, source_target_pairs={{0,32},{32,0},{2,34},{34,2},{4,36},{36,4},{6,38},{38,6},{64,96},{9... | collective-permute-start | bytes 14155784 | tf_op jit(solution)/shard_map/ppermute | solution.py:38
  15.2 5.0 %collective-permute-start.3 = (bf16[16,2304]{1,0:T(8,128)(2,1)S(1)}, bf16[16,2304]{1,0:T(8,128)(2,1)S(1)}, u32[]{:S(2)}, u32[]{:S(2)}) collective-permute-start(bf16[16,2304]{1,0:T(8,128)(2,1)S(1)} %maximum_select_fusion), channel_id=1, source_target_pairs={{0,65},{32,97},{2,67},{34,99},{4,69},{36,101},{6,71},{38,103},{64,... | collective-permute-start | bytes 221192 | tf_op jit(solution)/shard_map/ppermute | solution.py:38
  22.7 7.1 %collective-permute-start.6 = (bf16[32,2304]{1,0:T(8,128)(2,1)S(1)}, bf16[32,2304]{1,0:T(8,128)(2,1)S(1)}, u32[]{:S(2)}, u32[]{:S(2)}) collective-permute-start(bf16[32,2304]{1,0:T(8,128)(2,1)S(1)} %get-tuple-element.66), channel_id=1, source_target_pairs={{0,2},{32,40},{2,4},{34,42},{4,6},{36,44},{6,0},{38,46},{64,66},{9... | collective-permute-start | bytes 442376 | tf_op jit(solution)/shard_map/ppermute | solution.py:38
  22.8 5.9 %collective-permute-start.5 = (bf16[32,2304]{1,0:T(8,128)(2,1)S(1)}, bf16[32,2304]{1,0:T(8,128)(2,1)S(1)}, u32[]{:S(2)}, u32[]{:S(2)}) collective-permute-start(bf16[32,2304]{1,0:T(8,128)(2,1)S(1)} %get-tuple-element.66), channel_id=1, source_target_pairs={{0,4},{32,48},{2,6},{34,50},{4,0},{36,52},{6,2},{38,54},{64,68},{9... | collective-permute-start | bytes 442376 | tf_op jit(solution)/shard_map/ppermute | solution.py:38
  30.0 11.4 %collective-permute-start.11 = (bf16[128,2304]{1,0:T(8,128)(2,1)S(1)}, bf16[128,2304]{1,0:T(8,128)(2,1)S(1)}, u32[]{:S(2)}, u32[]{:S(2)}) collective-permute-start(bf16[128,2304]{1,0:T(8,128)(2,1)S(1)} %subtract_convert_fusion.after_ref.refs_0_), channel_id=1, source_target_pairs={{0,8},{32,34},{2,10},{34,36},{4,12},{36,38},{6,14},{38,32},{64,72}... | collective-permute-start | bytes 1769480 | tf_op jit(solution)/shard_map/ppermute | solution.py:38
  31.6 17.3 %collective-permute-start.10 = (bf16[128,2304]{1,0:T(8,128)(2,1)S(1)}, bf16[128,2304]{1,0:T(8,128)(2,1)S(1)}, u32[]{:S(2)}, u32[]{:S(2)}) collective-permute-start(bf16[128,2304]{1,0:T(8,128)(2,1)S(1)} %subtract_convert_fusion.after_ref.refs_0_), channel_id=1, source_target_pairs={{0,16},{32,36},{2,18},{34,38},{4,20},{36,32},{6,22},{38,34},{64,80... | collective-permute-start | bytes 1769480 | tf_op jit(solution)/shard_map/ppermute | solution.py:38
  35.0 14.4 %collective-permute-start.9 = (bf16[128,2304]{1,0:T(8,128)(2,1)S(1)}, bf16[128,2304]{1,0:T(8,128)(2,1)S(1)}, u32[]{:S(2)}, u32[]{:S(2)}) collective-permute-start(bf16[128,2304]{1,0:T(8,128)(2,1)S(1)} %subtract_convert_fusion.after_ref.refs_0_), channel_id=1, source_target_pairs={{0,24},{32,38},{2,26},{34,32},{4,28},{36,34},{6,30},{38,36},{64,88... | collective-permute-start | bytes 1769480 | tf_op jit(solution)/shard_map/ppermute | solution.py:38
  50.1 5.5 %collective-permute-start.12 = (f32[512,512]{1,0:T(8,128)S(1)}, f32[512,512]{1,0:T(8,128)S(1)}, u32[]{:S(2)}, u32[]{:S(2)}) collective-permute-start(f32[512,512]{1,0:T(8,128)S(1)} %bitcast.95), channel_id=1, source_target_pairs={{0,32},{32,0},{2,34},{34,2},{4,36},{36,4},{6,38},{38,6},{64,96},{9... | collective-permute-start | bytes 3145736 | tf_op jit(solution)/shard_map/ppermute | solution.py:38
  59.4 5.9 %collective-permute-start.19 = (bf16[4,2,8,2304]{3,2,1,0:T(8,128)(2,1)S(1)}, bf16[4,2,8,2304]{3,2,1,0:T(8,128)(2,1)S(1)}, u32[]{:S(2)}, u32[]{:S(2)}) collective-permute-start(bf16[4,2,8,2304]{3,2,1,0:T(8,128)(2,1)S(1)} %slice_select_fusion), channel_id=1, source_target_pairs={{0,65},{32,96},{2,67},{34,98},{4,69},{36,100},{6,71},{38,102},{64,... | collective-permute-start | bytes 884744 | tf_op jit(solution)/shard_map/ppermute | solution.py:38
  60.0 13.7 %collective-permute-start.15 = (bf16[128,2304]{1,0:T(8,128)(2,1)S(1)}, bf16[128,2304]{1,0:T(8,128)(2,1)S(1)}, u32[]{:S(2)}, u32[]{:S(2)}) collective-permute-start(bf16[128,2304]{1,0:T(8,128)(2,1)S(1)} %fusion.2), channel_id=1, source_target_pairs={{0,24},{32,38},{2,26},{34,32},{4,28},{36,34},{6,30},{38,36},{64,88... | collective-permute-start | bytes 1769480 | tf_op jit(solution)/shard_map/ppermute | solution.py:38
  62.5 11.2 %collective-permute-start.14 = (bf16[128,2304]{1,0:T(8,128)(2,1)S(1)}, bf16[128,2304]{1,0:T(8,128)(2,1)S(1)}, u32[]{:S(2)}, u32[]{:S(2)}) collective-permute-start(bf16[128,2304]{1,0:T(8,128)(2,1)S(1)} %fusion.1), channel_id=1, source_target_pairs={{0,8},{32,34},{2,10},{34,36},{4,12},{36,38},{6,14},{38,32},{64,72}... | collective-permute-start | bytes 1769480 | tf_op jit(solution)/shard_map/ppermute | solution.py:38
  65.5 7.8 %collective-permute-start.20 = (bf16[4,8,2304]{2,1,0:T(8,128)(2,1)S(1)}, bf16[4,8,2304]{2,1,0:T(8,128)(2,1)S(1)}, u32[]{:S(2)}, u32[]{:S(2)}) collective-permute-start(bf16[4,8,2304]{2,1,0:T(8,128)(2,1)S(1)} %slice_bitcast_fusion.1), channel_id=1, source_target_pairs={{0,64},{32,97},{2,66},{34,99},{4,68},{36,101},{6,70},{38,103},{64,... | collective-permute-start | bytes 442376 | tf_op jit(solution)/shard_map/ppermute | solution.py:38
  73.4 9.0 %collective-permute-start.21 = (bf16[32,2304]{1,0:T(8,128)(2,1)S(1)}, bf16[32,2304]{1,0:T(8,128)(2,1)S(1)}, u32[]{:S(2)}, u32[]{:S(2)}) collective-permute-start(bf16[32,2304]{1,0:T(8,128)(2,1)S(1)} %fusion.13), channel_id=1, source_target_pairs={{0,16},{32,36},{2,18},{34,38},{4,20},{36,32},{6,22},{38,34},{64,80... | collective-permute-start | bytes 442376 | tf_op jit(solution)/shard_map/ppermute | solution.py:38
  74.0 8.3 %collective-permute-start.16 = (bf16[32,2304]{1,0:T(8,128)(2,1)S(1)}, bf16[32,2304]{1,0:T(8,128)(2,1)S(1)}, u32[]{:S(2)}, u32[]{:S(2)}) collective-permute-start(bf16[32,2304]{1,0:T(8,128)(2,1)S(1)} %get-tuple-element.61), channel_id=1, source_target_pairs={{0,64},{32,96},{2,66},{34,98},{4,68},{36,100},{6,70},{38,102},{64,... | collective-permute-start | bytes 442376 | tf_op jit(solution)/shard_map/ppermute | solution.py:38
  74.6 7.8 %collective-permute-start.18 = (bf16[32,2304]{1,0:T(8,128)(2,1)S(1)}, bf16[32,2304]{1,0:T(8,128)(2,1)S(1)}, u32[]{:S(2)}, u32[]{:S(2)}) collective-permute-start(bf16[32,2304]{1,0:T(8,128)(2,1)S(1)} %get-tuple-element.62), channel_id=1, source_target_pairs={{0,1},{32,33},{2,3},{34,35},{4,5},{36,37},{6,7},{38,39},{64,65},{9... | collective-permute-start | bytes 442376 | tf_op jit(solution)/shard_map/ppermute | solution.py:38
  77.0 5.7 %collective-permute-start.17 = (bf16[32,2304]{1,0:T(8,128)(2,1)S(1)}, bf16[32,2304]{1,0:T(8,128)(2,1)S(1)}, u32[]{:S(2)}, u32[]{:S(2)}) collective-permute-start(bf16[32,2304]{1,0:T(8,128)(2,1)S(1)} %get-tuple-element.63), channel_id=1, source_target_pairs={{0,65},{32,97},{2,67},{34,99},{4,69},{36,101},{6,71},{38,103},{64,... | collective-permute-start | bytes 442376 | tf_op jit(solution)/shard_map/ppermute | solution.py:38
  78.0 21.1 %collective-permute-start.28 = (bf16[2304,512]{1,0:T(8,128)(2,1)S(1)}, bf16[2304,512]{1,0:T(8,128)(2,1)S(1)}, u32[]{:S(2)}, u32[]{:S(2)}) collective-permute-start(bf16[2304,512]{1,0:T(8,128)(2,1)S(1)} %get-tuple-element.45.refs_9_), channel_id=1, source_target_pairs={{0,32},{32,0},{2,34},{34,2},{4,36},{36,4},{6,38},{38,6},{64,96},{9... | collective-permute-start | bytes 7077896 | tf_op jit(solution)/shard_map/ppermute | solution.py:38
  82.8 5.6 %collective-permute-start.24 = (bf16[32,2304]{1,0:T(8,128)(2,1)S(1)}, bf16[32,2304]{1,0:T(8,128)(2,1)S(1)}, u32[]{:S(2)}, u32[]{:S(2)}) collective-permute-start(bf16[32,2304]{1,0:T(8,128)(2,1)S(1)} %fusion.12), channel_id=1, source_target_pairs={{0,2},{32,40},{2,4},{34,42},{4,6},{36,44},{6,0},{38,46},{64,66},{9... | collective-permute-start | bytes 442376 | tf_op jit(solution)/shard_map/ppermute | solution.py:38
  84.5 4.6 %collective-permute-start.22 = (bf16[32,2304]{1,0:T(8,128)(2,1)S(1)}, bf16[32,2304]{1,0:T(8,128)(2,1)S(1)}, u32[]{:S(2)}, u32[]{:S(2)}) collective-permute-start(bf16[32,2304]{1,0:T(8,128)(2,1)S(1)} %fusion.12), channel_id=1, source_target_pairs={{0,6},{32,56},{2,0},{34,58},{4,2},{36,60},{6,4},{38,62},{64,70},{9... | collective-permute-start | bytes 442376 | tf_op jit(solution)/shard_map/ppermute | solution.py:38
  85.5 5.5 %collective-permute-start.23 = (bf16[32,2304]{1,0:T(8,128)(2,1)S(1)}, bf16[32,2304]{1,0:T(8,128)(2,1)S(1)}, u32[]{:S(2)}, u32[]{:S(2)}) collective-permute-start(bf16[32,2304]{1,0:T(8,128)(2,1)S(1)} %fusion.12), channel_id=1, source_target_pairs={{0,4},{32,48},{2,6},{34,50},{4,0},{36,52},{6,2},{38,54},{64,68},{9... | collective-permute-start | bytes 442376 | tf_op jit(solution)/shard_map/ppermute | solution.py:38
  91.2 7.8 %collective-permute-start.27 = (bf16[32,2304]{1,0:T(8,128)(2,1)S(1)}, bf16[32,2304]{1,0:T(8,128)(2,1)S(1)}, u32[]{:S(2)}, u32[]{:S(2)}) collective-permute-start(bf16[32,2304]{1,0:T(8,128)(2,1)S(1)} %fusion.7), channel_id=1, source_target_pairs={{0,1},{32,33},{2,3},{34,35},{4,5},{36,37},{6,7},{38,39},{64,65},{9... | collective-permute-start | bytes 442376 | tf_op jit(solution)/shard_map/ppermute | solution.py:38
  92.3 6.6 %collective-permute-start.26 = (bf16[32,2304]{1,0:T(8,128)(2,1)S(1)}, bf16[32,2304]{1,0:T(8,128)(2,1)S(1)}, u32[]{:S(2)}, u32[]{:S(2)}) collective-permute-start(bf16[32,2304]{1,0:T(8,128)(2,1)S(1)} %fusion.7), channel_id=1, source_target_pairs={{0,65},{32,97},{2,67},{34,99},{4,69},{36,101},{6,71},{38,103},{64,... | collective-permute-start | bytes 442376 | tf_op jit(solution)/shard_map/ppermute | solution.py:38
  94.1 4.9 %collective-permute-start.25 = (bf16[32,2304]{1,0:T(8,128)(2,1)S(1)}, bf16[32,2304]{1,0:T(8,128)(2,1)S(1)}, u32[]{:S(2)}, u32[]{:S(2)}) collective-permute-start(bf16[32,2304]{1,0:T(8,128)(2,1)S(1)} %fusion.7), channel_id=1, source_target_pairs={{0,64},{32,96},{2,66},{34,98},{4,68},{36,100},{6,70},{38,102},{64,... | collective-permute-start | bytes 442376 | tf_op jit(solution)/shard_map/ppermute | solution.py:38
  94.3 9.2 %collective-permute-start.30 = (bf16[32,2304]{1,0:T(8,128)(2,1)S(1)}, bf16[32,2304]{1,0:T(8,128)(2,1)S(1)}, u32[]{:S(2)}, u32[]{:S(2)}) collective-permute-start(bf16[32,2304]{1,0:T(8,128)(2,1)S(1)} %fusion.7), channel_id=1, source_target_pairs={{0,16},{32,36},{2,18},{34,38},{4,20},{36,32},{6,22},{38,34},{64,80... | collective-permute-start | bytes 442376 | tf_op jit(solution)/shard_map/ppermute | solution.py:38
  99.1 19.0 %collective-permute-start.34 = (bf16[128,2304]{1,0:T(8,128)(2,1)S(1)}, bf16[128,2304]{1,0:T(8,128)(2,1)S(1)}, u32[]{:S(2)}, u32[]{:S(2)}) collective-permute-start(bf16[128,2304]{1,0:T(8,128)(2,1)S(1)} %bitcast.83), channel_id=1, source_target_pairs={{0,8},{32,34},{2,10},{34,36},{4,12},{36,38},{6,14},{38,32},{64,72}... | collective-permute-start | bytes 1769480 | tf_op jit(solution)/shard_map/ppermute | solution.py:38
  103.5 15.0 %collective-permute-start.29 = (bf16[128,2304]{1,0:T(8,128)(2,1)S(1)}, bf16[128,2304]{1,0:T(8,128)(2,1)S(1)}, u32[]{:S(2)}, u32[]{:S(2)}) collective-permute-start(bf16[128,2304]{1,0:T(8,128)(2,1)S(1)} %bitcast.84), channel_id=1, source_target_pairs={{0,24},{32,38},{2,26},{34,32},{4,28},{36,34},{6,30},{38,36},{64,88... | collective-permute-start | bytes 1769480 | tf_op jit(solution)/shard_map/ppermute | solution.py:38
  103.5 5.5 %collective-permute-start.33 = (bf16[32,2304]{1,0:T(8,128)(2,1)S(1)}, bf16[32,2304]{1,0:T(8,128)(2,1)S(1)}, u32[]{:S(2)}, u32[]{:S(2)}) collective-permute-start(bf16[32,2304]{1,0:T(8,128)(2,1)S(1)} %collective-permute-done.30), channel_id=1, source_target_pairs={{0,1},{32,33},{2,3},{34,35},{4,5},{36,37},{6,7},{38,39},{64,65},{9... | collective-permute-start | bytes 442376 | tf_op jit(solution)/shard_map/ppermute | solution.py:38
  105.6 5.5 %collective-permute-start.32 = (bf16[32,2304]{1,0:T(8,128)(2,1)S(1)}, bf16[32,2304]{1,0:T(8,128)(2,1)S(1)}, u32[]{:S(2)}, u32[]{:S(2)}) collective-permute-start(bf16[32,2304]{1,0:T(8,128)(2,1)S(1)} %collective-permute-done.30), channel_id=1, source_target_pairs={{0,65},{32,97},{2,67},{34,99},{4,69},{36,101},{6,71},{38,103},{64,... | collective-permute-start | bytes 442376 | tf_op jit(solution)/shard_map/ppermute | solution.py:38
  106.3 4.9 %collective-permute-start.31 = (bf16[32,2304]{1,0:T(8,128)(2,1)S(1)}, bf16[32,2304]{1,0:T(8,128)(2,1)S(1)}, u32[]{:S(2)}, u32[]{:S(2)}) collective-permute-start(bf16[32,2304]{1,0:T(8,128)(2,1)S(1)} %collective-permute-done.30), channel_id=1, source_target_pairs={{0,64},{32,96},{2,66},{34,98},{4,68},{36,100},{6,70},{38,102},{64,... | collective-permute-start | bytes 442376 | tf_op jit(solution)/shard_map/ppermute | solution.py:38
  111.4 10.7 %collective-permute-start.37 = (bf16[128,2304]{1,0:T(8,128)(2,1)S(1)}, bf16[128,2304]{1,0:T(8,128)(2,1)S(1)}, u32[]{:S(2)}, u32[]{:S(2)}) collective-permute-start(bf16[128,2304]{1,0:T(8,128)(2,1)S(1)} %bitcast.87), channel_id=1, source_target_pairs={{0,32},{32,0},{2,34},{34,2},{4,36},{36,4},{6,38},{38,6},{64,96},{9... | collective-permute-start | bytes 1769480 | tf_op jit(solution)/shard_map/ppermute | solution.py:38
  (16 other events, 88.6 us)

commit v5 on v4

--- a/solution.py
+++ b/solution.py
@@ -216,23 +216,9 @@
     pieces, refs = refs[:4], refs[4:]
     (weight, act, factor, penalty, rectified, flipped_own, flipped_mate) = refs[:7]
     (out, out_encoder, out_bias) = refs[7:10]
-    (errors, stage, turned, grads, grads_mate, encoder_stage, sems, encoder_sems) = refs[10:18]
-    (streams, stream_sems) = refs[18:]
-    loads = []
-    for k, flipped in enumerate((flipped_own, flipped_mate)):
-        for j in range(HALF // STEP):
-            slot = k * (HALF // STEP) + j
-            rows = slice(j * STEP, j * STEP + STEP)
-            loads.append(
-                pltpu.make_async_copy(flipped.at[rows, :], streams.at[slot], stream_sems.at[slot])
-            )
-            loads[-1].start()
+    (errors, stage, turned, grads, grads_mate, encoder_stage, sems, encoder_sems) = refs[10:]
     join(pieces, errors)
-    total = jnp.zeros((TOKENS, TOKENS), f32)
-    for j in range(HALF // STEP):
-        span = slice(j * STEP, j * STEP + STEP)
-        total = total + times_rows(errors[:, span], weight[:, span])
-    turned[...] = total
+    turned[...] = times_rows(errors[...], weight[...])
     bias = jnp.zeros((1, TOKENS), f32)
     for major in range(4):
         for minor in range(4):
@@ -244,12 +230,12 @@
             bias = bias + jnp.sum(rounded.astype(f32), axis=0, keepdims=True)
     out_bias[...] = bias
     copies = []
-    for k, grad in enumerate((grads, grads_mate)):
+    for k, (flipped, grad) in enumerate(((flipped_own, grads), (flipped_mate, grads_mate))):
         half = core[0] if k == 0 else 1 - core[0]
         for j in range(HALF // STEP):
             slot = k * (HALF // STEP) + j
-            loads[slot].wait()
-            part = jnp.dot(streams[slot], grad[...], preferred_element_type=f32)
+            part = flipped[j * STEP : j * STEP + STEP, :]
+            part = jnp.dot(part, grad[...], preferred_element_type=f32)
             encoder_stage[slot] = part.astype(bf16)
             rows = pl.ds(pl.multiple_of(half * HALF + j * STEP, STEP), STEP)
             copies.append(
@@ -265,7 +251,7 @@
 
 def last_gradients(core, grad_decoder, grad_acts, errors, *rest):
     ins = [(core, pltpu.SMEM), (grad_decoder, None), (grad_acts, VMEM)]
-    ins += [(v, VMEM) for v in [*errors, *rest[:-2]]] + [(v, None) for v in rest[-2:]]
+    ins += [(v, VMEM) for v in [*errors, *rest]]
     outs = [((TOKENS, D), bf16, None), ((D, TOKENS), bf16, None), ((1, TOKENS), f32, VMEM)]
     steps = HALF // STEP
     scratch = [
@@ -276,8 +262,6 @@
         pltpu.VMEM((TOKENS, TOKENS), bf16),
         pltpu.VMEM((2 * steps, STEP, TOKENS), bf16),
         pltpu.SemaphoreType.DMA((steps,)),
-        pltpu.SemaphoreType.DMA((2 * steps,)),
-        pltpu.VMEM((2 * steps, STEP, TOKENS), bf16),
         pltpu.SemaphoreType.DMA((2 * steps,)),
     ]
     flops = 8 * TOKENS * TOKENS * HALF
@@ -313,7 +297,12 @@
     core = (here % 2).reshape(1)
     partial_value = dot(head_outputs, out_weight)
     both = own_half(partial_value) + to_core(other_half(partial_value))
+    encoder_other = cut(encoder_weight, 0, 1 - core, both)
+    decoder_other = cut(decoder_weight, 1, 1 - core, both)
     projected = both + lax.ppermute(both, "prod", [(0, 2), (2, 0), (1, 3), (3, 1)])
+    projected, encoder_other, decoder_other = lax.optimization_barrier(
+        (projected, encoder_other, decoder_other)
+    )
     squares = jnp.broadcast_to(jnp.sum(projected * projected, axis=1, keepdims=True), (16, 128))
     squares = (squares + to_core(squares))[:, :1]
     gain = own_half(post_gain)
@@ -321,11 +310,11 @@
     stream = (own_half(residual_input).astype(f32) + normed).astype(bf16)
     stream = jnp.where(low, stream, jnp.roll(stream, 8, axis=0))
 
-    stream, encoder_send, decoder_send = lax.optimization_barrier(
-        (stream, encoder_weight, decoder_weight)
-    )
-    encoder_mate = to_core(encoder_send)
-    decoder_mate = to_core(decoder_send)
+    stream, encoder_other, decoder_other = lax.optimization_barrier(
+        (stream, encoder_other, decoder_other)
+    )
+    encoder_mate = to_core(encoder_other)
+    decoder_mate = to_core(decoder_other)
     bias_own = own_half(decoder_bias)
     stream = jnp.concatenate([stream, to_y(stream, 3)])
     stream = jnp.concatenate([stream] + [to_minor(stream, -d) for d in (1, 2, 3)])
@@ -334,8 +323,8 @@
     centred, encoder_mate, decoder_mate = lax.optimization_barrier(
         (centred, encoder_mate, decoder_mate)
     )
-    encoder_mate = cut(encoder_mate, 0, core, centred)
-    decoder_mate = cut(decoder_mate, 1, core, centred)
+    encoder_mate = cut(encoder_mate, 0, core * 0, centred)
+    decoder_mate = cut(decoder_mate, 1, core * 0, centred)
     encoder_own = cut(encoder_weight, 0, core, centred)
     decoder_own = cut(decoder_weight, 1, core, centred)
     centred = [centred] + [to_major(centred, -d) for d in (1, 2, 3)]

time: 131 us -> 130 us (level)
  waiting for transfers between devices: 32.3 us -> 28.1 us
  local copies, waits for them, and re-layouts: 3.84 us -> 6.88 us
    ppermute x1, waiting for transfers between devices: 3.69 us -> 0.01 us  [local(): lax.ppermute(both, 'prod', [(0, 2), (2, 0), (1, 3), (3, 1)])]
    unnamed x21 -> x27, local copies, waits for them, and re-layouts: 3.6 us -> 6.63 us
    pallas_call x8 -> x10, Pallas kernels: 17.7 us -> 17.3 us  [call(): pl.pallas_call(kernel, out_shape=tuple((jax.ShapeDtypeStruct(shape, dtype...]
  transfers between devices with their start and end apart: 39 -> 39, of which waited for: 19 -> 18; matrix products, arithmetic and copies ran while one was open for 5% -> 5% of each run, Pallas kernels for 7% -> 8%
where the time goes in v5:
time: 130 us
  starting transfers between devices  63.4 us (49%)
  waiting for transfers between devices  28.1 us (22%)
  Pallas kernels  17.3 us (13%)
  matrix products  11 us (8%)
  local copies, waits for them, and re-layouts  6.88 us (5%)
  other arithmetic  1.52 us (1%)
  between operations  1.38 us (1%)
    ppermute x38, starting transfers between devices, move(): return lax.ppermute(value, AXES, route(step))  61.9 us
    ppermute x38, waiting for transfers between devices, move(): return lax.ppermute(value, AXES, route(step))  28.1 us
    pallas_call x10, Pallas kernels, call(): pl.pallas_call(kernel, out_shape=tuple((jax.ShapeDtypeStruct(shape, dtype...  17.3 us
    dot_general x17, matrix products, dot(): return jnp.dot(a, b, preferred_element_type=f32)  11 us
    unnamed x27, local copies, waits for them, and re-layouts  6.63 us
  transfers between devices with their start and end apart: 39, of which 18 were waited for; matrix products, arithmetic and copies ran while one was open for 5% of the time, Pallas kernels for 8%

profile of v5, /device:TPU:1, one launch (start us, length us, event | category | flops | bytes accessed | tf_op | source)
XLA Modules:
  0.0 129.5 jit_solution(3576703276456883818)
XLA Ops:
  1.4 3.2 %fusion.33 = f32[16,4608]{1,0:T(8,128)S(1)} fusion(bf16[16,512]{1,0:T(8,128)(2,1)S(1)} %copy-done, bf16[512,4608]{1,0:T(8,128)(2,1)} %param.9), kind=kOutput, calls=%fused_computation.71 | convolution fusion | flops 75497472 | bytes 5029888 | tf_op jit(solution)/shard_map/dot_general | solution.py:274
  4.6 1.5 %collective-permute-start = (f32[16,2304]{1,0:T(8,128)S(1)}, f32[16,2304]{1,0:T(8,128)S(1)}, u32[]{:S(2)}, u32[]{:S(2)}) collective-permute-start(f32[16,2304]{1,0:T(8,128)S(1)} %slice_select_fusion.2), channel_id=1, source_target_pairs={{0,32},{32,0},{2,34},{34,2},{4,36},{36,4},{6,38},{38,6},{64,96},{9... | collective-permute-start | bytes 442376 | tf_op jit(solution)/shard_map/ppermute | solution.py:38
  8.8 2.1 %copy-done.3 = bf16[4608,512]{1,0:T(8,128)(2,1)S(1)} copy-done((bf16[4608,512]{1,0:T(8,128)(2,1)S(1)}, bf16[4608,512]{1,0:T(8,128)(2,1)}, u32[]{:S(2)}) %copy-start.3) | copy-done | bytes 4718616
  14.8 2.8 %collective-permute-start.3 = (bf16[16,2304]{1,0:T(8,128)(2,1)S(1)}, bf16[16,2304]{1,0:T(8,128)(2,1)S(1)}, u32[]{:S(2)}, u32[]{:S(2)}) collective-permute-start(bf16[16,2304]{1,0:T(8,128)(2,1)S(1)} %maximum_select_fusion), channel_id=1, source_target_pairs={{0,65},{32,97},{2,67},{34,99},{4,69},{36,101},{6,71},{38,103},{64,... | collective-permute-start | bytes 221192 | tf_op jit(solution)/shard_map/ppermute | solution.py:38
  18.3 1.5 %collective-permute-done.3 = bf16[16,2304]{1,0:T(8,128)(2,1)S(1)} collective-permute-done((bf16[16,2304]{1,0:T(8,128)(2,1)S(1)}, bf16[16,2304]{1,0:T(8,128)(2,1)S(1)}, u32[]{:S(2)}, u32[]{:S(2)}) %collective-permute-start.3) | collective-permute-done | bytes 73760 | tf_op jit(solution)/shard_map/ppermute | solution.py:38
  19.8 2.5 %collective-permute-start.4 = (bf16[32,2304]{1,0:T(8,128)(2,1)S(1)}, bf16[32,2304]{1,0:T(8,128)(2,1)S(1)}, u32[]{:S(2)}, u32[]{:S(2)}) collective-permute-start(bf16[32,2304]{1,0:T(8,128)(2,1)S(1)} %get-tuple-element.70), channel_id=1, source_target_pairs={{0,6},{32,56},{2,0},{34,58},{4,2},{36,60},{6,4},{38,62},{64,70},{9... | collective-permute-start | bytes 442376 | tf_op jit(solution)/shard_map/ppermute | solution.py:38
  22.4 1.7 %collective-permute-start.5 = (bf16[32,2304]{1,0:T(8,128)(2,1)S(1)}, bf16[32,2304]{1,0:T(8,128)(2,1)S(1)}, u32[]{:S(2)}, u32[]{:S(2)}) collective-permute-start(bf16[32,2304]{1,0:T(8,128)(2,1)S(1)} %get-tuple-element.70), channel_id=1, source_target_pairs={{0,4},{32,48},{2,6},{34,50},{4,0},{36,52},{6,2},{38,54},{64,68},{9... | collective-permute-start | bytes 442376 | tf_op jit(solution)/shard_map/ppermute | solution.py:38
  24.5 3.9 %collective-permute-done.5 = bf16[32,2304]{1,0:T(8,128)(2,1)S(1)} collective-permute-done((bf16[32,2304]{1,0:T(8,128)(2,1)S(1)}, bf16[32,2304]{1,0:T(8,128)(2,1)S(1)}, u32[]{:S(2)}, u32[]{:S(2)}) %collective-permute-start.5) | collective-permute-done | bytes 147488 | tf_op jit(solution)/shard_map/ppermute | solution.py:38
  29.7 1.5 %collective-permute-start.11 = (bf16[128,2304]{1,0:T(8,128)(2,1)S(1)}, bf16[128,2304]{1,0:T(8,128)(2,1)S(1)}, u32[]{:S(2)}, u32[]{:S(2)}) collective-permute-start(bf16[128,2304]{1,0:T(8,128)(2,1)S(1)} %subtract_convert_fusion.after_ref.refs_0_), channel_id=1, source_target_pairs={{0,8},{32,34},{2,10},{34,36},{4,12},{36,38},{6,14},{38,32},{64,72}... | collective-permute-start | bytes 1769480 | tf_op jit(solution)/shard_map/ppermute | solution.py:38
  31.2 3.5 %collective-permute-start.10 = (bf16[128,2304]{1,0:T(8,128)(2,1)S(1)}, bf16[128,2304]{1,0:T(8,128)(2,1)S(1)}, u32[]{:S(2)}, u32[]{:S(2)}) collective-permute-start(bf16[128,2304]{1,0:T(8,128)(2,1)S(1)} %subtract_convert_fusion.after_ref.refs_0_), channel_id=1, source_target_pairs={{0,16},{32,36},{2,18},{34,38},{4,20},{36,32},{6,22},{38,34},{64,80... | collective-permute-start | bytes 1769480 | tf_op jit(solution)/shard_map/ppermute | solution.py:38
  35.2 2.3 %copy-done.4 = bf16[4608,512]{1,0:T(8,128)(2,1)S(1)} copy-done((bf16[4608,512]{1,0:T(8,128)(2,1)S(1)}, bf16[4608,512]{1,0:T(8,128)(2,1)}, u32[]{:S(2)}) %copy-start.4) | copy-done | bytes 4718616
  41.5 7.0 %collective-permute-done.10.refs_2_ = bf16[128,2304]{1,0:T(8,128)(2,1)S(1)} collective-permute-done((bf16[128,2304]{1,0:T(8,128)(2,1)S(1)}, bf16[128,2304]{1,0:T(8,128)(2,1)S(1)}, u32[]{:S(2)}, u32[]{:S(2)}) %collective-permute-start.10) | collective-permute-done | bytes 589856 | tf_op jit(solution)/shard_map/ppermute | solution.py:38
  49.7 3.2 %collective-permute-start.12 = (f32[512,512]{1,0:T(8,128)S(1)}, f32[512,512]{1,0:T(8,128)S(1)}, u32[]{:S(2)}, u32[]{:S(2)}) collective-permute-start(f32[512,512]{1,0:T(8,128)S(1)} %bitcast.95), channel_id=1, source_target_pairs={{0,32},{32,0},{2,34},{34,2},{4,36},{36,4},{6,38},{38,6},{64,96},{9... | collective-permute-start | bytes 3145736 | tf_op jit(solution)/shard_map/ppermute | solution.py:38
  59.7 1.9 %collective-permute-start.15 = (bf16[128,2304]{1,0:T(8,128)(2,1)S(1)}, bf16[128,2304]{1,0:T(8,128)(2,1)S(1)}, u32[]{:S(2)}, u32[]{:S(2)}) collective-permute-start(bf16[128,2304]{1,0:T(8,128)(2,1)S(1)} %fusion.2), channel_id=1, source_target_pairs={{0,24},{32,38},{2,26},{34,32},{4,28},{36,34},{6,30},{38,36},{64,88... | collective-permute-start | bytes 1769480 | tf_op jit(solution)/shard_map/ppermute | solution.py:38
  62.2 2.7 %collective-permute-done.19 = bf16[4,2,8,2304]{3,2,1,0:T(8,128)(2,1)S(1)} collective-permute-done((bf16[4,2,8,2304]{3,2,1,0:T(8,128)(2,1)S(1)}, bf16[4,2,8,2304]{3,2,1,0:T(8,128)(2,1)S(1)}, u32[]{:S(2)}, u32[]{:S(2)}) %collective-permute-start.19) | collective-permute-done | bytes 294944 | tf_op jit(solution)/shard_map/ppermute | solution.py:38
  65.1 2.8 %collective-permute-start.20 = (bf16[4,8,2304]{2,1,0:T(8,128)(2,1)S(1)}, bf16[4,8,2304]{2,1,0:T(8,128)(2,1)S(1)}, u32[]{:S(2)}, u32[]{:S(2)}) collective-permute-start(bf16[4,8,2304]{2,1,0:T(8,128)(2,1)S(1)} %slice_bitcast_fusion.1), channel_id=1, source_target_pairs={{0,64},{32,97},{2,66},{34,99},{4,68},{36,101},{6,70},{38,103},{64,... | collective-permute-start | bytes 442376 | tf_op jit(solution)/shard_map/ppermute | solution.py:38
  68.4 2.9 %shard_map.109 = (bf16[2304,512]{1,0:T(8,128)(2,1)S(1)}, bf16[512,512]{1,0:T(8,128)(2,1)S(1)}, bf16[512,512]{1,0:T(8,128)(2,1)S(1)}) custom-call(bf16[128,2304]{1,0:T(8,128)(2,1)S(1)} %subtract_convert_fusion.after_ref.refs_0_, bf16[128,2304]{1,0:T(8,128)(2,1)S(1)} %collective-permute-done.9.refs_1_, bf16[128,2304]{1,0:T(8,128)(2,1)S(1)} %collective-permute-done.10.refs_2_, ...), custom_call_target="tpu_custom_call" | custom-call | bytes 6291456 | tf_op jit(solution)/shard_map/pallas_call | solution.py:103
  71.2 1.7 %shard_map.110 = (bf16[512,2304]{1,0:T(8,128)(2,1)S(1)}, f32[512,1]{1,0:T(8,128)S(1)}, f32[1,512]{1,0:T(1,128)S(1)}) custom-call(s32[1]{0:T(128)} %bitcast.half_ref.core, bf16[128,2304]{1,0:T(8,128)(2,1)S(1)} %fusion.refs_6_._, bf16[512,4608]{1,0:T(8,128)(2,1)S(1)} %bitcast.79, bf16[512,2304]{1,0:T(8,128)(2,1)S(1)} %shard_map.107.own.refs_4_, ...), custom_call_target="tpu_custom_call" | custom-call | bytes 6291456 | tf_op jit(solution)/shard_map/pallas_call | solution.py:103
  74.2 2.4 %collective-permute-start.18 = (bf16[32,2304]{1,0:T(8,128)(2,1)S(1)}, bf16[32,2304]{1,0:T(8,128)(2,1)S(1)}, u32[]{:S(2)}, u32[]{:S(2)}) collective-permute-start(bf16[32,2304]{1,0:T(8,128)(2,1)S(1)} %get-tuple-element.66), channel_id=1, source_target_pairs={{0,1},{32,33},{2,3},{34,35},{4,5},{36,37},{6,7},{38,39},{64,65},{9... | collective-permute-start | bytes 442376 | tf_op jit(solution)/shard_map/ppermute | solution.py:38
  77.6 4.4 %collective-permute-start.28 = (bf16[2304,512]{1,0:T(8,128)(2,1)S(1)}, bf16[2304,512]{1,0:T(8,128)(2,1)S(1)}, u32[]{:S(2)}, u32[]{:S(2)}) collective-permute-start(bf16[2304,512]{1,0:T(8,128)(2,1)S(1)} %get-tuple-element.51.refs_9_), channel_id=1, source_target_pairs={{0,32},{32,0},{2,34},{34,2},{4,36},{36,4},{6,38},{38,6},{64,96},{9... | collective-permute-start | bytes 7077896 | tf_op jit(solution)/shard_map/ppermute | solution.py:38
  82.5 1.7 %collective-permute-start.24 = (bf16[32,2304]{1,0:T(8,128)(2,1)S(1)}, bf16[32,2304]{1,0:T(8,128)(2,1)S(1)}, u32[]{:S(2)}, u32[]{:S(2)}) collective-permute-start(bf16[32,2304]{1,0:T(8,128)(2,1)S(1)} %fusion.12), channel_id=1, source_target_pairs={{0,2},{32,40},{2,4},{34,42},{4,6},{36,44},{6,0},{38,46},{64,66},{9... | collective-permute-start | bytes 442376 | tf_op jit(solution)/shard_map/ppermute | solution.py:38
  85.2 2.8 %collective-permute-start.23 = (bf16[32,2304]{1,0:T(8,128)(2,1)S(1)}, bf16[32,2304]{1,0:T(8,128)(2,1)S(1)}, u32[]{:S(2)}, u32[]{:S(2)}) collective-permute-start(bf16[32,2304]{1,0:T(8,128)(2,1)S(1)} %fusion.12), channel_id=1, source_target_pairs={{0,4},{32,48},{2,6},{34,50},{4,0},{36,52},{6,2},{38,54},{64,68},{9... | collective-permute-start | bytes 442376 | tf_op jit(solution)/shard_map/ppermute | solution.py:38
  88.8 1.9 %collective-permute-done.23 = bf16[32,2304]{1,0:T(8,128)(2,1)S(1)} collective-permute-done((bf16[32,2304]{1,0:T(8,128)(2,1)S(1)}, bf16[32,2304]{1,0:T(8,128)(2,1)S(1)}, u32[]{:S(2)}, u32[]{:S(2)}) %collective-permute-start.23) | collective-permute-done | bytes 147488 | tf_op jit(solution)/shard_map/ppermute | solution.py:38
  90.8 1.5 %collective-permute-start.27 = (bf16[32,2304]{1,0:T(8,128)(2,1)S(1)}, bf16[32,2304]{1,0:T(8,128)(2,1)S(1)}, u32[]{:S(2)}, u32[]{:S(2)}) collective-permute-start(bf16[32,2304]{1,0:T(8,128)(2,1)S(1)} %fusion.7), channel_id=1, source_target_pairs={{0,1},{32,33},{2,3},{34,35},{4,5},{36,37},{6,7},{38,39},{64,65},{9... | collective-permute-start | bytes 442376 | tf_op jit(solution)/shard_map/ppermute | solution.py:38
  94.0 4.5 %collective-permute-start.30 = (bf16[32,2304]{1,0:T(8,128)(2,1)S(1)}, bf16[32,2304]{1,0:T(8,128)(2,1)S(1)}, u32[]{:S(2)}, u32[]{:S(2)}) collective-permute-start(bf16[32,2304]{1,0:T(8,128)(2,1)S(1)} %fusion.7), channel_id=1, source_target_pairs={{0,16},{32,36},{2,18},{34,38},{4,20},{36,32},{6,22},{38,34},{64,80... | collective-permute-start | bytes 442376 | tf_op jit(solution)/shard_map/ppermute | solution.py:38
  98.6 4.5 %collective-permute-start.34 = (bf16[128,2304]{1,0:T(8,128)(2,1)S(1)}, bf16[128,2304]{1,0:T(8,128)(2,1)S(1)}, u32[]{:S(2)}, u32[]{:S(2)}) collective-permute-start(bf16[128,2304]{1,0:T(8,128)(2,1)S(1)} %bitcast.83), channel_id=1, source_target_pairs={{0,8},{32,34},{2,10},{34,36},{4,12},{36,38},{6,14},{38,32},{64,72}... | collective-permute-start | bytes 1769480 | tf_op jit(solution)/shard_map/ppermute | solution.py:38
  103.1 2.1 %collective-permute-start.33 = (bf16[32,2304]{1,0:T(8,128)(2,1)S(1)}, bf16[32,2304]{1,0:T(8,128)(2,1)S(1)}, u32[]{:S(2)}, u32[]{:S(2)}) collective-permute-start(bf16[32,2304]{1,0:T(8,128)(2,1)S(1)} %collective-permute-done.30), channel_id=1, source_target_pairs={{0,1},{32,33},{2,3},{34,35},{4,5},{36,37},{6,7},{38,39},{64,65},{9... | collective-permute-start | bytes 442376 | tf_op jit(solution)/shard_map/ppermute | solution.py:38
  106.3 2.4 %collective-permute-done.33 = bf16[32,2304]{1,0:T(8,128)(2,1)S(1)} collective-permute-done((bf16[32,2304]{1,0:T(8,128)(2,1)S(1)}, bf16[32,2304]{1,0:T(8,128)(2,1)S(1)}, u32[]{:S(2)}, u32[]{:S(2)}) %collective-permute-start.33) | collective-permute-done | bytes 147488 | tf_op jit(solution)/shard_map/ppermute | solution.py:38
  108.6 1.8 %collective-permute-done.32 = bf16[32,2304]{1,0:T(8,128)(2,1)S(1)} collective-permute-done((bf16[32,2304]{1,0:T(8,128)(2,1)S(1)}, bf16[32,2304]{1,0:T(8,128)(2,1)S(1)}, u32[]{:S(2)}, u32[]{:S(2)}) %collective-permute-start.32) | collective-permute-done | bytes 147488 | tf_op jit(solution)/shard_map/ppermute | solution.py:38
  110.8 7.3 %collective-permute-start.37 = (bf16[128,2304]{1,0:T(8,128)(2,1)S(1)}, bf16[128,2304]{1,0:T(8,128)(2,1)S(1)}, u32[]{:S(2)}, u32[]{:S(2)}) collective-permute-start(bf16[128,2304]{1,0:T(8,128)(2,1)S(1)} %bitcast.87), channel_id=1, source_target_pairs={{0,32},{32,0},{2,34},{34,2},{4,36},{36,4},{6,38},{38,6},{64,96},{9... | collective-permute-start | bytes 1769480 | tf_op jit(solution)/shard_map/ppermute | solution.py:38
  118.9 3.2 %shard_map.111 = (f32[512,512]{1,0:T(8,128)S(1)}, bf16[512,4608]{1,0:T(8,128)(2,1)}) custom-call(s32[1]{0:T(128)} %bitcast.half_ref.core, bf16[128,2304]{1,0:T(8,128)(2,1)S(1)} %bitcast.86, bf16[128,2304]{1,0:T(8,128)(2,1)S(1)} %collective-permute-done.29.refs_1_, bf16[128,2304]{1,0:T(8,128)(2,1)S(1)} %bitcast.88, ...), custom_call_target="tpu_custom_call" | custom-call | flops 2415919104 | bytes 8388608 | tf_op jit(solution)/shard_map/pallas_call | solution.py:103
  122.3 7.0 %shard_map.112 = (bf16[512,4608]{1,0:T(8,128)(2,1)}, bf16[4608,512]{1,0:T(8,128)(2,1)}, f32[1,512]{1,0:T(1,128)}) custom-call(s32[1]{0:T(128)} %bitcast.half_ref.core, bf16[512,4608]{1,0:T(8,128)(2,1)} %get-tuple-element.54._, f32[512,512]{1,0:T(8,128)S(1)} %get-tuple-element.55.own_acts, ...), custom_call_target="tpu_custom_call", output_to_operand_aliasing={{0}: (1, {})} | custom-call | flops 4831838208 | bytes 16777216 | tf_op jit(solution)/shard_map/pallas_call | solution.py:103
  (134 shorter events, 31.7 us)
Async XLA Ops:
  7.1 5.7 %collective-permute-start.1 = (f32[16,2304]{1,0:T(8,128)S(1)}, f32[16,2304]{1,0:T(8,128)S(1)}, u32[]{:S(2)}, u32[]{:S(2)}) collective-permute-start(f32[16,2304]{1,0:T(8,128)S(1)} %select_add_fusion.after_ref), channel_id=1, source_target_pairs={{0,64},{64,0},{32,96},{96,32},{1,65},{65,1},{33,97},{97,33},{2,66}... | collective-permute-start | bytes 442376 | tf_op jit(solution)/shard_map/ppermute | solution.py:302
  14.8 5.0 %collective-permute-start.3 = (bf16[16,2304]{1,0:T(8,128)(2,1)S(1)}, bf16[16,2304]{1,0:T(8,128)(2,1)S(1)}, u32[]{:S(2)}, u32[]{:S(2)}) collective-permute-start(bf16[16,2304]{1,0:T(8,128)(2,1)S(1)} %maximum_select_fusion), channel_id=1, source_target_pairs={{0,65},{32,97},{2,67},{34,99},{4,69},{36,101},{6,71},{38,103},{64,... | collective-permute-start | bytes 221192 | tf_op jit(solution)/shard_map/ppermute | solution.py:38
  17.7 12.0 %collective-permute-start.7 = (bf16[2304,512]{1,0:T(8,128)(2,1)}, bf16[2304,512]{1,0:T(8,128)(2,1)S(1)}, u32[]{:S(2)}, u32[]{:S(2)}) collective-permute-start(bf16[2304,512]{1,0:T(8,128)(2,1)} %copy-done.5), channel_id=1, source_target_pairs={{0,32},{32,0},{2,34},{34,2},{4,36},{36,4},{6,38},{38,6},{64,96},{9... | collective-permute-start | bytes 7077896 | tf_op jit(solution)/shard_map/ppermute | solution.py:38
  18.3 11.4 %collective-permute-start.8 = (bf16[512,2304]{1,0:T(8,128)(2,1)S(1)}, bf16[512,2304]{1,0:T(8,128)(2,1)S(1)}, u32[]{:S(2)}, u32[]{:S(2)}) collective-permute-start(bf16[512,2304]{1,0:T(8,128)(2,1)S(1)} %shard_map.104), channel_id=1, source_target_pairs={{0,32},{32,0},{2,34},{34,2},{4,36},{36,4},{6,38},{38,6},{64,96},{9... | collective-permute-start | bytes 7077896 | tf_op jit(solution)/shard_map/ppermute | solution.py:38
  22.3 7.1 %collective-permute-start.6 = (bf16[32,2304]{1,0:T(8,128)(2,1)S(1)}, bf16[32,2304]{1,0:T(8,128)(2,1)S(1)}, u32[]{:S(2)}, u32[]{:S(2)}) collective-permute-start(bf16[32,2304]{1,0:T(8,128)(2,1)S(1)} %get-tuple-element.70), channel_id=1, source_target_pairs={{0,2},{32,40},{2,4},{34,42},{4,6},{36,44},{6,0},{38,46},{64,66},{9... | collective-permute-start | bytes 442376 | tf_op jit(solution)/shard_map/ppermute | solution.py:38
  22.4 5.9 %collective-permute-start.5 = (bf16[32,2304]{1,0:T(8,128)(2,1)S(1)}, bf16[32,2304]{1,0:T(8,128)(2,1)S(1)}, u32[]{:S(2)}, u32[]{:S(2)}) collective-permute-start(bf16[32,2304]{1,0:T(8,128)(2,1)S(1)} %get-tuple-element.70), channel_id=1, source_target_pairs={{0,4},{32,48},{2,6},{34,50},{4,0},{36,52},{6,2},{38,54},{64,68},{9... | collective-permute-start | bytes 442376 | tf_op jit(solution)/shard_map/ppermute | solution.py:38
  29.7 11.4 %collective-permute-start.11 = (bf16[128,2304]{1,0:T(8,128)(2,1)S(1)}, bf16[128,2304]{1,0:T(8,128)(2,1)S(1)}, u32[]{:S(2)}, u32[]{:S(2)}) collective-permute-start(bf16[128,2304]{1,0:T(8,128)(2,1)S(1)} %subtract_convert_fusion.after_ref.refs_0_), channel_id=1, source_target_pairs={{0,8},{32,34},{2,10},{34,36},{4,12},{36,38},{6,14},{38,32},{64,72}... | collective-permute-start | bytes 1769480 | tf_op jit(solution)/shard_map/ppermute | solution.py:38
  31.2 17.3 %collective-permute-start.10 = (bf16[128,2304]{1,0:T(8,128)(2,1)S(1)}, bf16[128,2304]{1,0:T(8,128)(2,1)S(1)}, u32[]{:S(2)}, u32[]{:S(2)}) collective-permute-start(bf16[128,2304]{1,0:T(8,128)(2,1)S(1)} %subtract_convert_fusion.after_ref.refs_0_), channel_id=1, source_target_pairs={{0,16},{32,36},{2,18},{34,38},{4,20},{36,32},{6,22},{38,34},{64,80... | collective-permute-start | bytes 1769480 | tf_op jit(solution)/shard_map/ppermute | solution.py:38
  34.7 14.4 %collective-permute-start.9 = (bf16[128,2304]{1,0:T(8,128)(2,1)S(1)}, bf16[128,2304]{1,0:T(8,128)(2,1)S(1)}, u32[]{:S(2)}, u32[]{:S(2)}) collective-permute-start(bf16[128,2304]{1,0:T(8,128)(2,1)S(1)} %subtract_convert_fusion.after_ref.refs_0_), channel_id=1, source_target_pairs={{0,24},{32,38},{2,26},{34,32},{4,28},{36,34},{6,30},{38,36},{64,88... | collective-permute-start | bytes 1769480 | tf_op jit(solution)/shard_map/ppermute | solution.py:38
  49.7 5.5 %collective-permute-start.12 = (f32[512,512]{1,0:T(8,128)S(1)}, f32[512,512]{1,0:T(8,128)S(1)}, u32[]{:S(2)}, u32[]{:S(2)}) collective-permute-start(f32[512,512]{1,0:T(8,128)S(1)} %bitcast.95), channel_id=1, source_target_pairs={{0,32},{32,0},{2,34},{34,2},{4,36},{36,4},{6,38},{38,6},{64,96},{9... | collective-permute-start | bytes 3145736 | tf_op jit(solution)/shard_map/ppermute | solution.py:38
  59.0 5.9 %collective-permute-start.19 = (bf16[4,2,8,2304]{3,2,1,0:T(8,128)(2,1)S(1)}, bf16[4,2,8,2304]{3,2,1,0:T(8,128)(2,1)S(1)}, u32[]{:S(2)}, u32[]{:S(2)}) collective-permute-start(bf16[4,2,8,2304]{3,2,1,0:T(8,128)(2,1)S(1)} %slice_select_fusion), channel_id=1, source_target_pairs={{0,65},{32,96},{2,67},{34,98},{4,69},{36,100},{6,71},{38,102},{64,... | collective-permute-start | bytes 884744 | tf_op jit(solution)/shard_map/ppermute | solution.py:38
  59.7 13.7 %collective-permute-start.15 = (bf16[128,2304]{1,0:T(8,128)(2,1)S(1)}, bf16[128,2304]{1,0:T(8,128)(2,1)S(1)}, u32[]{:S(2)}, u32[]{:S(2)}) collective-permute-start(bf16[128,2304]{1,0:T(8,128)(2,1)S(1)} %fusion.2), channel_id=1, source_target_pairs={{0,24},{32,38},{2,26},{34,32},{4,28},{36,34},{6,30},{38,36},{64,88... | collective-permute-start | bytes 1769480 | tf_op jit(solution)/shard_map/ppermute | solution.py:38
  62.2 11.2 %collective-permute-start.14 = (bf16[128,2304]{1,0:T(8,128)(2,1)S(1)}, bf16[128,2304]{1,0:T(8,128)(2,1)S(1)}, u32[]{:S(2)}, u32[]{:S(2)}) collective-permute-start(bf16[128,2304]{1,0:T(8,128)(2,1)S(1)} %fusion.1), channel_id=1, source_target_pairs={{0,8},{32,34},{2,10},{34,36},{4,12},{36,38},{6,14},{38,32},{64,72}... | collective-permute-start | bytes 1769480 | tf_op jit(solution)/shard_map/ppermute | solution.py:38
  65.1 7.8 %collective-permute-start.20 = (bf16[4,8,2304]{2,1,0:T(8,128)(2,1)S(1)}, bf16[4,8,2304]{2,1,0:T(8,128)(2,1)S(1)}, u32[]{:S(2)}, u32[]{:S(2)}) collective-permute-start(bf16[4,8,2304]{2,1,0:T(8,128)(2,1)S(1)} %slice_bitcast_fusion.1), channel_id=1, source_target_pairs={{0,64},{32,97},{2,66},{34,99},{4,68},{36,101},{6,70},{38,103},{64,... | collective-permute-start | bytes 442376 | tf_op jit(solution)/shard_map/ppermute | solution.py:38
  73.0 9.1 %collective-permute-start.21 = (bf16[32,2304]{1,0:T(8,128)(2,1)S(1)}, bf16[32,2304]{1,0:T(8,128)(2,1)S(1)}, u32[]{:S(2)}, u32[]{:S(2)}) collective-permute-start(bf16[32,2304]{1,0:T(8,128)(2,1)S(1)} %fusion.13), channel_id=1, source_target_pairs={{0,16},{32,36},{2,18},{34,38},{4,20},{36,32},{6,22},{38,34},{64,80... | collective-permute-start | bytes 442376 | tf_op jit(solution)/shard_map/ppermute | solution.py:38
  73.7 8.4 %collective-permute-start.16 = (bf16[32,2304]{1,0:T(8,128)(2,1)S(1)}, bf16[32,2304]{1,0:T(8,128)(2,1)S(1)}, u32[]{:S(2)}, u32[]{:S(2)}) collective-permute-start(bf16[32,2304]{1,0:T(8,128)(2,1)S(1)} %get-tuple-element.65), channel_id=1, source_target_pairs={{0,64},{32,96},{2,66},{34,98},{4,68},{36,100},{6,70},{38,102},{64,... | collective-permute-start | bytes 442376 | tf_op jit(solution)/shard_map/ppermute | solution.py:38
  74.2 7.8 %collective-permute-start.18 = (bf16[32,2304]{1,0:T(8,128)(2,1)S(1)}, bf16[32,2304]{1,0:T(8,128)(2,1)S(1)}, u32[]{:S(2)}, u32[]{:S(2)}) collective-permute-start(bf16[32,2304]{1,0:T(8,128)(2,1)S(1)} %get-tuple-element.66), channel_id=1, source_target_pairs={{0,1},{32,33},{2,3},{34,35},{4,5},{36,37},{6,7},{38,39},{64,65},{9... | collective-permute-start | bytes 442376 | tf_op jit(solution)/shard_map/ppermute | solution.py:38
  76.7 5.7 %collective-permute-start.17 = (bf16[32,2304]{1,0:T(8,128)(2,1)S(1)}, bf16[32,2304]{1,0:T(8,128)(2,1)S(1)}, u32[]{:S(2)}, u32[]{:S(2)}) collective-permute-start(bf16[32,2304]{1,0:T(8,128)(2,1)S(1)} %get-tuple-element.67), channel_id=1, source_target_pairs={{0,65},{32,97},{2,67},{34,99},{4,69},{36,101},{6,71},{38,103},{64,... | collective-permute-start | bytes 442376 | tf_op jit(solution)/shard_map/ppermute | solution.py:38
  77.6 21.0 %collective-permute-start.28 = (bf16[2304,512]{1,0:T(8,128)(2,1)S(1)}, bf16[2304,512]{1,0:T(8,128)(2,1)S(1)}, u32[]{:S(2)}, u32[]{:S(2)}) collective-permute-start(bf16[2304,512]{1,0:T(8,128)(2,1)S(1)} %get-tuple-element.51.refs_9_), channel_id=1, source_target_pairs={{0,32},{32,0},{2,34},{34,2},{4,36},{36,4},{6,38},{38,6},{64,96},{9... | collective-permute-start | bytes 7077896 | tf_op jit(solution)/shard_map/ppermute | solution.py:38
  82.5 5.6 %collective-permute-start.24 = (bf16[32,2304]{1,0:T(8,128)(2,1)S(1)}, bf16[32,2304]{1,0:T(8,128)(2,1)S(1)}, u32[]{:S(2)}, u32[]{:S(2)}) collective-permute-start(bf16[32,2304]{1,0:T(8,128)(2,1)S(1)} %fusion.12), channel_id=1, source_target_pairs={{0,2},{32,40},{2,4},{34,42},{4,6},{36,44},{6,0},{38,46},{64,66},{9... | collective-permute-start | bytes 442376 | tf_op jit(solution)/shard_map/ppermute | solution.py:38
  84.1 4.6 %collective-permute-start.22 = (bf16[32,2304]{1,0:T(8,128)(2,1)S(1)}, bf16[32,2304]{1,0:T(8,128)(2,1)S(1)}, u32[]{:S(2)}, u32[]{:S(2)}) collective-permute-start(bf16[32,2304]{1,0:T(8,128)(2,1)S(1)} %fusion.12), channel_id=1, source_target_pairs={{0,6},{32,56},{2,0},{34,58},{4,2},{36,60},{6,4},{38,62},{64,70},{9... | collective-permute-start | bytes 442376 | tf_op jit(solution)/shard_map/ppermute | solution.py:38
  85.2 5.5 %collective-permute-start.23 = (bf16[32,2304]{1,0:T(8,128)(2,1)S(1)}, bf16[32,2304]{1,0:T(8,128)(2,1)S(1)}, u32[]{:S(2)}, u32[]{:S(2)}) collective-permute-start(bf16[32,2304]{1,0:T(8,128)(2,1)S(1)} %fusion.12), channel_id=1, source_target_pairs={{0,4},{32,48},{2,6},{34,50},{4,0},{36,52},{6,2},{38,54},{64,68},{9... | collective-permute-start | bytes 442376 | tf_op jit(solution)/shard_map/ppermute | solution.py:38
  90.8 7.7 %collective-permute-start.27 = (bf16[32,2304]{1,0:T(8,128)(2,1)S(1)}, bf16[32,2304]{1,0:T(8,128)(2,1)S(1)}, u32[]{:S(2)}, u32[]{:S(2)}) collective-permute-start(bf16[32,2304]{1,0:T(8,128)(2,1)S(1)} %fusion.7), channel_id=1, source_target_pairs={{0,1},{32,33},{2,3},{34,35},{4,5},{36,37},{6,7},{38,39},{64,65},{9... | collective-permute-start | bytes 442376 | tf_op jit(solution)/shard_map/ppermute | solution.py:38
  92.3 6.2 %collective-permute-start.26 = (bf16[32,2304]{1,0:T(8,128)(2,1)S(1)}, bf16[32,2304]{1,0:T(8,128)(2,1)S(1)}, u32[]{:S(2)}, u32[]{:S(2)}) collective-permute-start(bf16[32,2304]{1,0:T(8,128)(2,1)S(1)} %fusion.7), channel_id=1, source_target_pairs={{0,65},{32,97},{2,67},{34,99},{4,69},{36,101},{6,71},{38,103},{64,... | collective-permute-start | bytes 442376 | tf_op jit(solution)/shard_map/ppermute | solution.py:38
  93.8 4.8 %collective-permute-start.25 = (bf16[32,2304]{1,0:T(8,128)(2,1)S(1)}, bf16[32,2304]{1,0:T(8,128)(2,1)S(1)}, u32[]{:S(2)}, u32[]{:S(2)}) collective-permute-start(bf16[32,2304]{1,0:T(8,128)(2,1)S(1)} %fusion.7), channel_id=1, source_target_pairs={{0,64},{32,96},{2,66},{34,98},{4,68},{36,100},{6,70},{38,102},{64,... | collective-permute-start | bytes 442376 | tf_op jit(solution)/shard_map/ppermute | solution.py:38
  94.0 9.1 %collective-permute-start.30 = (bf16[32,2304]{1,0:T(8,128)(2,1)S(1)}, bf16[32,2304]{1,0:T(8,128)(2,1)S(1)}, u32[]{:S(2)}, u32[]{:S(2)}) collective-permute-start(bf16[32,2304]{1,0:T(8,128)(2,1)S(1)} %fusion.7), channel_id=1, source_target_pairs={{0,16},{32,36},{2,18},{34,38},{4,20},{36,32},{6,22},{38,34},{64,80... | collective-permute-start | bytes 442376 | tf_op jit(solution)/shard_map/ppermute | solution.py:38
  98.6 19.6 %collective-permute-start.34 = (bf16[128,2304]{1,0:T(8,128)(2,1)S(1)}, bf16[128,2304]{1,0:T(8,128)(2,1)S(1)}, u32[]{:S(2)}, u32[]{:S(2)}) collective-permute-start(bf16[128,2304]{1,0:T(8,128)(2,1)S(1)} %bitcast.83), channel_id=1, source_target_pairs={{0,8},{32,34},{2,10},{34,36},{4,12},{36,38},{6,14},{38,32},{64,72}... | collective-permute-start | bytes 1769480 | tf_op jit(solution)/shard_map/ppermute | solution.py:38
  103.1 15.5 %collective-permute-start.29 = (bf16[128,2304]{1,0:T(8,128)(2,1)S(1)}, bf16[128,2304]{1,0:T(8,128)(2,1)S(1)}, u32[]{:S(2)}, u32[]{:S(2)}) collective-permute-start(bf16[128,2304]{1,0:T(8,128)(2,1)S(1)} %bitcast.84), channel_id=1, source_target_pairs={{0,24},{32,38},{2,26},{34,32},{4,28},{36,34},{6,30},{38,36},{64,88... | collective-permute-start | bytes 1769480 | tf_op jit(solution)/shard_map/ppermute | solution.py:38
  103.1 5.5 %collective-permute-start.33 = (bf16[32,2304]{1,0:T(8,128)(2,1)S(1)}, bf16[32,2304]{1,0:T(8,128)(2,1)S(1)}, u32[]{:S(2)}, u32[]{:S(2)}) collective-permute-start(bf16[32,2304]{1,0:T(8,128)(2,1)S(1)} %collective-permute-done.30), channel_id=1, source_target_pairs={{0,1},{32,33},{2,3},{34,35},{4,5},{36,37},{6,7},{38,39},{64,65},{9... | collective-permute-start | bytes 442376 | tf_op jit(solution)/shard_map/ppermute | solution.py:38
  105.2 5.2 %collective-permute-start.32 = (bf16[32,2304]{1,0:T(8,128)(2,1)S(1)}, bf16[32,2304]{1,0:T(8,128)(2,1)S(1)}, u32[]{:S(2)}, u32[]{:S(2)}) collective-permute-start(bf16[32,2304]{1,0:T(8,128)(2,1)S(1)} %collective-permute-done.30), channel_id=1, source_target_pairs={{0,65},{32,97},{2,67},{34,99},{4,69},{36,101},{6,71},{38,103},{64,... | collective-permute-start | bytes 442376 | tf_op jit(solution)/shard_map/ppermute | solution.py:38
  105.8 4.9 %collective-permute-start.31 = (bf16[32,2304]{1,0:T(8,128)(2,1)S(1)}, bf16[32,2304]{1,0:T(8,128)(2,1)S(1)}, u32[]{:S(2)}, u32[]{:S(2)}) collective-permute-start(bf16[32,2304]{1,0:T(8,128)(2,1)S(1)} %collective-permute-done.30), channel_id=1, source_target_pairs={{0,64},{32,96},{2,66},{34,98},{4,68},{36,100},{6,70},{38,102},{64,... | collective-permute-start | bytes 442376 | tf_op jit(solution)/shard_map/ppermute | solution.py:38
  110.8 11.4 %collective-permute-start.37 = (bf16[128,2304]{1,0:T(8,128)(2,1)S(1)}, bf16[128,2304]{1,0:T(8,128)(2,1)S(1)}, u32[]{:S(2)}, u32[]{:S(2)}) collective-permute-start(bf16[128,2304]{1,0:T(8,128)(2,1)S(1)} %bitcast.87), channel_id=1, source_target_pairs={{0,32},{32,0},{2,34},{34,2},{4,36},{36,4},{6,38},{38,6},{64,96},{9... | collective-permute-start | bytes 1769480 | tf_op jit(solution)/shard_map/ppermute | solution.py:38
  (19 other events, 79.4 us)

commit v6 on v5

--- a/solution.py
+++ b/solution.py
@@ -71,6 +71,17 @@
 
 def swap_blocks(value):
     return value.reshape(4, 4, 32, value.shape[-1]).transpose(1, 0, 2, 3).reshape(value.shape)
+
+
+def product_kernel(a, b, out):
+    for j in range(HALF // STEP):
+        span = slice(j * STEP, j * STEP + STEP)
+        out[:, span] = jnp.dot(a[...], b[:, span], preferred_element_type=f32)
+
+
+def product(a, b):
+    outs = [((a.shape[0], b.shape[1]), f32, VMEM)]
+    return call(product_kernel, outs, [(a, VMEM), (b, VMEM)], [], 12, 1024, 1024)[0]
 
 
 def cut_kernel(axis, half_ref, after_ref, weight_ref, out_ref, sems):
@@ -340,11 +351,11 @@
     swapped = swap_blocks(activations)
     mate_activations = to_core(swapped)
 
+    own = product(activations, decoder_own)
     pieces = {}
     for d in range(4):
         rows = slice(128 * d, 128 * d + 128)
-        own = dot(activations[rows], decoder_own)
-        pieces[d] = (own + dot(mate_activations[rows], decoder_mate)).astype(bf16)
+        pieces[d] = (own[rows] + dot(mate_activations[rows], decoder_mate)).astype(bf16)
     far = pieces[2].reshape(4, 4, 8, HALF)
     keep = jnp.where(first, far[:, :2], far[:, ::2])
     send = jnp.where(first, far[:, 2:], far[:, 1::2])

time: 130 us -> 129 us (level)
  matrix products: 11 us -> 9.04 us
  Pallas kernels: 17.3 us -> 18.7 us
    dot_general x17 -> x13, matrix products: 11 us -> 9.04 us  [dot(): return jnp.dot(a, b, preferred_element_type=f32)]
    pallas_call x10 -> x11, Pallas kernels: 17.3 us -> 18.7 us  [call(): pl.pallas_call(kernel, out_shape=tuple((jax.ShapeDtypeStruct(shape, dtype...]
  transfers between devices with their start and end apart: 39 -> 39, of which waited for: 18 -> 17; matrix products, arithmetic and copies ran while one was open for 5% -> 5% of each run, Pallas kernels for 8% -> 9%
where the time goes in v6:
time: 129 us
  starting transfers between devices  64 us (50%)
  waiting for transfers between devices  27.1 us (21%)
  Pallas kernels  18.7 us (14%)
  matrix products  9.04 us (7%)
  local copies, waits for them, and re-layouts  6.87 us (5%)
  other arithmetic  1.52 us (1%)
  between operations  1.36 us (1%)
    ppermute x38, starting transfers between devices, move(): return lax.ppermute(value, AXES, route(step))  62.5 us
    ppermute x38, waiting for transfers between devices, move(): return lax.ppermute(value, AXES, route(step))  27.1 us
    pallas_call x11, Pallas kernels, call(): pl.pallas_call(kernel, out_shape=tuple((jax.ShapeDtypeStruct(shape, dtype...  18.7 us
    dot_general x13, matrix products, dot(): return jnp.dot(a, b, preferred_element_type=f32)  9.04 us
    unnamed x27, local copies, waits for them, and re-layouts  6.63 us
  transfers between devices with their start and end apart: 39, of which 17 were waited for; matrix products, arithmetic and copies ran while one was open for 5% of the time, Pallas kernels for 9%

profile of v6, /device:TPU:1, one launch (start us, length us, event | category | flops | bytes accessed | tf_op | source)
XLA Modules:
  0.0 128.5 jit_solution(13195490766795407339)
XLA Ops:
  1.4 3.2 %fusion.25 = f32[16,4608]{1,0:T(8,128)S(1)} fusion(bf16[16,512]{1,0:T(8,128)(2,1)S(1)} %copy-done, bf16[512,4608]{1,0:T(8,128)(2,1)} %param.9), kind=kOutput, calls=%fused_computation.63 | convolution fusion | flops 75497472 | bytes 5029888 | tf_op jit(solution)/shard_map/dot_general | solution.py:285
  8.8 2.1 %copy-done.3 = bf16[4608,512]{1,0:T(8,128)(2,1)S(1)} copy-done((bf16[4608,512]{1,0:T(8,128)(2,1)S(1)}, bf16[4608,512]{1,0:T(8,128)(2,1)}, u32[]{:S(2)}) %copy-start.3) | copy-done | bytes 4718616
  14.8 2.8 %collective-permute-start.3 = (bf16[16,2304]{1,0:T(8,128)(2,1)S(1)}, bf16[16,2304]{1,0:T(8,128)(2,1)S(1)}, u32[]{:S(2)}, u32[]{:S(2)}) collective-permute-start(bf16[16,2304]{1,0:T(8,128)(2,1)S(1)} %maximum_select_fusion), channel_id=1, source_target_pairs={{0,65},{32,97},{2,67},{34,99},{4,69},{36,101},{6,71},{38,103},{64,... | collective-permute-start | bytes 221192 | tf_op jit(solution)/shard_map/ppermute | solution.py:38
  18.3 1.5 %collective-permute-done.3 = bf16[16,2304]{1,0:T(8,128)(2,1)S(1)} collective-permute-done((bf16[16,2304]{1,0:T(8,128)(2,1)S(1)}, bf16[16,2304]{1,0:T(8,128)(2,1)S(1)}, u32[]{:S(2)}, u32[]{:S(2)}) %collective-permute-start.3) | collective-permute-done | bytes 73760 | tf_op jit(solution)/shard_map/ppermute | solution.py:38
  19.8 2.5 %collective-permute-start.4 = (bf16[32,2304]{1,0:T(8,128)(2,1)S(1)}, bf16[32,2304]{1,0:T(8,128)(2,1)S(1)}, u32[]{:S(2)}, u32[]{:S(2)}) collective-permute-start(bf16[32,2304]{1,0:T(8,128)(2,1)S(1)} %get-tuple-element.70), channel_id=1, source_target_pairs={{0,6},{32,56},{2,0},{34,58},{4,2},{36,60},{6,4},{38,62},{64,70},{9... | collective-permute-start | bytes 442376 | tf_op jit(solution)/shard_map/ppermute | solution.py:38
  22.4 1.7 %collective-permute-start.5 = (bf16[32,2304]{1,0:T(8,128)(2,1)S(1)}, bf16[32,2304]{1,0:T(8,128)(2,1)S(1)}, u32[]{:S(2)}, u32[]{:S(2)}) collective-permute-start(bf16[32,2304]{1,0:T(8,128)(2,1)S(1)} %get-tuple-element.70), channel_id=1, source_target_pairs={{0,4},{32,48},{2,6},{34,50},{4,0},{36,52},{6,2},{38,54},{64,68},{9... | collective-permute-start | bytes 442376 | tf_op jit(solution)/shard_map/ppermute | solution.py:38
  24.5 3.9 %collective-permute-done.5 = bf16[32,2304]{1,0:T(8,128)(2,1)S(1)} collective-permute-done((bf16[32,2304]{1,0:T(8,128)(2,1)S(1)}, bf16[32,2304]{1,0:T(8,128)(2,1)S(1)}, u32[]{:S(2)}, u32[]{:S(2)}) %collective-permute-start.5) | collective-permute-done | bytes 147488 | tf_op jit(solution)/shard_map/ppermute | solution.py:38
  29.7 1.5 %collective-permute-start.11 = (bf16[128,2304]{1,0:T(8,128)(2,1)S(1)}, bf16[128,2304]{1,0:T(8,128)(2,1)S(1)}, u32[]{:S(2)}, u32[]{:S(2)}) collective-permute-start(bf16[128,2304]{1,0:T(8,128)(2,1)S(1)} %subtract_convert_fusion.after_ref.refs_0_), channel_id=1, source_target_pairs={{0,8},{32,34},{2,10},{34,36},{4,12},{36,38},{6,14},{38,32},{64,72}... | collective-permute-start | bytes 1769480 | tf_op jit(solution)/shard_map/ppermute | solution.py:38
  31.2 3.5 %collective-permute-start.10 = (bf16[128,2304]{1,0:T(8,128)(2,1)S(1)}, bf16[128,2304]{1,0:T(8,128)(2,1)S(1)}, u32[]{:S(2)}, u32[]{:S(2)}) collective-permute-start(bf16[128,2304]{1,0:T(8,128)(2,1)S(1)} %subtract_convert_fusion.after_ref.refs_0_), channel_id=1, source_target_pairs={{0,16},{32,36},{2,18},{34,38},{4,20},{36,32},{6,22},{38,34},{64,80... | collective-permute-start | bytes 1769480 | tf_op jit(solution)/shard_map/ppermute | solution.py:38
  35.2 2.3 %copy-done.4 = bf16[4608,512]{1,0:T(8,128)(2,1)S(1)} copy-done((bf16[4608,512]{1,0:T(8,128)(2,1)S(1)}, bf16[4608,512]{1,0:T(8,128)(2,1)}, u32[]{:S(2)}) %copy-start.4) | copy-done | bytes 4718616
  41.5 7.0 %collective-permute-done.10.refs_2_ = bf16[128,2304]{1,0:T(8,128)(2,1)S(1)} collective-permute-done((bf16[128,2304]{1,0:T(8,128)(2,1)S(1)}, bf16[128,2304]{1,0:T(8,128)(2,1)S(1)}, u32[]{:S(2)}, u32[]{:S(2)}) %collective-permute-start.10) | collective-permute-done | bytes 589856 | tf_op jit(solution)/shard_map/ppermute | solution.py:38
  49.7 3.2 %collective-permute-start.12 = (f32[512,512]{1,0:T(8,128)S(1)}, f32[512,512]{1,0:T(8,128)S(1)}, u32[]{:S(2)}, u32[]{:S(2)}) collective-permute-start(f32[512,512]{1,0:T(8,128)S(1)} %bitcast.91), channel_id=1, source_target_pairs={{0,32},{32,0},{2,34},{34,2},{4,36},{36,4},{6,38},{38,6},{64,96},{9... | collective-permute-start | bytes 3145736 | tf_op jit(solution)/shard_map/ppermute | solution.py:38
  59.3 2.9 %collective-permute-start.15 = (bf16[128,2304]{1,0:T(8,128)(2,1)S(1)}, bf16[128,2304]{1,0:T(8,128)(2,1)S(1)}, u32[]{:S(2)}, u32[]{:S(2)}) collective-permute-start(bf16[128,2304]{1,0:T(8,128)(2,1)S(1)} %fusion.2), channel_id=1, source_target_pairs={{0,24},{32,38},{2,26},{34,32},{4,28},{36,34},{6,30},{38,36},{64,88... | collective-permute-start | bytes 1769480 | tf_op jit(solution)/shard_map/ppermute | solution.py:38
  62.2 1.8 %collective-permute-done.19 = bf16[4,2,8,2304]{3,2,1,0:T(8,128)(2,1)S(1)} collective-permute-done((bf16[4,2,8,2304]{3,2,1,0:T(8,128)(2,1)S(1)}, bf16[4,2,8,2304]{3,2,1,0:T(8,128)(2,1)S(1)}, u32[]{:S(2)}, u32[]{:S(2)}) %collective-permute-start.19) | collective-permute-done | bytes 294944 | tf_op jit(solution)/shard_map/ppermute | solution.py:38
  64.1 2.8 %collective-permute-start.20 = (bf16[4,8,2304]{2,1,0:T(8,128)(2,1)S(1)}, bf16[4,8,2304]{2,1,0:T(8,128)(2,1)S(1)}, u32[]{:S(2)}, u32[]{:S(2)}) collective-permute-start(bf16[4,8,2304]{2,1,0:T(8,128)(2,1)S(1)} %slice_bitcast_fusion.1), channel_id=1, source_target_pairs={{0,64},{32,97},{2,66},{34,99},{4,68},{36,101},{6,70},{38,103},{64,... | collective-permute-start | bytes 442376 | tf_op jit(solution)/shard_map/ppermute | solution.py:38
  67.4 2.9 %shard_map.110 = (bf16[2304,512]{1,0:T(8,128)(2,1)S(1)}, bf16[512,512]{1,0:T(8,128)(2,1)S(1)}, bf16[512,512]{1,0:T(8,128)(2,1)S(1)}) custom-call(bf16[128,2304]{1,0:T(8,128)(2,1)S(1)} %subtract_convert_fusion.after_ref.refs_0_, bf16[128,2304]{1,0:T(8,128)(2,1)S(1)} %collective-permute-done.9.refs_1_, bf16[128,2304]{1,0:T(8,128)(2,1)S(1)} %collective-permute-done.10.refs_2_, ...), custom_call_target="tpu_custom_call" | custom-call | bytes 6291456 | tf_op jit(solution)/shard_map/pallas_call | solution.py:114
  70.2 1.7 %shard_map.111 = (bf16[512,2304]{1,0:T(8,128)(2,1)S(1)}, f32[512,1]{1,0:T(8,128)S(1)}, f32[1,512]{1,0:T(1,128)S(1)}) custom-call(s32[1]{0:T(128)} %bitcast.half_ref.core, bf16[128,2304]{1,0:T(8,128)(2,1)S(1)} %fusion.refs_6_._, bf16[512,4608]{1,0:T(8,128)(2,1)S(1)} %bitcast.75, bf16[512,2304]{1,0:T(8,128)(2,1)S(1)} %shard_map.107.b.own.refs_4_, ...), custom_call_target="tpu_custom_call" | custom-call | bytes 6291456 | tf_op jit(solution)/shard_map/pallas_call | solution.py:114
  72.8 1.6 %collective-permute-start.18 = (bf16[32,2304]{1,0:T(8,128)(2,1)S(1)}, bf16[32,2304]{1,0:T(8,128)(2,1)S(1)}, u32[]{:S(2)}, u32[]{:S(2)}) collective-permute-start(bf16[32,2304]{1,0:T(8,128)(2,1)S(1)} %get-tuple-element.66), channel_id=1, source_target_pairs={{0,1},{32,33},{2,3},{34,35},{4,5},{36,37},{6,7},{38,39},{64,65},{9... | collective-permute-start | bytes 442376 | tf_op jit(solution)/shard_map/ppermute | solution.py:38
  74.4 2.3 %collective-permute-start.17 = (bf16[32,2304]{1,0:T(8,128)(2,1)S(1)}, bf16[32,2304]{1,0:T(8,128)(2,1)S(1)}, u32[]{:S(2)}, u32[]{:S(2)}) collective-permute-start(bf16[32,2304]{1,0:T(8,128)(2,1)S(1)} %get-tuple-element.67), channel_id=1, source_target_pairs={{0,65},{32,97},{2,67},{34,99},{4,69},{36,101},{6,71},{38,103},{64,... | collective-permute-start | bytes 442376 | tf_op jit(solution)/shard_map/ppermute | solution.py:38
  76.6 3.5 %collective-permute-start.28 = (bf16[2304,512]{1,0:T(8,128)(2,1)S(1)}, bf16[2304,512]{1,0:T(8,128)(2,1)S(1)}, u32[]{:S(2)}, u32[]{:S(2)}) collective-permute-start(bf16[2304,512]{1,0:T(8,128)(2,1)S(1)} %get-tuple-element.51.refs_9_), channel_id=1, source_target_pairs={{0,32},{32,0},{2,34},{34,2},{4,36},{36,4},{6,38},{38,6},{64,96},{9... | collective-permute-start | bytes 7077896 | tf_op jit(solution)/shard_map/ppermute | solution.py:38
  81.2 1.7 %collective-permute-start.22 = (bf16[32,2304]{1,0:T(8,128)(2,1)S(1)}, bf16[32,2304]{1,0:T(8,128)(2,1)S(1)}, u32[]{:S(2)}, u32[]{:S(2)}) collective-permute-start(bf16[32,2304]{1,0:T(8,128)(2,1)S(1)} %fusion.12), channel_id=1, source_target_pairs={{0,6},{32,56},{2,0},{34,58},{4,2},{36,60},{6,4},{38,62},{64,70},{9... | collective-permute-start | bytes 442376 | tf_op jit(solution)/shard_map/ppermute | solution.py:38
  83.0 2.7 %collective-permute-start.23 = (bf16[32,2304]{1,0:T(8,128)(2,1)S(1)}, bf16[32,2304]{1,0:T(8,128)(2,1)S(1)}, u32[]{:S(2)}, u32[]{:S(2)}) collective-permute-start(bf16[32,2304]{1,0:T(8,128)(2,1)S(1)} %fusion.12), channel_id=1, source_target_pairs={{0,4},{32,48},{2,6},{34,50},{4,0},{36,52},{6,2},{38,54},{64,68},{9... | collective-permute-start | bytes 442376 | tf_op jit(solution)/shard_map/ppermute | solution.py:38
  86.4 2.1 %collective-permute-done.23 = bf16[32,2304]{1,0:T(8,128)(2,1)S(1)} collective-permute-done((bf16[32,2304]{1,0:T(8,128)(2,1)S(1)}, bf16[32,2304]{1,0:T(8,128)(2,1)S(1)}, u32[]{:S(2)}, u32[]{:S(2)}) %collective-permute-start.23) | collective-permute-done | bytes 147488 | tf_op jit(solution)/shard_map/ppermute | solution.py:38
  88.6 2.7 %collective-permute-start.27 = (bf16[32,2304]{1,0:T(8,128)(2,1)S(1)}, bf16[32,2304]{1,0:T(8,128)(2,1)S(1)}, u32[]{:S(2)}, u32[]{:S(2)}) collective-permute-start(bf16[32,2304]{1,0:T(8,128)(2,1)S(1)} %fusion.7), channel_id=1, source_target_pairs={{0,1},{32,33},{2,3},{34,35},{4,5},{36,37},{6,7},{38,39},{64,65},{9... | collective-permute-start | bytes 442376 | tf_op jit(solution)/shard_map/ppermute | solution.py:38
  92.6 5.4 %collective-permute-start.30 = (bf16[32,2304]{1,0:T(8,128)(2,1)S(1)}, bf16[32,2304]{1,0:T(8,128)(2,1)S(1)}, u32[]{:S(2)}, u32[]{:S(2)}) collective-permute-start(bf16[32,2304]{1,0:T(8,128)(2,1)S(1)} %fusion.7), channel_id=1, source_target_pairs={{0,16},{32,36},{2,18},{34,38},{4,20},{36,32},{6,22},{38,34},{64,80... | collective-permute-start | bytes 442376 | tf_op jit(solution)/shard_map/ppermute | solution.py:38
  98.2 6.1 %collective-permute-start.34 = (bf16[128,2304]{1,0:T(8,128)(2,1)S(1)}, bf16[128,2304]{1,0:T(8,128)(2,1)S(1)}, u32[]{:S(2)}, u32[]{:S(2)}) collective-permute-start(bf16[128,2304]{1,0:T(8,128)(2,1)S(1)} %bitcast.79), channel_id=1, source_target_pairs={{0,8},{32,34},{2,10},{34,36},{4,12},{36,38},{6,14},{38,32},{64,72}... | collective-permute-start | bytes 1769480 | tf_op jit(solution)/shard_map/ppermute | solution.py:38
  105.2 2.3 %collective-permute-start.32 = (bf16[32,2304]{1,0:T(8,128)(2,1)S(1)}, bf16[32,2304]{1,0:T(8,128)(2,1)S(1)}, u32[]{:S(2)}, u32[]{:S(2)}) collective-permute-start(bf16[32,2304]{1,0:T(8,128)(2,1)S(1)} %collective-permute-done.30), channel_id=1, source_target_pairs={{0,65},{32,97},{2,67},{34,99},{4,69},{36,101},{6,71},{38,103},{64,... | collective-permute-start | bytes 442376 | tf_op jit(solution)/shard_map/ppermute | solution.py:38
  108.1 1.8 %collective-permute-done.33 = bf16[32,2304]{1,0:T(8,128)(2,1)S(1)} collective-permute-done((bf16[32,2304]{1,0:T(8,128)(2,1)S(1)}, bf16[32,2304]{1,0:T(8,128)(2,1)S(1)}, u32[]{:S(2)}, u32[]{:S(2)}) %collective-permute-start.33) | collective-permute-done | bytes 147488 | tf_op jit(solution)/shard_map/ppermute | solution.py:38
  109.9 1.8 %collective-permute-done.32 = bf16[32,2304]{1,0:T(8,128)(2,1)S(1)} collective-permute-done((bf16[32,2304]{1,0:T(8,128)(2,1)S(1)}, bf16[32,2304]{1,0:T(8,128)(2,1)S(1)}, u32[]{:S(2)}, u32[]{:S(2)}) %collective-permute-start.32) | collective-permute-done | bytes 147488 | tf_op jit(solution)/shard_map/ppermute | solution.py:38
  113.1 4.0 %collective-permute-start.37 = (bf16[128,2304]{1,0:T(8,128)(2,1)S(1)}, bf16[128,2304]{1,0:T(8,128)(2,1)S(1)}, u32[]{:S(2)}, u32[]{:S(2)}) collective-permute-start(bf16[128,2304]{1,0:T(8,128)(2,1)S(1)} %bitcast.83), channel_id=1, source_target_pairs={{0,32},{32,0},{2,34},{34,2},{4,36},{36,4},{6,38},{38,6},{64,96},{9... | collective-permute-start | bytes 1769480 | tf_op jit(solution)/shard_map/ppermute | solution.py:38
  117.9 3.2 %shard_map.112 = (f32[512,512]{1,0:T(8,128)S(1)}, bf16[512,4608]{1,0:T(8,128)(2,1)}) custom-call(s32[1]{0:T(128)} %bitcast.half_ref.core, bf16[128,2304]{1,0:T(8,128)(2,1)S(1)} %bitcast.82, bf16[128,2304]{1,0:T(8,128)(2,1)S(1)} %collective-permute-done.29.refs_1_, bf16[128,2304]{1,0:T(8,128)(2,1)S(1)} %bitcast.84, ...), custom_call_target="tpu_custom_call" | custom-call | flops 2415919104 | bytes 8388608 | tf_op jit(solution)/shard_map/pallas_call | solution.py:114
  121.3 7.0 %shard_map.113 = (bf16[512,4608]{1,0:T(8,128)(2,1)}, bf16[4608,512]{1,0:T(8,128)(2,1)}, f32[1,512]{1,0:T(1,128)}) custom-call(s32[1]{0:T(128)} %bitcast.half_ref.core, bf16[512,4608]{1,0:T(8,128)(2,1)} %get-tuple-element.54._, f32[512,512]{1,0:T(8,128)S(1)} %get-tuple-element.55.own_acts, ...), custom_call_target="tpu_custom_call", output_to_operand_aliasing={{0}: (1, {})} | custom-call | flops 4831838208 | bytes 16777216 | tf_op jit(solution)/shard_map/pallas_call | solution.py:114
  (131 shorter events, 31.6 us)
Async XLA Ops:
  7.1 5.7 %collective-permute-start.1 = (f32[16,2304]{1,0:T(8,128)S(1)}, f32[16,2304]{1,0:T(8,128)S(1)}, u32[]{:S(2)}, u32[]{:S(2)}) collective-permute-start(f32[16,2304]{1,0:T(8,128)S(1)} %select_add_fusion.after_ref), channel_id=1, source_target_pairs={{0,64},{64,0},{32,96},{96,32},{1,65},{65,1},{33,97},{97,33},{2,66}... | collective-permute-start | bytes 442376 | tf_op jit(solution)/shard_map/ppermute | solution.py:313
  14.8 5.0 %collective-permute-start.3 = (bf16[16,2304]{1,0:T(8,128)(2,1)S(1)}, bf16[16,2304]{1,0:T(8,128)(2,1)S(1)}, u32[]{:S(2)}, u32[]{:S(2)}) collective-permute-start(bf16[16,2304]{1,0:T(8,128)(2,1)S(1)} %maximum_select_fusion), channel_id=1, source_target_pairs={{0,65},{32,97},{2,67},{34,99},{4,69},{36,101},{6,71},{38,103},{64,... | collective-permute-start | bytes 221192 | tf_op jit(solution)/shard_map/ppermute | solution.py:38
  17.7 12.0 %collective-permute-start.7 = (bf16[2304,512]{1,0:T(8,128)(2,1)}, bf16[2304,512]{1,0:T(8,128)(2,1)S(1)}, u32[]{:S(2)}, u32[]{:S(2)}) collective-permute-start(bf16[2304,512]{1,0:T(8,128)(2,1)} %copy-done.5), channel_id=1, source_target_pairs={{0,32},{32,0},{2,34},{34,2},{4,36},{36,4},{6,38},{38,6},{64,96},{9... | collective-permute-start | bytes 7077896 | tf_op jit(solution)/shard_map/ppermute | solution.py:38
  18.3 11.4 %collective-permute-start.8 = (bf16[512,2304]{1,0:T(8,128)(2,1)S(1)}, bf16[512,2304]{1,0:T(8,128)(2,1)S(1)}, u32[]{:S(2)}, u32[]{:S(2)}) collective-permute-start(bf16[512,2304]{1,0:T(8,128)(2,1)S(1)} %shard_map.104), channel_id=1, source_target_pairs={{0,32},{32,0},{2,34},{34,2},{4,36},{36,4},{6,38},{38,6},{64,96},{9... | collective-permute-start | bytes 7077896 | tf_op jit(solution)/shard_map/ppermute | solution.py:38
  22.4 7.1 %collective-permute-start.6 = (bf16[32,2304]{1,0:T(8,128)(2,1)S(1)}, bf16[32,2304]{1,0:T(8,128)(2,1)S(1)}, u32[]{:S(2)}, u32[]{:S(2)}) collective-permute-start(bf16[32,2304]{1,0:T(8,128)(2,1)S(1)} %get-tuple-element.70), channel_id=1, source_target_pairs={{0,2},{32,40},{2,4},{34,42},{4,6},{36,44},{6,0},{38,46},{64,66},{9... | collective-permute-start | bytes 442376 | tf_op jit(solution)/shard_map/ppermute | solution.py:38
  22.4 5.9 %collective-permute-start.5 = (bf16[32,2304]{1,0:T(8,128)(2,1)S(1)}, bf16[32,2304]{1,0:T(8,128)(2,1)S(1)}, u32[]{:S(2)}, u32[]{:S(2)}) collective-permute-start(bf16[32,2304]{1,0:T(8,128)(2,1)S(1)} %get-tuple-element.70), channel_id=1, source_target_pairs={{0,4},{32,48},{2,6},{34,50},{4,0},{36,52},{6,2},{38,54},{64,68},{9... | collective-permute-start | bytes 442376 | tf_op jit(solution)/shard_map/ppermute | solution.py:38
  29.7 11.4 %collective-permute-start.11 = (bf16[128,2304]{1,0:T(8,128)(2,1)S(1)}, bf16[128,2304]{1,0:T(8,128)(2,1)S(1)}, u32[]{:S(2)}, u32[]{:S(2)}) collective-permute-start(bf16[128,2304]{1,0:T(8,128)(2,1)S(1)} %subtract_convert_fusion.after_ref.refs_0_), channel_id=1, source_target_pairs={{0,8},{32,34},{2,10},{34,36},{4,12},{36,38},{6,14},{38,32},{64,72}... | collective-permute-start | bytes 1769480 | tf_op jit(solution)/shard_map/ppermute | solution.py:38
  31.2 17.3 %collective-permute-start.10 = (bf16[128,2304]{1,0:T(8,128)(2,1)S(1)}, bf16[128,2304]{1,0:T(8,128)(2,1)S(1)}, u32[]{:S(2)}, u32[]{:S(2)}) collective-permute-start(bf16[128,2304]{1,0:T(8,128)(2,1)S(1)} %subtract_convert_fusion.after_ref.refs_0_), channel_id=1, source_target_pairs={{0,16},{32,36},{2,18},{34,38},{4,20},{36,32},{6,22},{38,34},{64,80... | collective-permute-start | bytes 1769480 | tf_op jit(solution)/shard_map/ppermute | solution.py:38
  34.7 14.4 %collective-permute-start.9 = (bf16[128,2304]{1,0:T(8,128)(2,1)S(1)}, bf16[128,2304]{1,0:T(8,128)(2,1)S(1)}, u32[]{:S(2)}, u32[]{:S(2)}) collective-permute-start(bf16[128,2304]{1,0:T(8,128)(2,1)S(1)} %subtract_convert_fusion.after_ref.refs_0_), channel_id=1, source_target_pairs={{0,24},{32,38},{2,26},{34,32},{4,28},{36,34},{6,30},{38,36},{64,88... | collective-permute-start | bytes 1769480 | tf_op jit(solution)/shard_map/ppermute | solution.py:38
  49.7 5.5 %collective-permute-start.12 = (f32[512,512]{1,0:T(8,128)S(1)}, f32[512,512]{1,0:T(8,128)S(1)}, u32[]{:S(2)}, u32[]{:S(2)}) collective-permute-start(f32[512,512]{1,0:T(8,128)S(1)} %bitcast.91), channel_id=1, source_target_pairs={{0,32},{32,0},{2,34},{34,2},{4,36},{36,4},{6,38},{38,6},{64,96},{9... | collective-permute-start | bytes 3145736 | tf_op jit(solution)/shard_map/ppermute | solution.py:38
  58.0 5.9 %collective-permute-start.19 = (bf16[4,2,8,2304]{3,2,1,0:T(8,128)(2,1)S(1)}, bf16[4,2,8,2304]{3,2,1,0:T(8,128)(2,1)S(1)}, u32[]{:S(2)}, u32[]{:S(2)}) collective-permute-start(bf16[4,2,8,2304]{3,2,1,0:T(8,128)(2,1)S(1)} %slice_select_fusion), channel_id=1, source_target_pairs={{0,65},{32,96},{2,67},{34,98},{4,69},{36,100},{6,71},{38,102},{64,... | collective-permute-start | bytes 884744 | tf_op jit(solution)/shard_map/ppermute | solution.py:38
  58.7 13.7 %collective-permute-start.14 = (bf16[128,2304]{1,0:T(8,128)(2,1)S(1)}, bf16[128,2304]{1,0:T(8,128)(2,1)S(1)}, u32[]{:S(2)}, u32[]{:S(2)}) collective-permute-start(bf16[128,2304]{1,0:T(8,128)(2,1)S(1)} %fusion.1), channel_id=1, source_target_pairs={{0,8},{32,34},{2,10},{34,36},{4,12},{36,38},{6,14},{38,32},{64,72}... | collective-permute-start | bytes 1769480 | tf_op jit(solution)/shard_map/ppermute | solution.py:38
  59.3 13.1 %collective-permute-start.15 = (bf16[128,2304]{1,0:T(8,128)(2,1)S(1)}, bf16[128,2304]{1,0:T(8,128)(2,1)S(1)}, u32[]{:S(2)}, u32[]{:S(2)}) collective-permute-start(bf16[128,2304]{1,0:T(8,128)(2,1)S(1)} %fusion.2), channel_id=1, source_target_pairs={{0,24},{32,38},{2,26},{34,32},{4,28},{36,34},{6,30},{38,36},{64,88... | collective-permute-start | bytes 1769480 | tf_op jit(solution)/shard_map/ppermute | solution.py:38
  64.1 7.9 %collective-permute-start.20 = (bf16[4,8,2304]{2,1,0:T(8,128)(2,1)S(1)}, bf16[4,8,2304]{2,1,0:T(8,128)(2,1)S(1)}, u32[]{:S(2)}, u32[]{:S(2)}) collective-permute-start(bf16[4,8,2304]{2,1,0:T(8,128)(2,1)S(1)} %slice_bitcast_fusion.1), channel_id=1, source_target_pairs={{0,64},{32,97},{2,66},{34,99},{4,68},{36,101},{6,70},{38,103},{64,... | collective-permute-start | bytes 442376 | tf_op jit(solution)/shard_map/ppermute | solution.py:38
  72.0 8.1 %collective-permute-start.21 = (bf16[32,2304]{1,0:T(8,128)(2,1)S(1)}, bf16[32,2304]{1,0:T(8,128)(2,1)S(1)}, u32[]{:S(2)}, u32[]{:S(2)}) collective-permute-start(bf16[32,2304]{1,0:T(8,128)(2,1)S(1)} %fusion.13), channel_id=1, source_target_pairs={{0,16},{32,36},{2,18},{34,38},{4,20},{36,32},{6,22},{38,34},{64,80... | collective-permute-start | bytes 442376 | tf_op jit(solution)/shard_map/ppermute | solution.py:38
  72.7 7.4 %collective-permute-start.16 = (bf16[32,2304]{1,0:T(8,128)(2,1)S(1)}, bf16[32,2304]{1,0:T(8,128)(2,1)S(1)}, u32[]{:S(2)}, u32[]{:S(2)}) collective-permute-start(bf16[32,2304]{1,0:T(8,128)(2,1)S(1)} %get-tuple-element.65), channel_id=1, source_target_pairs={{0,64},{32,96},{2,66},{34,98},{4,68},{36,100},{6,70},{38,102},{64,... | collective-permute-start | bytes 442376 | tf_op jit(solution)/shard_map/ppermute | solution.py:38
  72.8 7.3 %collective-permute-start.18 = (bf16[32,2304]{1,0:T(8,128)(2,1)S(1)}, bf16[32,2304]{1,0:T(8,128)(2,1)S(1)}, u32[]{:S(2)}, u32[]{:S(2)}) collective-permute-start(bf16[32,2304]{1,0:T(8,128)(2,1)S(1)} %get-tuple-element.66), channel_id=1, source_target_pairs={{0,1},{32,33},{2,3},{34,35},{4,5},{36,37},{6,7},{38,39},{64,65},{9... | collective-permute-start | bytes 442376 | tf_op jit(solution)/shard_map/ppermute | solution.py:38
  74.4 5.8 %collective-permute-start.17 = (bf16[32,2304]{1,0:T(8,128)(2,1)S(1)}, bf16[32,2304]{1,0:T(8,128)(2,1)S(1)}, u32[]{:S(2)}, u32[]{:S(2)}) collective-permute-start(bf16[32,2304]{1,0:T(8,128)(2,1)S(1)} %get-tuple-element.67), channel_id=1, source_target_pairs={{0,65},{32,97},{2,67},{34,99},{4,69},{36,101},{6,71},{38,103},{64,... | collective-permute-start | bytes 442376 | tf_op jit(solution)/shard_map/ppermute | solution.py:38
  76.6 21.5 %collective-permute-start.28 = (bf16[2304,512]{1,0:T(8,128)(2,1)S(1)}, bf16[2304,512]{1,0:T(8,128)(2,1)S(1)}, u32[]{:S(2)}, u32[]{:S(2)}) collective-permute-start(bf16[2304,512]{1,0:T(8,128)(2,1)S(1)} %get-tuple-element.51.refs_9_), channel_id=1, source_target_pairs={{0,32},{32,0},{2,34},{34,2},{4,36},{36,4},{6,38},{38,6},{64,96},{9... | collective-permute-start | bytes 7077896 | tf_op jit(solution)/shard_map/ppermute | solution.py:38
  80.2 5.4 %collective-permute-start.24 = (bf16[32,2304]{1,0:T(8,128)(2,1)S(1)}, bf16[32,2304]{1,0:T(8,128)(2,1)S(1)}, u32[]{:S(2)}, u32[]{:S(2)}) collective-permute-start(bf16[32,2304]{1,0:T(8,128)(2,1)S(1)} %fusion.12), channel_id=1, source_target_pairs={{0,2},{32,40},{2,4},{34,42},{4,6},{36,44},{6,0},{38,46},{64,66},{9... | collective-permute-start | bytes 442376 | tf_op jit(solution)/shard_map/ppermute | solution.py:38
  81.2 5.1 %collective-permute-start.22 = (bf16[32,2304]{1,0:T(8,128)(2,1)S(1)}, bf16[32,2304]{1,0:T(8,128)(2,1)S(1)}, u32[]{:S(2)}, u32[]{:S(2)}) collective-permute-start(bf16[32,2304]{1,0:T(8,128)(2,1)S(1)} %fusion.12), channel_id=1, source_target_pairs={{0,6},{32,56},{2,0},{34,58},{4,2},{36,60},{6,4},{38,62},{64,70},{9... | collective-permute-start | bytes 442376 | tf_op jit(solution)/shard_map/ppermute | solution.py:38
  83.0 5.5 %collective-permute-start.23 = (bf16[32,2304]{1,0:T(8,128)(2,1)S(1)}, bf16[32,2304]{1,0:T(8,128)(2,1)S(1)}, u32[]{:S(2)}, u32[]{:S(2)}) collective-permute-start(bf16[32,2304]{1,0:T(8,128)(2,1)S(1)} %fusion.12), channel_id=1, source_target_pairs={{0,4},{32,48},{2,6},{34,50},{4,0},{36,52},{6,2},{38,54},{64,68},{9... | collective-permute-start | bytes 442376 | tf_op jit(solution)/shard_map/ppermute | solution.py:38
  88.6 9.4 %collective-permute-start.27 = (bf16[32,2304]{1,0:T(8,128)(2,1)S(1)}, bf16[32,2304]{1,0:T(8,128)(2,1)S(1)}, u32[]{:S(2)}, u32[]{:S(2)}) collective-permute-start(bf16[32,2304]{1,0:T(8,128)(2,1)S(1)} %fusion.7), channel_id=1, source_target_pairs={{0,1},{32,33},{2,3},{34,35},{4,5},{36,37},{6,7},{38,39},{64,65},{9... | collective-permute-start | bytes 442376 | tf_op jit(solution)/shard_map/ppermute | solution.py:38
  91.3 6.7 %collective-permute-start.26 = (bf16[32,2304]{1,0:T(8,128)(2,1)S(1)}, bf16[32,2304]{1,0:T(8,128)(2,1)S(1)}, u32[]{:S(2)}, u32[]{:S(2)}) collective-permute-start(bf16[32,2304]{1,0:T(8,128)(2,1)S(1)} %fusion.7), channel_id=1, source_target_pairs={{0,65},{32,97},{2,67},{34,99},{4,69},{36,101},{6,71},{38,103},{64,... | collective-permute-start | bytes 442376 | tf_op jit(solution)/shard_map/ppermute | solution.py:38
  92.2 5.9 %collective-permute-start.25 = (bf16[32,2304]{1,0:T(8,128)(2,1)S(1)}, bf16[32,2304]{1,0:T(8,128)(2,1)S(1)}, u32[]{:S(2)}, u32[]{:S(2)}) collective-permute-start(bf16[32,2304]{1,0:T(8,128)(2,1)S(1)} %fusion.7), channel_id=1, source_target_pairs={{0,64},{32,96},{2,66},{34,98},{4,68},{36,100},{6,70},{38,102},{64,... | collective-permute-start | bytes 442376 | tf_op jit(solution)/shard_map/ppermute | solution.py:38
  92.6 11.6 %collective-permute-start.30 = (bf16[32,2304]{1,0:T(8,128)(2,1)S(1)}, bf16[32,2304]{1,0:T(8,128)(2,1)S(1)}, u32[]{:S(2)}, u32[]{:S(2)}) collective-permute-start(bf16[32,2304]{1,0:T(8,128)(2,1)S(1)} %fusion.7), channel_id=1, source_target_pairs={{0,16},{32,36},{2,18},{34,38},{4,20},{36,32},{6,22},{38,34},{64,80... | collective-permute-start | bytes 442376 | tf_op jit(solution)/shard_map/ppermute | solution.py:38
  98.2 19.1 %collective-permute-start.34 = (bf16[128,2304]{1,0:T(8,128)(2,1)S(1)}, bf16[128,2304]{1,0:T(8,128)(2,1)S(1)}, u32[]{:S(2)}, u32[]{:S(2)}) collective-permute-start(bf16[128,2304]{1,0:T(8,128)(2,1)S(1)} %bitcast.79), channel_id=1, source_target_pairs={{0,8},{32,34},{2,10},{34,36},{4,12},{36,38},{6,14},{38,32},{64,72}... | collective-permute-start | bytes 1769480 | tf_op jit(solution)/shard_map/ppermute | solution.py:38
  104.3 13.4 %collective-permute-start.29 = (bf16[128,2304]{1,0:T(8,128)(2,1)S(1)}, bf16[128,2304]{1,0:T(8,128)(2,1)S(1)}, u32[]{:S(2)}, u32[]{:S(2)}) collective-permute-start(bf16[128,2304]{1,0:T(8,128)(2,1)S(1)} %bitcast.80), channel_id=1, source_target_pairs={{0,24},{32,38},{2,26},{34,32},{4,28},{36,34},{6,30},{38,36},{64,88... | collective-permute-start | bytes 1769480 | tf_op jit(solution)/shard_map/ppermute | solution.py:38
  104.3 5.6 %collective-permute-start.33 = (bf16[32,2304]{1,0:T(8,128)(2,1)S(1)}, bf16[32,2304]{1,0:T(8,128)(2,1)S(1)}, u32[]{:S(2)}, u32[]{:S(2)}) collective-permute-start(bf16[32,2304]{1,0:T(8,128)(2,1)S(1)} %collective-permute-done.30), channel_id=1, source_target_pairs={{0,1},{32,33},{2,3},{34,35},{4,5},{36,37},{6,7},{38,39},{64,65},{9... | collective-permute-start | bytes 442376 | tf_op jit(solution)/shard_map/ppermute | solution.py:38
  105.2 6.4 %collective-permute-start.32 = (bf16[32,2304]{1,0:T(8,128)(2,1)S(1)}, bf16[32,2304]{1,0:T(8,128)(2,1)S(1)}, u32[]{:S(2)}, u32[]{:S(2)}) collective-permute-start(bf16[32,2304]{1,0:T(8,128)(2,1)S(1)} %collective-permute-done.30), channel_id=1, source_target_pairs={{0,65},{32,97},{2,67},{34,99},{4,69},{36,101},{6,71},{38,103},{64,... | collective-permute-start | bytes 442376 | tf_op jit(solution)/shard_map/ppermute | solution.py:38
  107.6 5.4 %collective-permute-start.31 = (bf16[32,2304]{1,0:T(8,128)(2,1)S(1)}, bf16[32,2304]{1,0:T(8,128)(2,1)S(1)}, u32[]{:S(2)}, u32[]{:S(2)}) collective-permute-start(bf16[32,2304]{1,0:T(8,128)(2,1)S(1)} %collective-permute-done.30), channel_id=1, source_target_pairs={{0,64},{32,96},{2,66},{34,98},{4,68},{36,100},{6,70},{38,102},{64,... | collective-permute-start | bytes 442376 | tf_op jit(solution)/shard_map/ppermute | solution.py:38
  113.1 8.1 %collective-permute-start.37 = (bf16[128,2304]{1,0:T(8,128)(2,1)S(1)}, bf16[128,2304]{1,0:T(8,128)(2,1)S(1)}, u32[]{:S(2)}, u32[]{:S(2)}) collective-permute-start(bf16[128,2304]{1,0:T(8,128)(2,1)S(1)} %bitcast.83), channel_id=1, source_target_pairs={{0,32},{32,0},{2,34},{34,2},{4,36},{36,4},{6,38},{38,6},{64,96},{9... | collective-permute-start | bytes 1769480 | tf_op jit(solution)/shard_map/ppermute | solution.py:38
  (19 other events, 79.4 us)

commit v7 on v6

--- a/solution.py
+++ b/solution.py
@@ -124,7 +124,7 @@
 
 
 def flip_kernel(*refs):
-    pieces, squares, (_, out, *square_outs) = refs[:4], refs[4:6], refs[6:]
+    pieces, squares, (norms, _, out, *square_outs, factor) = refs[:4], refs[4:6], refs[6:]
     for k, piece in enumerate(pieces):
 
         def tile(j, carry, piece=piece, column=128 * k):
@@ -136,15 +136,18 @@
     for square, square_out in zip(squares, square_outs):
         for i in range(4):
             square_out[:, 128 * i : 128 * i + 128] = square[128 * i : 128 * i + 128, :].T
-
-
-def flip(pieces, squares, after):
-    ins = [(v, VMEM) for v in pieces + squares] + [(after, None)]
+    act_sum = jnp.sum(square_outs[0][...].astype(f32), axis=1, keepdims=True)
+    factor[...] = sparsity_weight / TOKENS * (act_sum / norms[...])
+
+
+def flip(pieces, squares, norms, after):
+    ins = [(v, VMEM) for v in pieces + squares + [norms]] + [(after, None)]
     outs = [((HALF, TOKENS), bf16, VMEM)] + [((TOKENS, TOKENS), bf16, VMEM)] * 2
+    outs += [((TOKENS, 1), f32, VMEM)]
     return call(flip_kernel, outs, ins, [], 8, 0, 6 * 2**20)
 
 
-def rows_kernel(core, _, weight, own, act, other, factor, penalty, sems):
+def rows_kernel(core, _, weight, own, other, norms_out, penalty, sems):
     columns = pl.ds(pl.multiple_of((1 - core[0]) * HALF, HALF), HALF)
     copies = []
     for i in range(4):
@@ -162,14 +165,13 @@
             wide = part[:, 128 * j : 128 * j + 128].astype(f32)
             squares = squares + wide * wide
     norms = jnp.sqrt(jnp.sum(squares, axis=1, keepdims=True) + norm_epsilon)
-    act_sum = jnp.sum(act[...].astype(f32), axis=1, keepdims=True)
-    factor[...] = sparsity_weight / TOKENS * (act_sum / norms)
+    norms_out[...] = norms
     norms = jnp.broadcast_to(sparsity_weight * norms / TOKENS, (TOKENS, 128))
     penalty[...] = norms.T[:1, :]
 
 
-def decoder_rows(core, after, weight, own, act):
-    ins = [(core, pltpu.SMEM), (after, None), (weight, None), (own, VMEM), (act, VMEM)]
+def decoder_rows(core, after, weight, own):
+    ins = [(core, pltpu.SMEM), (after, None), (weight, None), (own, VMEM)]
     outs = [((TOKENS, HALF), bf16, VMEM)]
     outs += [((TOKENS, 1), f32, VMEM), ((1, TOKENS), f32, VMEM)]
     scratch = [pltpu.SemaphoreType.DMA((4,))]
@@ -186,13 +188,14 @@
 
 
 def decoder_part(half, out, errors, weight, act, factor, stage, sems):
+    step = stage.shape[-1]
     copies = []
-    for j in range(HALF // STEP):
-        span = slice(j * STEP, j * STEP + STEP)
+    for j in range(HALF // step):
+        span = slice(j * step, j * step + step)
         part = jnp.dot(act[...], errors[:, span], preferred_element_type=f32)
         part = part + factor[...] * weight[:, span].astype(f32)
         stage[j] = part.astype(bf16)
-        columns = pl.ds(pl.multiple_of(half * HALF + j * STEP, STEP), STEP)
+        columns = pl.ds(pl.multiple_of(half * HALF + j * step, step), step)
         copies.append(pltpu.make_async_copy(stage.at[j], out.at[:, columns], sems.at[j]))
         copies[-1].start()
     return copies
@@ -202,11 +205,7 @@
     pieces, (weight, act, factor, grad_acts, out, errors, stage, sems) = refs[:4], refs[4:]
     join(pieces, errors)
     copies = decoder_part(core[0], out, errors, weight, act, factor, stage, sems)
-    total = jnp.zeros((TOKENS, TOKENS), f32)
-    for j in range(HALF // STEP):
-        span = slice(j * STEP, j * STEP + STEP)
-        total = total + times_rows(errors[:, span], weight[:, span])
-    grad_acts[...] = total
+    grad_acts[...] = times_rows(errors[...], weight[...])
     for copy in copies:
         copy.wait()
 
@@ -216,8 +215,8 @@
     outs = [((TOKENS, TOKENS), f32, VMEM), ((TOKENS, D), bf16, None)]
     scratch = [
         pltpu.VMEM((TOKENS, HALF), bf16),
-        pltpu.VMEM((HALF // STEP, TOKENS, STEP), bf16),
-        pltpu.SemaphoreType.DMA((HALF // STEP,)),
+        pltpu.VMEM((2, TOKENS, HALF // 2), bf16),
+        pltpu.SemaphoreType.DMA((2,)),
     ]
     flops = 4 * TOKENS * TOKENS * HALF
     return call(first_kernel, outs, ins, scratch, 24, flops, 8 * 2**20)
@@ -341,8 +340,9 @@
     centred = [centred] + [to_major(centred, -d) for d in (1, 2, 3)]
 
     for_mate = swap_blocks(jnp.concatenate([dot(piece, encoder_mate) for piece in centred]))
-    for_mate, decoder_own, decoder_mate = lax.optimization_barrier(
-        (for_mate, decoder_own, decoder_mate)
+    decoder_other, norms, penalty = decoder_rows(core, centred[0], decoder_weight, decoder_own)
+    for_mate, decoder_own, decoder_mate, decoder_other, norms, penalty = lax.optimization_barrier(
+        (for_mate, decoder_own, decoder_mate, decoder_other, norms, penalty)
     )
     preact = jnp.concatenate([dot(piece, encoder_own) for piece in centred])
     preact = preact + to_core(for_mate) + encoder_bias
@@ -365,13 +365,10 @@
     far = (far[:, 0].astype(f32) + send.astype(f32)).astype(bf16).reshape(32, HALF)
     recon = [pieces[0], to_major(pieces[1], 1), to_major(pieces[3], 3)]
     recon = sum(piece.astype(f32) for piece in recon).astype(bf16)
-    flipped_own, flipped_act, flipped_swapped = flip(centred, [activations, swapped], pieces[0])
-    decoder_other, factor, penalty = decoder_rows(
-        core, pieces[0], decoder_weight, decoder_own, flipped_act
-    )
-    recon, flipped_own, decoder_other, factor, penalty = lax.optimization_barrier(
-        (recon, flipped_own, decoder_other, factor, penalty)
-    )
+    flipped_own, flipped_act, flipped_swapped, factor = flip(
+        centred, [activations, swapped], norms, pieces[0]
+    )
+    recon, flipped_own = lax.optimization_barrier((recon, flipped_own))
     flipped_mate = to_core(flipped_own)
     recon = (scatter_y(recon) + to_major(far, 2).astype(f32)).astype(bf16)
     summed = recon.astype(f32)

time: 129 us -> 128 us (level)
  transfers between devices with their start and end apart: 39 -> 39, of which waited for: 17 -> 18; matrix products, arithmetic and copies ran while one was open for 5% -> 5% of each run, Pallas kernels for 9% -> 9%
where the time goes in v7:
time: 128 us
  starting transfers between devices  63.2 us (49%)
  waiting for transfers between devices  27.5 us (21%)
  Pallas kernels  18.3 us (14%)
  matrix products  9.05 us (7%)
  local copies, waits for them, and re-layouts  6.88 us (5%)
  other arithmetic  1.54 us (1%)
  between operations  1.35 us (1%)
    ppermute x38, starting transfers between devices, move(): return lax.ppermute(value, AXES, route(step))  61.7 us
    ppermute x38, waiting for transfers between devices, move(): return lax.ppermute(value, AXES, route(step))  27.5 us
    pallas_call x11, Pallas kernels, call(): pl.pallas_call(kernel, out_shape=tuple((jax.ShapeDtypeStruct(shape, dtype...  18.3 us
    dot_general x13, matrix products, dot(): return jnp.dot(a, b, preferred_element_type=f32)  9.05 us
    unnamed x27, local copies, waits for them, and re-layouts  6.63 us
  transfers between devices with their start and end apart: 39, of which 18 were waited for; matrix products, arithmetic and copies ran while one was open for 5% of the time, Pallas kernels for 9%

profile of v7, /device:TPU:1, one launch (start us, length us, event | category | flops | bytes accessed | tf_op | source)
XLA Modules:
  0.0 127.8 jit_solution(6198124940051798161)
XLA Ops:
  1.4 3.2 %fusion.25 = f32[16,4608]{1,0:T(8,128)S(1)} fusion(bf16[16,512]{1,0:T(8,128)(2,1)S(1)} %copy-done, bf16[512,4608]{1,0:T(8,128)(2,1)} %param.9), kind=kOutput, calls=%fused_computation.63 | convolution fusion | flops 75497472 | bytes 5029888 | tf_op jit(solution)/shard_map/dot_general | solution.py:284
  4.6 1.5 %collective-permute-start = (f32[16,2304]{1,0:T(8,128)S(1)}, f32[16,2304]{1,0:T(8,128)S(1)}, u32[]{:S(2)}, u32[]{:S(2)}) collective-permute-start(f32[16,2304]{1,0:T(8,128)S(1)} %slice_select_fusion.2), channel_id=1, source_target_pairs={{0,32},{32,0},{2,34},{34,2},{4,36},{36,4},{6,38},{38,6},{64,96},{9... | collective-permute-start | bytes 442376 | tf_op jit(solution)/shard_map/ppermute | solution.py:38
  8.8 2.1 %copy-done.3 = bf16[4608,512]{1,0:T(8,128)(2,1)S(1)} copy-done((bf16[4608,512]{1,0:T(8,128)(2,1)S(1)}, bf16[4608,512]{1,0:T(8,128)(2,1)}, u32[]{:S(2)}) %copy-start.3) | copy-done | bytes 4718616
  14.8 2.8 %collective-permute-start.3 = (bf16[16,2304]{1,0:T(8,128)(2,1)S(1)}, bf16[16,2304]{1,0:T(8,128)(2,1)S(1)}, u32[]{:S(2)}, u32[]{:S(2)}) collective-permute-start(bf16[16,2304]{1,0:T(8,128)(2,1)S(1)} %maximum_select_fusion), channel_id=1, source_target_pairs={{0,65},{32,97},{2,67},{34,99},{4,69},{36,101},{6,71},{38,103},{64,... | collective-permute-start | bytes 221192 | tf_op jit(solution)/shard_map/ppermute | solution.py:38
  18.3 1.5 %collective-permute-done.3 = bf16[16,2304]{1,0:T(8,128)(2,1)S(1)} collective-permute-done((bf16[16,2304]{1,0:T(8,128)(2,1)S(1)}, bf16[16,2304]{1,0:T(8,128)(2,1)S(1)}, u32[]{:S(2)}, u32[]{:S(2)}) %collective-permute-start.3) | collective-permute-done | bytes 73760 | tf_op jit(solution)/shard_map/ppermute | solution.py:38
  19.8 2.5 %collective-permute-start.4 = (bf16[32,2304]{1,0:T(8,128)(2,1)S(1)}, bf16[32,2304]{1,0:T(8,128)(2,1)S(1)}, u32[]{:S(2)}, u32[]{:S(2)}) collective-permute-start(bf16[32,2304]{1,0:T(8,128)(2,1)S(1)} %get-tuple-element.72), channel_id=1, source_target_pairs={{0,6},{32,56},{2,0},{34,58},{4,2},{36,60},{6,4},{38,62},{64,70},{9... | collective-permute-start | bytes 442376 | tf_op jit(solution)/shard_map/ppermute | solution.py:38
  22.4 1.7 %collective-permute-start.5 = (bf16[32,2304]{1,0:T(8,128)(2,1)S(1)}, bf16[32,2304]{1,0:T(8,128)(2,1)S(1)}, u32[]{:S(2)}, u32[]{:S(2)}) collective-permute-start(bf16[32,2304]{1,0:T(8,128)(2,1)S(1)} %get-tuple-element.72), channel_id=1, source_target_pairs={{0,4},{32,48},{2,6},{34,50},{4,0},{36,52},{6,2},{38,54},{64,68},{9... | collective-permute-start | bytes 442376 | tf_op jit(solution)/shard_map/ppermute | solution.py:38
  24.5 3.9 %collective-permute-done.5 = bf16[32,2304]{1,0:T(8,128)(2,1)S(1)} collective-permute-done((bf16[32,2304]{1,0:T(8,128)(2,1)S(1)}, bf16[32,2304]{1,0:T(8,128)(2,1)S(1)}, u32[]{:S(2)}, u32[]{:S(2)}) %collective-permute-start.5) | collective-permute-done | bytes 147488 | tf_op jit(solution)/shard_map/ppermute | solution.py:38
  29.7 1.5 %collective-permute-start.11 = (bf16[128,2304]{1,0:T(8,128)(2,1)S(1)}, bf16[128,2304]{1,0:T(8,128)(2,1)S(1)}, u32[]{:S(2)}, u32[]{:S(2)}) collective-permute-start(bf16[128,2304]{1,0:T(8,128)(2,1)S(1)} %subtract_convert_fusion.after_ref._.refs_0_), channel_id=1, source_target_pairs={{0,8},{32,34},{2,10},{34,36},{4,12},{36,38},{6,14},{38,32},{64,72}... | collective-permute-start | bytes 1769480 | tf_op jit(solution)/shard_map/ppermute | solution.py:38
  31.2 3.5 %collective-permute-start.10 = (bf16[128,2304]{1,0:T(8,128)(2,1)S(1)}, bf16[128,2304]{1,0:T(8,128)(2,1)S(1)}, u32[]{:S(2)}, u32[]{:S(2)}) collective-permute-start(bf16[128,2304]{1,0:T(8,128)(2,1)S(1)} %subtract_convert_fusion.after_ref._.refs_0_), channel_id=1, source_target_pairs={{0,16},{32,36},{2,18},{34,38},{4,20},{36,32},{6,22},{38,34},{64,80... | collective-permute-start | bytes 1769480 | tf_op jit(solution)/shard_map/ppermute | solution.py:38
  35.2 2.3 %copy-done.4 = bf16[4608,512]{1,0:T(8,128)(2,1)S(1)} copy-done((bf16[4608,512]{1,0:T(8,128)(2,1)S(1)}, bf16[4608,512]{1,0:T(8,128)(2,1)}, u32[]{:S(2)}) %copy-start.4) | copy-done | bytes 4718616
  39.4 1.6 %shard_map.109 = (bf16[512,2304]{1,0:T(8,128)(2,1)S(1)}, f32[512,1]{1,0:T(8,128)S(1)}, f32[1,512]{1,0:T(1,128)S(1)}) custom-call(s32[1]{0:T(128)} %bitcast.half_ref.core, bf16[128,2304]{1,0:T(8,128)(2,1)S(1)} %subtract_convert_fusion.after_ref._.refs_0_, bf16[512,4608]{1,0:T(8,128)(2,1)S(1)} %bitcast.75, bf16[512,2304]{1,0:T(8,128)(2,1)S(1)} %shard_map.107.own.b.refs_4_), custom_call_target="tpu_custom_call" | custom-call | bytes 6291456 | tf_op jit(solution)/shard_map/pallas_call | solution.py:114
  42.0 6.6 %collective-permute-done.10.refs_2_ = bf16[128,2304]{1,0:T(8,128)(2,1)S(1)} collective-permute-done((bf16[128,2304]{1,0:T(8,128)(2,1)S(1)}, bf16[128,2304]{1,0:T(8,128)(2,1)S(1)}, u32[]{:S(2)}, u32[]{:S(2)}) %collective-permute-start.10) | collective-permute-done | bytes 589856 | tf_op jit(solution)/shard_map/ppermute | solution.py:38
  49.7 3.2 %collective-permute-start.12 = (f32[512,512]{1,0:T(8,128)S(1)}, f32[512,512]{1,0:T(8,128)S(1)}, u32[]{:S(2)}, u32[]{:S(2)}) collective-permute-start(f32[512,512]{1,0:T(8,128)S(1)} %bitcast.91), channel_id=1, source_target_pairs={{0,32},{32,0},{2,34},{34,2},{4,36},{36,4},{6,38},{38,6},{64,96},{9... | collective-permute-start | bytes 3145736 | tf_op jit(solution)/shard_map/ppermute | solution.py:38
  59.5 2.7 %collective-permute-start.15 = (bf16[128,2304]{1,0:T(8,128)(2,1)S(1)}, bf16[128,2304]{1,0:T(8,128)(2,1)S(1)}, u32[]{:S(2)}, u32[]{:S(2)}) collective-permute-start(bf16[128,2304]{1,0:T(8,128)(2,1)S(1)} %fusion.2), channel_id=1, source_target_pairs={{0,24},{32,38},{2,26},{34,32},{4,28},{36,34},{6,30},{38,36},{64,88... | collective-permute-start | bytes 1769480 | tf_op jit(solution)/shard_map/ppermute | solution.py:38
  62.2 2.0 %collective-permute-done.19 = bf16[4,2,8,2304]{3,2,1,0:T(8,128)(2,1)S(1)} collective-permute-done((bf16[4,2,8,2304]{3,2,1,0:T(8,128)(2,1)S(1)}, bf16[4,2,8,2304]{3,2,1,0:T(8,128)(2,1)S(1)}, u32[]{:S(2)}, u32[]{:S(2)}) %collective-permute-start.19) | collective-permute-done | bytes 294944 | tf_op jit(solution)/shard_map/ppermute | solution.py:38
  64.3 2.8 %collective-permute-start.20 = (bf16[4,8,2304]{2,1,0:T(8,128)(2,1)S(1)}, bf16[4,8,2304]{2,1,0:T(8,128)(2,1)S(1)}, u32[]{:S(2)}, u32[]{:S(2)}) collective-permute-start(bf16[4,8,2304]{2,1,0:T(8,128)(2,1)S(1)} %slice_bitcast_fusion.1), channel_id=1, source_target_pairs={{0,64},{32,97},{2,66},{34,99},{4,68},{36,101},{6,70},{38,103},{64,... | collective-permute-start | bytes 442376 | tf_op jit(solution)/shard_map/ppermute | solution.py:38
  67.6 2.9 %shard_map.111 = (bf16[2304,512]{1,0:T(8,128)(2,1)S(1)}, bf16[512,512]{1,0:T(8,128)(2,1)S(1)}, bf16[512,512]{1,0:T(8,128)(2,1)S(1)}, f32[512,1]{1,0:T(8,128)S(1)}) custom-call(bf16[128,2304]{1,0:T(8,128)(2,1)S(1)} %subtract_convert_fusion.after_ref._.refs_0_, bf16[128,2304]{1,0:T(8,128)(2,1)S(1)} %collective-permute-done.9.refs_1_, ...), custom_call_target="tpu_custom_call" | custom-call | bytes 6291456 | tf_op jit(solution)/shard_map/pallas_call | solution.py:114
  71.4 3.2 %collective-permute-start.18 = (bf16[32,2304]{1,0:T(8,128)(2,1)S(1)}, bf16[32,2304]{1,0:T(8,128)(2,1)S(1)}, u32[]{:S(2)}, u32[]{:S(2)}) collective-permute-start(bf16[32,2304]{1,0:T(8,128)(2,1)S(1)} %get-tuple-element.68), channel_id=1, source_target_pairs={{0,1},{32,33},{2,3},{34,35},{4,5},{36,37},{6,7},{38,39},{64,65},{9... | collective-permute-start | bytes 442376 | tf_op jit(solution)/shard_map/ppermute | solution.py:38
  75.2 4.7 %collective-permute-start.28 = (bf16[2304,512]{1,0:T(8,128)(2,1)S(1)}, bf16[2304,512]{1,0:T(8,128)(2,1)S(1)}, u32[]{:S(2)}, u32[]{:S(2)}) collective-permute-start(bf16[2304,512]{1,0:T(8,128)(2,1)S(1)} %get-tuple-element.52.refs_9_), channel_id=1, source_target_pairs={{0,32},{32,0},{2,34},{34,2},{4,36},{36,4},{6,38},{38,6},{64,96},{9... | collective-permute-start | bytes 7077896 | tf_op jit(solution)/shard_map/ppermute | solution.py:38
  81.3 1.8 %collective-permute-start.22 = (bf16[32,2304]{1,0:T(8,128)(2,1)S(1)}, bf16[32,2304]{1,0:T(8,128)(2,1)S(1)}, u32[]{:S(2)}, u32[]{:S(2)}) collective-permute-start(bf16[32,2304]{1,0:T(8,128)(2,1)S(1)} %fusion.12), channel_id=1, source_target_pairs={{0,6},{32,56},{2,0},{34,58},{4,2},{36,60},{6,4},{38,62},{64,70},{9... | collective-permute-start | bytes 442376 | tf_op jit(solution)/shard_map/ppermute | solution.py:38
  84.0 1.7 %collective-permute-done.24 = bf16[32,2304]{1,0:T(8,128)(2,1)S(1)} collective-permute-done((bf16[32,2304]{1,0:T(8,128)(2,1)S(1)}, bf16[32,2304]{1,0:T(8,128)(2,1)S(1)}, u32[]{:S(2)}, u32[]{:S(2)}) %collective-permute-start.24) | collective-permute-done | bytes 147488 | tf_op jit(solution)/shard_map/ppermute | solution.py:38
  86.8 1.8 %collective-permute-done.23 = bf16[32,2304]{1,0:T(8,128)(2,1)S(1)} collective-permute-done((bf16[32,2304]{1,0:T(8,128)(2,1)S(1)}, bf16[32,2304]{1,0:T(8,128)(2,1)S(1)}, u32[]{:S(2)}, u32[]{:S(2)}) %collective-permute-start.23) | collective-permute-done | bytes 147488 | tf_op jit(solution)/shard_map/ppermute | solution.py:38
  90.0 1.5 %collective-permute-start.26 = (bf16[32,2304]{1,0:T(8,128)(2,1)S(1)}, bf16[32,2304]{1,0:T(8,128)(2,1)S(1)}, u32[]{:S(2)}, u32[]{:S(2)}) collective-permute-start(bf16[32,2304]{1,0:T(8,128)(2,1)S(1)} %fusion.7), channel_id=1, source_target_pairs={{0,65},{32,97},{2,67},{34,99},{4,69},{36,101},{6,71},{38,103},{64,... | collective-permute-start | bytes 442376 | tf_op jit(solution)/shard_map/ppermute | solution.py:38
  91.9 4.1 %collective-permute-start.30 = (bf16[32,2304]{1,0:T(8,128)(2,1)S(1)}, bf16[32,2304]{1,0:T(8,128)(2,1)S(1)}, u32[]{:S(2)}, u32[]{:S(2)}) collective-permute-start(bf16[32,2304]{1,0:T(8,128)(2,1)S(1)} %fusion.7), channel_id=1, source_target_pairs={{0,16},{32,36},{2,18},{34,38},{4,20},{36,32},{6,22},{38,34},{64,80... | collective-permute-start | bytes 442376 | tf_op jit(solution)/shard_map/ppermute | solution.py:38
  96.2 5.3 %collective-permute-start.34 = (bf16[128,2304]{1,0:T(8,128)(2,1)S(1)}, bf16[128,2304]{1,0:T(8,128)(2,1)S(1)}, u32[]{:S(2)}, u32[]{:S(2)}) collective-permute-start(bf16[128,2304]{1,0:T(8,128)(2,1)S(1)} %bitcast.79), channel_id=1, source_target_pairs={{0,8},{32,34},{2,10},{34,36},{4,12},{36,38},{6,14},{38,32},{64,72}... | collective-permute-start | bytes 1769480 | tf_op jit(solution)/shard_map/ppermute | solution.py:38
  101.5 1.5 %collective-permute-start.33 = (bf16[32,2304]{1,0:T(8,128)(2,1)S(1)}, bf16[32,2304]{1,0:T(8,128)(2,1)S(1)}, u32[]{:S(2)}, u32[]{:S(2)}) collective-permute-start(bf16[32,2304]{1,0:T(8,128)(2,1)S(1)} %collective-permute-done.30), channel_id=1, source_target_pairs={{0,1},{32,33},{2,3},{34,35},{4,5},{36,37},{6,7},{38,39},{64,65},{9... | collective-permute-start | bytes 442376 | tf_op jit(solution)/shard_map/ppermute | solution.py:38
  104.6 2.4 %collective-permute-done.33 = bf16[32,2304]{1,0:T(8,128)(2,1)S(1)} collective-permute-done((bf16[32,2304]{1,0:T(8,128)(2,1)S(1)}, bf16[32,2304]{1,0:T(8,128)(2,1)S(1)}, u32[]{:S(2)}, u32[]{:S(2)}) %collective-permute-start.33) | collective-permute-done | bytes 147488 | tf_op jit(solution)/shard_map/ppermute | solution.py:38
  107.0 1.5 %collective-permute-done.32 = bf16[32,2304]{1,0:T(8,128)(2,1)S(1)} collective-permute-done((bf16[32,2304]{1,0:T(8,128)(2,1)S(1)}, bf16[32,2304]{1,0:T(8,128)(2,1)S(1)}, u32[]{:S(2)}, u32[]{:S(2)}) %collective-permute-start.32) | collective-permute-done | bytes 147488 | tf_op jit(solution)/shard_map/ppermute | solution.py:38
  109.1 7.4 %collective-permute-start.37 = (bf16[128,2304]{1,0:T(8,128)(2,1)S(1)}, bf16[128,2304]{1,0:T(8,128)(2,1)S(1)}, u32[]{:S(2)}, u32[]{:S(2)}) collective-permute-start(bf16[128,2304]{1,0:T(8,128)(2,1)S(1)} %bitcast.83), channel_id=1, source_target_pairs={{0,32},{32,0},{2,34},{34,2},{4,36},{36,4},{6,38},{38,6},{64,96},{9... | collective-permute-start | bytes 1769480 | tf_op jit(solution)/shard_map/ppermute | solution.py:38
  117.3 2.9 %shard_map.112 = (f32[512,512]{1,0:T(8,128)S(1)}, bf16[512,4608]{1,0:T(8,128)(2,1)}) custom-call(s32[1]{0:T(128)} %bitcast.half_ref.core, bf16[128,2304]{1,0:T(8,128)(2,1)S(1)} %bitcast.82, bf16[128,2304]{1,0:T(8,128)(2,1)S(1)} %collective-permute-done.29.refs_1_, bf16[128,2304]{1,0:T(8,128)(2,1)S(1)} %bitcast.84, ...), custom_call_target="tpu_custom_call" | custom-call | flops 2415919104 | bytes 8388608 | tf_op jit(solution)/shard_map/pallas_call | solution.py:114
  120.6 6.9 %shard_map.113 = (bf16[512,4608]{1,0:T(8,128)(2,1)}, bf16[4608,512]{1,0:T(8,128)(2,1)}, f32[1,512]{1,0:T(1,128)}) custom-call(s32[1]{0:T(128)} %bitcast.half_ref.core, bf16[512,4608]{1,0:T(8,128)(2,1)} %get-tuple-element.56._, f32[512,512]{1,0:T(8,128)S(1)} %get-tuple-element.57.own_acts, ...), custom_call_target="tpu_custom_call", output_to_operand_aliasing={{0}: (1, {})} | custom-call | flops 4831838208 | bytes 16777216 | tf_op jit(solution)/shard_map/pallas_call | solution.py:114
  (131 shorter events, 31.2 us)
Async XLA Ops:
  7.1 5.7 %collective-permute-start.1 = (f32[16,2304]{1,0:T(8,128)S(1)}, f32[16,2304]{1,0:T(8,128)S(1)}, u32[]{:S(2)}, u32[]{:S(2)}) collective-permute-start(f32[16,2304]{1,0:T(8,128)S(1)} %select_add_fusion.after_ref), channel_id=1, source_target_pairs={{0,64},{64,0},{32,96},{96,32},{1,65},{65,1},{33,97},{97,33},{2,66}... | collective-permute-start | bytes 442376 | tf_op jit(solution)/shard_map/ppermute | solution.py:312
  14.8 5.0 %collective-permute-start.3 = (bf16[16,2304]{1,0:T(8,128)(2,1)S(1)}, bf16[16,2304]{1,0:T(8,128)(2,1)S(1)}, u32[]{:S(2)}, u32[]{:S(2)}) collective-permute-start(bf16[16,2304]{1,0:T(8,128)(2,1)S(1)} %maximum_select_fusion), channel_id=1, source_target_pairs={{0,65},{32,97},{2,67},{34,99},{4,69},{36,101},{6,71},{38,103},{64,... | collective-permute-start | bytes 221192 | tf_op jit(solution)/shard_map/ppermute | solution.py:38
  17.7 12.0 %collective-permute-start.7 = (bf16[2304,512]{1,0:T(8,128)(2,1)}, bf16[2304,512]{1,0:T(8,128)(2,1)S(1)}, u32[]{:S(2)}, u32[]{:S(2)}) collective-permute-start(bf16[2304,512]{1,0:T(8,128)(2,1)} %copy-done.5), channel_id=1, source_target_pairs={{0,32},{32,0},{2,34},{34,2},{4,36},{36,4},{6,38},{38,6},{64,96},{9... | collective-permute-start | bytes 7077896 | tf_op jit(solution)/shard_map/ppermute | solution.py:38
  18.3 11.4 %collective-permute-start.8 = (bf16[512,2304]{1,0:T(8,128)(2,1)S(1)}, bf16[512,2304]{1,0:T(8,128)(2,1)S(1)}, u32[]{:S(2)}, u32[]{:S(2)}) collective-permute-start(bf16[512,2304]{1,0:T(8,128)(2,1)S(1)} %shard_map.104), channel_id=1, source_target_pairs={{0,32},{32,0},{2,34},{34,2},{4,36},{36,4},{6,38},{38,6},{64,96},{9... | collective-permute-start | bytes 7077896 | tf_op jit(solution)/shard_map/ppermute | solution.py:38
  22.4 7.1 %collective-permute-start.6 = (bf16[32,2304]{1,0:T(8,128)(2,1)S(1)}, bf16[32,2304]{1,0:T(8,128)(2,1)S(1)}, u32[]{:S(2)}, u32[]{:S(2)}) collective-permute-start(bf16[32,2304]{1,0:T(8,128)(2,1)S(1)} %get-tuple-element.72), channel_id=1, source_target_pairs={{0,2},{32,40},{2,4},{34,42},{4,6},{36,44},{6,0},{38,46},{64,66},{9... | collective-permute-start | bytes 442376 | tf_op jit(solution)/shard_map/ppermute | solution.py:38
  22.4 5.9 %collective-permute-start.5 = (bf16[32,2304]{1,0:T(8,128)(2,1)S(1)}, bf16[32,2304]{1,0:T(8,128)(2,1)S(1)}, u32[]{:S(2)}, u32[]{:S(2)}) collective-permute-start(bf16[32,2304]{1,0:T(8,128)(2,1)S(1)} %get-tuple-element.72), channel_id=1, source_target_pairs={{0,4},{32,48},{2,6},{34,50},{4,0},{36,52},{6,2},{38,54},{64,68},{9... | collective-permute-start | bytes 442376 | tf_op jit(solution)/shard_map/ppermute | solution.py:38
  29.7 11.8 %collective-permute-start.11 = (bf16[128,2304]{1,0:T(8,128)(2,1)S(1)}, bf16[128,2304]{1,0:T(8,128)(2,1)S(1)}, u32[]{:S(2)}, u32[]{:S(2)}) collective-permute-start(bf16[128,2304]{1,0:T(8,128)(2,1)S(1)} %subtract_convert_fusion.after_ref._.refs_0_), channel_id=1, source_target_pairs={{0,8},{32,34},{2,10},{34,36},{4,12},{36,38},{6,14},{38,32},{64,72}... | collective-permute-start | bytes 1769480 | tf_op jit(solution)/shard_map/ppermute | solution.py:38
  31.2 17.3 %collective-permute-start.10 = (bf16[128,2304]{1,0:T(8,128)(2,1)S(1)}, bf16[128,2304]{1,0:T(8,128)(2,1)S(1)}, u32[]{:S(2)}, u32[]{:S(2)}) collective-permute-start(bf16[128,2304]{1,0:T(8,128)(2,1)S(1)} %subtract_convert_fusion.after_ref._.refs_0_), channel_id=1, source_target_pairs={{0,16},{32,36},{2,18},{34,38},{4,20},{36,32},{6,22},{38,34},{64,80... | collective-permute-start | bytes 1769480 | tf_op jit(solution)/shard_map/ppermute | solution.py:38
  34.7 14.4 %collective-permute-start.9 = (bf16[128,2304]{1,0:T(8,128)(2,1)S(1)}, bf16[128,2304]{1,0:T(8,128)(2,1)S(1)}, u32[]{:S(2)}, u32[]{:S(2)}) collective-permute-start(bf16[128,2304]{1,0:T(8,128)(2,1)S(1)} %subtract_convert_fusion.after_ref._.refs_0_), channel_id=1, source_target_pairs={{0,24},{32,38},{2,26},{34,32},{4,28},{36,34},{6,30},{38,36},{64,88... | collective-permute-start | bytes 1769480 | tf_op jit(solution)/shard_map/ppermute | solution.py:38
  49.7 5.5 %collective-permute-start.12 = (f32[512,512]{1,0:T(8,128)S(1)}, f32[512,512]{1,0:T(8,128)S(1)}, u32[]{:S(2)}, u32[]{:S(2)}) collective-permute-start(f32[512,512]{1,0:T(8,128)S(1)} %bitcast.91), channel_id=1, source_target_pairs={{0,32},{32,0},{2,34},{34,2},{4,36},{36,4},{6,38},{38,6},{64,96},{9... | collective-permute-start | bytes 3145736 | tf_op jit(solution)/shard_map/ppermute | solution.py:38
  58.0 6.1 %collective-permute-start.19 = (bf16[4,2,8,2304]{3,2,1,0:T(8,128)(2,1)S(1)}, bf16[4,2,8,2304]{3,2,1,0:T(8,128)(2,1)S(1)}, u32[]{:S(2)}, u32[]{:S(2)}) collective-permute-start(bf16[4,2,8,2304]{3,2,1,0:T(8,128)(2,1)S(1)} %slice_select_fusion), channel_id=1, source_target_pairs={{0,65},{32,96},{2,67},{34,98},{4,69},{36,100},{6,71},{38,102},{64,... | collective-permute-start | bytes 884744 | tf_op jit(solution)/shard_map/ppermute | solution.py:38
  58.9 12.1 %collective-permute-start.14 = (bf16[128,2304]{1,0:T(8,128)(2,1)S(1)}, bf16[128,2304]{1,0:T(8,128)(2,1)S(1)}, u32[]{:S(2)}, u32[]{:S(2)}) collective-permute-start(bf16[128,2304]{1,0:T(8,128)(2,1)S(1)} %fusion.1), channel_id=1, source_target_pairs={{0,8},{32,34},{2,10},{34,36},{4,12},{36,38},{6,14},{38,32},{64,72}... | collective-permute-start | bytes 1769480 | tf_op jit(solution)/shard_map/ppermute | solution.py:38
  59.5 11.5 %collective-permute-start.15 = (bf16[128,2304]{1,0:T(8,128)(2,1)S(1)}, bf16[128,2304]{1,0:T(8,128)(2,1)S(1)}, u32[]{:S(2)}, u32[]{:S(2)}) collective-permute-start(bf16[128,2304]{1,0:T(8,128)(2,1)S(1)} %fusion.2), channel_id=1, source_target_pairs={{0,24},{32,38},{2,26},{34,32},{4,28},{36,34},{6,30},{38,36},{64,88... | collective-permute-start | bytes 1769480 | tf_op jit(solution)/shard_map/ppermute | solution.py:38
  64.3 6.2 %collective-permute-start.20 = (bf16[4,8,2304]{2,1,0:T(8,128)(2,1)S(1)}, bf16[4,8,2304]{2,1,0:T(8,128)(2,1)S(1)}, u32[]{:S(2)}, u32[]{:S(2)}) collective-permute-start(bf16[4,8,2304]{2,1,0:T(8,128)(2,1)S(1)} %slice_bitcast_fusion.1), channel_id=1, source_target_pairs={{0,64},{32,97},{2,66},{34,99},{4,68},{36,101},{6,70},{38,103},{64,... | collective-permute-start | bytes 442376 | tf_op jit(solution)/shard_map/ppermute | solution.py:38
  70.6 9.3 %collective-permute-start.21 = (bf16[32,2304]{1,0:T(8,128)(2,1)S(1)}, bf16[32,2304]{1,0:T(8,128)(2,1)S(1)}, u32[]{:S(2)}, u32[]{:S(2)}) collective-permute-start(bf16[32,2304]{1,0:T(8,128)(2,1)S(1)} %fusion.13), channel_id=1, source_target_pairs={{0,16},{32,36},{2,18},{34,38},{4,20},{36,32},{6,22},{38,34},{64,80... | collective-permute-start | bytes 442376 | tf_op jit(solution)/shard_map/ppermute | solution.py:38
  71.3 8.7 %collective-permute-start.16 = (bf16[32,2304]{1,0:T(8,128)(2,1)S(1)}, bf16[32,2304]{1,0:T(8,128)(2,1)S(1)}, u32[]{:S(2)}, u32[]{:S(2)}) collective-permute-start(bf16[32,2304]{1,0:T(8,128)(2,1)S(1)} %get-tuple-element.67), channel_id=1, source_target_pairs={{0,64},{32,96},{2,66},{34,98},{4,68},{36,100},{6,70},{38,102},{64,... | collective-permute-start | bytes 442376 | tf_op jit(solution)/shard_map/ppermute | solution.py:38
  71.4 8.6 %collective-permute-start.18 = (bf16[32,2304]{1,0:T(8,128)(2,1)S(1)}, bf16[32,2304]{1,0:T(8,128)(2,1)S(1)}, u32[]{:S(2)}, u32[]{:S(2)}) collective-permute-start(bf16[32,2304]{1,0:T(8,128)(2,1)S(1)} %get-tuple-element.68), channel_id=1, source_target_pairs={{0,1},{32,33},{2,3},{34,35},{4,5},{36,37},{6,7},{38,39},{64,65},{9... | collective-permute-start | bytes 442376 | tf_op jit(solution)/shard_map/ppermute | solution.py:38
  74.6 5.7 %collective-permute-start.17 = (bf16[32,2304]{1,0:T(8,128)(2,1)S(1)}, bf16[32,2304]{1,0:T(8,128)(2,1)S(1)}, u32[]{:S(2)}, u32[]{:S(2)}) collective-permute-start(bf16[32,2304]{1,0:T(8,128)(2,1)S(1)} %get-tuple-element.69), channel_id=1, source_target_pairs={{0,65},{32,97},{2,67},{34,99},{4,69},{36,101},{6,71},{38,103},{64,... | collective-permute-start | bytes 442376 | tf_op jit(solution)/shard_map/ppermute | solution.py:38
  75.2 20.9 %collective-permute-start.28 = (bf16[2304,512]{1,0:T(8,128)(2,1)S(1)}, bf16[2304,512]{1,0:T(8,128)(2,1)S(1)}, u32[]{:S(2)}, u32[]{:S(2)}) collective-permute-start(bf16[2304,512]{1,0:T(8,128)(2,1)S(1)} %get-tuple-element.52.refs_9_), channel_id=1, source_target_pairs={{0,32},{32,0},{2,34},{34,2},{4,36},{36,4},{6,38},{38,6},{64,96},{9... | collective-permute-start | bytes 7077896 | tf_op jit(solution)/shard_map/ppermute | solution.py:38
  80.3 5.4 %collective-permute-start.24 = (bf16[32,2304]{1,0:T(8,128)(2,1)S(1)}, bf16[32,2304]{1,0:T(8,128)(2,1)S(1)}, u32[]{:S(2)}, u32[]{:S(2)}) collective-permute-start(bf16[32,2304]{1,0:T(8,128)(2,1)S(1)} %fusion.12), channel_id=1, source_target_pairs={{0,2},{32,40},{2,4},{34,42},{4,6},{36,44},{6,0},{38,46},{64,66},{9... | collective-permute-start | bytes 442376 | tf_op jit(solution)/shard_map/ppermute | solution.py:38
  81.3 5.5 %collective-permute-start.22 = (bf16[32,2304]{1,0:T(8,128)(2,1)S(1)}, bf16[32,2304]{1,0:T(8,128)(2,1)S(1)}, u32[]{:S(2)}, u32[]{:S(2)}) collective-permute-start(bf16[32,2304]{1,0:T(8,128)(2,1)S(1)} %fusion.12), channel_id=1, source_target_pairs={{0,6},{32,56},{2,0},{34,58},{4,2},{36,60},{6,4},{38,62},{64,70},{9... | collective-permute-start | bytes 442376 | tf_op jit(solution)/shard_map/ppermute | solution.py:38
  83.1 5.5 %collective-permute-start.23 = (bf16[32,2304]{1,0:T(8,128)(2,1)S(1)}, bf16[32,2304]{1,0:T(8,128)(2,1)S(1)}, u32[]{:S(2)}, u32[]{:S(2)}) collective-permute-start(bf16[32,2304]{1,0:T(8,128)(2,1)S(1)} %fusion.12), channel_id=1, source_target_pairs={{0,4},{32,48},{2,6},{34,50},{4,0},{36,52},{6,2},{38,54},{64,68},{9... | collective-permute-start | bytes 442376 | tf_op jit(solution)/shard_map/ppermute | solution.py:38
  88.7 7.3 %collective-permute-start.27 = (bf16[32,2304]{1,0:T(8,128)(2,1)S(1)}, bf16[32,2304]{1,0:T(8,128)(2,1)S(1)}, u32[]{:S(2)}, u32[]{:S(2)}) collective-permute-start(bf16[32,2304]{1,0:T(8,128)(2,1)S(1)} %fusion.7), channel_id=1, source_target_pairs={{0,1},{32,33},{2,3},{34,35},{4,5},{36,37},{6,7},{38,39},{64,65},{9... | collective-permute-start | bytes 442376 | tf_op jit(solution)/shard_map/ppermute | solution.py:38
  90.0 6.1 %collective-permute-start.26 = (bf16[32,2304]{1,0:T(8,128)(2,1)S(1)}, bf16[32,2304]{1,0:T(8,128)(2,1)S(1)}, u32[]{:S(2)}, u32[]{:S(2)}) collective-permute-start(bf16[32,2304]{1,0:T(8,128)(2,1)S(1)} %fusion.7), channel_id=1, source_target_pairs={{0,65},{32,97},{2,67},{34,99},{4,69},{36,101},{6,71},{38,103},{64,... | collective-permute-start | bytes 442376 | tf_op jit(solution)/shard_map/ppermute | solution.py:38
  91.4 4.6 %collective-permute-start.25 = (bf16[32,2304]{1,0:T(8,128)(2,1)S(1)}, bf16[32,2304]{1,0:T(8,128)(2,1)S(1)}, u32[]{:S(2)}, u32[]{:S(2)}) collective-permute-start(bf16[32,2304]{1,0:T(8,128)(2,1)S(1)} %fusion.7), channel_id=1, source_target_pairs={{0,64},{32,96},{2,66},{34,98},{4,68},{36,100},{6,70},{38,102},{64,... | collective-permute-start | bytes 442376 | tf_op jit(solution)/shard_map/ppermute | solution.py:38
  91.9 9.5 %collective-permute-start.30 = (bf16[32,2304]{1,0:T(8,128)(2,1)S(1)}, bf16[32,2304]{1,0:T(8,128)(2,1)S(1)}, u32[]{:S(2)}, u32[]{:S(2)}) collective-permute-start(bf16[32,2304]{1,0:T(8,128)(2,1)S(1)} %fusion.7), channel_id=1, source_target_pairs={{0,16},{32,36},{2,18},{34,38},{4,20},{36,32},{6,22},{38,34},{64,80... | collective-permute-start | bytes 442376 | tf_op jit(solution)/shard_map/ppermute | solution.py:38
  96.2 20.4 %collective-permute-start.34 = (bf16[128,2304]{1,0:T(8,128)(2,1)S(1)}, bf16[128,2304]{1,0:T(8,128)(2,1)S(1)}, u32[]{:S(2)}, u32[]{:S(2)}) collective-permute-start(bf16[128,2304]{1,0:T(8,128)(2,1)S(1)} %bitcast.79), channel_id=1, source_target_pairs={{0,8},{32,34},{2,10},{34,36},{4,12},{36,38},{6,14},{38,32},{64,72}... | collective-permute-start | bytes 1769480 | tf_op jit(solution)/shard_map/ppermute | solution.py:38
  101.5 15.5 %collective-permute-start.29 = (bf16[128,2304]{1,0:T(8,128)(2,1)S(1)}, bf16[128,2304]{1,0:T(8,128)(2,1)S(1)}, u32[]{:S(2)}, u32[]{:S(2)}) collective-permute-start(bf16[128,2304]{1,0:T(8,128)(2,1)S(1)} %bitcast.80), channel_id=1, source_target_pairs={{0,24},{32,38},{2,26},{34,32},{4,28},{36,34},{6,30},{38,36},{64,88... | collective-permute-start | bytes 1769480 | tf_op jit(solution)/shard_map/ppermute | solution.py:38
  101.5 5.5 %collective-permute-start.33 = (bf16[32,2304]{1,0:T(8,128)(2,1)S(1)}, bf16[32,2304]{1,0:T(8,128)(2,1)S(1)}, u32[]{:S(2)}, u32[]{:S(2)}) collective-permute-start(bf16[32,2304]{1,0:T(8,128)(2,1)S(1)} %collective-permute-done.30), channel_id=1, source_target_pairs={{0,1},{32,33},{2,3},{34,35},{4,5},{36,37},{6,7},{38,39},{64,65},{9... | collective-permute-start | bytes 442376 | tf_op jit(solution)/shard_map/ppermute | solution.py:38
  103.0 5.6 %collective-permute-start.32 = (bf16[32,2304]{1,0:T(8,128)(2,1)S(1)}, bf16[32,2304]{1,0:T(8,128)(2,1)S(1)}, u32[]{:S(2)}, u32[]{:S(2)}) collective-permute-start(bf16[32,2304]{1,0:T(8,128)(2,1)S(1)} %collective-permute-done.30), channel_id=1, source_target_pairs={{0,65},{32,97},{2,67},{34,99},{4,69},{36,101},{6,71},{38,103},{64,... | collective-permute-start | bytes 442376 | tf_op jit(solution)/shard_map/ppermute | solution.py:38
  104.4 4.6 %collective-permute-start.31 = (bf16[32,2304]{1,0:T(8,128)(2,1)S(1)}, bf16[32,2304]{1,0:T(8,128)(2,1)S(1)}, u32[]{:S(2)}, u32[]{:S(2)}) collective-permute-start(bf16[32,2304]{1,0:T(8,128)(2,1)S(1)} %collective-permute-done.30), channel_id=1, source_target_pairs={{0,64},{32,96},{2,66},{34,98},{4,68},{36,100},{6,70},{38,102},{64,... | collective-permute-start | bytes 442376 | tf_op jit(solution)/shard_map/ppermute | solution.py:38
  109.1 11.1 %collective-permute-start.37 = (bf16[128,2304]{1,0:T(8,128)(2,1)S(1)}, bf16[128,2304]{1,0:T(8,128)(2,1)S(1)}, u32[]{:S(2)}, u32[]{:S(2)}) collective-permute-start(bf16[128,2304]{1,0:T(8,128)(2,1)S(1)} %bitcast.83), channel_id=1, source_target_pairs={{0,32},{32,0},{2,34},{34,2},{4,36},{36,4},{6,38},{38,6},{64,96},{9... | collective-permute-start | bytes 1769480 | tf_op jit(solution)/shard_map/ppermute | solution.py:38
  (19 other events, 78.7 us)

commit v8 on v7

--- a/solution.py
+++ b/solution.py
@@ -345,7 +345,7 @@
         (for_mate, decoder_own, decoder_mate, decoder_other, norms, penalty)
     )
     preact = jnp.concatenate([dot(piece, encoder_own) for piece in centred])
-    preact = preact + to_core(for_mate) + encoder_bias
+    preact = preact + to_core(for_mate.astype(bf16)).astype(f32) + encoder_bias
     rectified = jnp.maximum(preact, 0.0)
     activations = jnp.square(rectified).astype(bf16)
     swapped = swap_blocks(activations)

time: 128 us -> 127 us (level)
  transfers between devices with their start and end apart: 39 -> 39, of which waited for: 18 -> 17; matrix products, arithmetic and copies ran while one was open for 5% -> 5% of each run, Pallas kernels for 9% -> 9%
where the time goes in v8:
time: 127 us
  starting transfers between devices  62.6 us (49%)
  waiting for transfers between devices  27.3 us (21%)
  Pallas kernels  18.3 us (14%)
  matrix products  8.96 us (7%)
  local copies, waits for them, and re-layouts  6.93 us (5%)
  other arithmetic  1.45 us (1%)
  between operations  1.36 us (1%)
    ppermute x38, starting transfers between devices, move(): return lax.ppermute(value, AXES, route(step))  61.1 us
    ppermute x38, waiting for transfers between devices, move(): return lax.ppermute(value, AXES, route(step))  27.3 us
    pallas_call x11, Pallas kernels, call(): pl.pallas_call(kernel, out_shape=tuple((jax.ShapeDtypeStruct(shape, dtype...  18.3 us
    dot_general x13, matrix products, dot(): return jnp.dot(a, b, preferred_element_type=f32)  8.96 us
    unnamed x27, local copies, waits for them, and re-layouts  6.73 us
  transfers between devices with their start and end apart: 39, of which 17 were waited for; matrix products, arithmetic and copies ran while one was open for 5% of the time, Pallas kernels for 9%

profile of v8, /device:TPU:1, one launch (start us, length us, event | category | flops | bytes accessed | tf_op | source)
XLA Modules:
  0.0 126.9 jit_solution(13373106932790214090)
XLA Ops:
  1.4 3.2 %fusion.25 = f32[16,4608]{1,0:T(8,128)S(1)} fusion(bf16[16,512]{1,0:T(8,128)(2,1)S(1)} %copy-done, bf16[512,4608]{1,0:T(8,128)(2,1)} %param.9), kind=kOutput, calls=%fused_computation.63 | convolution fusion | flops 75497472 | bytes 5029888 | tf_op jit(solution)/shard_map/dot_general | solution.py:284
  4.6 1.5 %collective-permute-start = (f32[16,2304]{1,0:T(8,128)S(1)}, f32[16,2304]{1,0:T(8,128)S(1)}, u32[]{:S(2)}, u32[]{:S(2)}) collective-permute-start(f32[16,2304]{1,0:T(8,128)S(1)} %slice_select_fusion.2), channel_id=1, source_target_pairs={{0,32},{32,0},{2,34},{34,2},{4,36},{36,4},{6,38},{38,6},{64,96},{9... | collective-permute-start | bytes 442376 | tf_op jit(solution)/shard_map/ppermute | solution.py:38
  7.1 1.5 %collective-permute-start.1 = (f32[16,2304]{1,0:T(8,128)S(1)}, f32[16,2304]{1,0:T(8,128)S(1)}, u32[]{:S(2)}, u32[]{:S(2)}) collective-permute-start(f32[16,2304]{1,0:T(8,128)S(1)} %select_add_fusion.after_ref), channel_id=1, source_target_pairs={{0,64},{64,0},{32,96},{96,32},{1,65},{65,1},{33,97},{97,33},{2,66}... | collective-permute-start | bytes 442376 | tf_op jit(solution)/shard_map/ppermute | solution.py:312
  8.8 2.1 %copy-done.3 = bf16[4608,512]{1,0:T(8,128)(2,1)S(1)} copy-done((bf16[4608,512]{1,0:T(8,128)(2,1)S(1)}, bf16[4608,512]{1,0:T(8,128)(2,1)}, u32[]{:S(2)}) %copy-start.3) | copy-done | bytes 4718616
  14.8 2.8 %collective-permute-start.3 = (bf16[16,2304]{1,0:T(8,128)(2,1)S(1)}, bf16[16,2304]{1,0:T(8,128)(2,1)S(1)}, u32[]{:S(2)}, u32[]{:S(2)}) collective-permute-start(bf16[16,2304]{1,0:T(8,128)(2,1)S(1)} %maximum_select_fusion), channel_id=1, source_target_pairs={{0,65},{32,97},{2,67},{34,99},{4,69},{36,101},{6,71},{38,103},{64,... | collective-permute-start | bytes 221192 | tf_op jit(solution)/shard_map/ppermute | solution.py:38
  18.3 1.5 %collective-permute-done.3 = bf16[16,2304]{1,0:T(8,128)(2,1)S(1)} collective-permute-done((bf16[16,2304]{1,0:T(8,128)(2,1)S(1)}, bf16[16,2304]{1,0:T(8,128)(2,1)S(1)}, u32[]{:S(2)}, u32[]{:S(2)}) %collective-permute-start.3) | collective-permute-done | bytes 73760 | tf_op jit(solution)/shard_map/ppermute | solution.py:38
  19.8 2.5 %collective-permute-start.4 = (bf16[32,2304]{1,0:T(8,128)(2,1)S(1)}, bf16[32,2304]{1,0:T(8,128)(2,1)S(1)}, u32[]{:S(2)}, u32[]{:S(2)}) collective-permute-start(bf16[32,2304]{1,0:T(8,128)(2,1)S(1)} %get-tuple-element.72), channel_id=1, source_target_pairs={{0,6},{32,56},{2,0},{34,58},{4,2},{36,60},{6,4},{38,62},{64,70},{9... | collective-permute-start | bytes 442376 | tf_op jit(solution)/shard_map/ppermute | solution.py:38
  22.4 1.7 %collective-permute-start.5 = (bf16[32,2304]{1,0:T(8,128)(2,1)S(1)}, bf16[32,2304]{1,0:T(8,128)(2,1)S(1)}, u32[]{:S(2)}, u32[]{:S(2)}) collective-permute-start(bf16[32,2304]{1,0:T(8,128)(2,1)S(1)} %get-tuple-element.72), channel_id=1, source_target_pairs={{0,4},{32,48},{2,6},{34,50},{4,0},{36,52},{6,2},{38,54},{64,68},{9... | collective-permute-start | bytes 442376 | tf_op jit(solution)/shard_map/ppermute | solution.py:38
  24.5 3.9 %collective-permute-done.5 = bf16[32,2304]{1,0:T(8,128)(2,1)S(1)} collective-permute-done((bf16[32,2304]{1,0:T(8,128)(2,1)S(1)}, bf16[32,2304]{1,0:T(8,128)(2,1)S(1)}, u32[]{:S(2)}, u32[]{:S(2)}) %collective-permute-start.5) | collective-permute-done | bytes 147488 | tf_op jit(solution)/shard_map/ppermute | solution.py:38
  29.7 1.5 %collective-permute-start.11 = (bf16[128,2304]{1,0:T(8,128)(2,1)S(1)}, bf16[128,2304]{1,0:T(8,128)(2,1)S(1)}, u32[]{:S(2)}, u32[]{:S(2)}) collective-permute-start(bf16[128,2304]{1,0:T(8,128)(2,1)S(1)} %subtract_convert_fusion.after_ref._.refs_0_), channel_id=1, source_target_pairs={{0,8},{32,34},{2,10},{34,36},{4,12},{36,38},{6,14},{38,32},{64,72}... | collective-permute-start | bytes 1769480 | tf_op jit(solution)/shard_map/ppermute | solution.py:38
  31.2 3.5 %collective-permute-start.10 = (bf16[128,2304]{1,0:T(8,128)(2,1)S(1)}, bf16[128,2304]{1,0:T(8,128)(2,1)S(1)}, u32[]{:S(2)}, u32[]{:S(2)}) collective-permute-start(bf16[128,2304]{1,0:T(8,128)(2,1)S(1)} %subtract_convert_fusion.after_ref._.refs_0_), channel_id=1, source_target_pairs={{0,16},{32,36},{2,18},{34,38},{4,20},{36,32},{6,22},{38,34},{64,80... | collective-permute-start | bytes 1769480 | tf_op jit(solution)/shard_map/ppermute | solution.py:38
  35.2 2.3 %copy-done.4 = bf16[4608,512]{1,0:T(8,128)(2,1)S(1)} copy-done((bf16[4608,512]{1,0:T(8,128)(2,1)S(1)}, bf16[4608,512]{1,0:T(8,128)(2,1)}, u32[]{:S(2)}) %copy-start.4) | copy-done | bytes 4718616
  39.4 1.6 %shard_map.109 = (bf16[512,2304]{1,0:T(8,128)(2,1)S(1)}, f32[512,1]{1,0:T(8,128)S(1)}, f32[1,512]{1,0:T(1,128)S(1)}) custom-call(s32[1]{0:T(128)} %bitcast.half_ref.core, bf16[128,2304]{1,0:T(8,128)(2,1)S(1)} %subtract_convert_fusion.after_ref._.refs_0_, bf16[512,4608]{1,0:T(8,128)(2,1)S(1)} %bitcast.75, bf16[512,2304]{1,0:T(8,128)(2,1)S(1)} %shard_map.107.own.b.refs_4_), custom_call_target="tpu_custom_call" | custom-call | bytes 6291456 | tf_op jit(solution)/shard_map/pallas_call | solution.py:114
  42.5 6.1 %collective-permute-done.10.refs_2_ = bf16[128,2304]{1,0:T(8,128)(2,1)S(1)} collective-permute-done((bf16[128,2304]{1,0:T(8,128)(2,1)S(1)}, bf16[128,2304]{1,0:T(8,128)(2,1)S(1)}, u32[]{:S(2)}, u32[]{:S(2)}) %collective-permute-start.10) | collective-permute-done | bytes 589856 | tf_op jit(solution)/shard_map/ppermute | solution.py:38
  49.6 3.2 %collective-permute-start.12 = (bf16[512,512]{1,0:T(8,128)(2,1)S(1)}, bf16[512,512]{1,0:T(8,128)(2,1)S(1)}, u32[]{:S(2)}, u32[]{:S(2)}) collective-permute-start(bf16[512,512]{1,0:T(8,128)(2,1)S(1)} %bitcast.92), channel_id=1, source_target_pairs={{0,32},{32,0},{2,34},{34,2},{4,36},{36,4},{6,38},{38,6},{64,96},{9... | collective-permute-start | bytes 1572872 | tf_op jit(solution)/shard_map/ppermute | solution.py:38
  58.6 2.7 %collective-permute-start.15 = (bf16[128,2304]{1,0:T(8,128)(2,1)S(1)}, bf16[128,2304]{1,0:T(8,128)(2,1)S(1)}, u32[]{:S(2)}, u32[]{:S(2)}) collective-permute-start(bf16[128,2304]{1,0:T(8,128)(2,1)S(1)} %fusion.2), channel_id=1, source_target_pairs={{0,24},{32,38},{2,26},{34,32},{4,28},{36,34},{6,30},{38,36},{64,88... | collective-permute-start | bytes 1769480 | tf_op jit(solution)/shard_map/ppermute | solution.py:38
  61.4 2.0 %collective-permute-done.19 = bf16[4,2,8,2304]{3,2,1,0:T(8,128)(2,1)S(1)} collective-permute-done((bf16[4,2,8,2304]{3,2,1,0:T(8,128)(2,1)S(1)}, bf16[4,2,8,2304]{3,2,1,0:T(8,128)(2,1)S(1)}, u32[]{:S(2)}, u32[]{:S(2)}) %collective-permute-start.19) | collective-permute-done | bytes 294944 | tf_op jit(solution)/shard_map/ppermute | solution.py:38
  63.5 2.8 %collective-permute-start.20 = (bf16[4,8,2304]{2,1,0:T(8,128)(2,1)S(1)}, bf16[4,8,2304]{2,1,0:T(8,128)(2,1)S(1)}, u32[]{:S(2)}, u32[]{:S(2)}) collective-permute-start(bf16[4,8,2304]{2,1,0:T(8,128)(2,1)S(1)} %slice_bitcast_fusion.1), channel_id=1, source_target_pairs={{0,64},{32,97},{2,66},{34,99},{4,68},{36,101},{6,70},{38,103},{64,... | collective-permute-start | bytes 442376 | tf_op jit(solution)/shard_map/ppermute | solution.py:38
  66.8 2.9 %shard_map.111 = (bf16[2304,512]{1,0:T(8,128)(2,1)S(1)}, bf16[512,512]{1,0:T(8,128)(2,1)S(1)}, bf16[512,512]{1,0:T(8,128)(2,1)S(1)}, f32[512,1]{1,0:T(8,128)S(1)}) custom-call(bf16[128,2304]{1,0:T(8,128)(2,1)S(1)} %subtract_convert_fusion.after_ref._.refs_0_, bf16[128,2304]{1,0:T(8,128)(2,1)S(1)} %collective-permute-done.9.refs_1_, ...), custom_call_target="tpu_custom_call" | custom-call | bytes 6291456 | tf_op jit(solution)/shard_map/pallas_call | solution.py:114
  70.5 3.2 %collective-permute-start.18 = (bf16[32,2304]{1,0:T(8,128)(2,1)S(1)}, bf16[32,2304]{1,0:T(8,128)(2,1)S(1)}, u32[]{:S(2)}, u32[]{:S(2)}) collective-permute-start(bf16[32,2304]{1,0:T(8,128)(2,1)S(1)} %get-tuple-element.68), channel_id=1, source_target_pairs={{0,1},{32,33},{2,3},{34,35},{4,5},{36,37},{6,7},{38,39},{64,65},{9... | collective-permute-start | bytes 442376 | tf_op jit(solution)/shard_map/ppermute | solution.py:38
  74.4 4.6 %collective-permute-start.28 = (bf16[2304,512]{1,0:T(8,128)(2,1)S(1)}, bf16[2304,512]{1,0:T(8,128)(2,1)S(1)}, u32[]{:S(2)}, u32[]{:S(2)}) collective-permute-start(bf16[2304,512]{1,0:T(8,128)(2,1)S(1)} %get-tuple-element.52.refs_9_), channel_id=1, source_target_pairs={{0,32},{32,0},{2,34},{34,2},{4,36},{36,4},{6,38},{38,6},{64,96},{9... | collective-permute-start | bytes 7077896 | tf_op jit(solution)/shard_map/ppermute | solution.py:38
  80.4 1.8 %collective-permute-start.22 = (bf16[32,2304]{1,0:T(8,128)(2,1)S(1)}, bf16[32,2304]{1,0:T(8,128)(2,1)S(1)}, u32[]{:S(2)}, u32[]{:S(2)}) collective-permute-start(bf16[32,2304]{1,0:T(8,128)(2,1)S(1)} %fusion.12), channel_id=1, source_target_pairs={{0,6},{32,56},{2,0},{34,58},{4,2},{36,60},{6,4},{38,62},{64,70},{9... | collective-permute-start | bytes 442376 | tf_op jit(solution)/shard_map/ppermute | solution.py:38
  83.2 1.6 %collective-permute-done.24 = bf16[32,2304]{1,0:T(8,128)(2,1)S(1)} collective-permute-done((bf16[32,2304]{1,0:T(8,128)(2,1)S(1)}, bf16[32,2304]{1,0:T(8,128)(2,1)S(1)}, u32[]{:S(2)}, u32[]{:S(2)}) %collective-permute-start.24) | collective-permute-done | bytes 147488 | tf_op jit(solution)/shard_map/ppermute | solution.py:38
  86.0 1.8 %collective-permute-done.23 = bf16[32,2304]{1,0:T(8,128)(2,1)S(1)} collective-permute-done((bf16[32,2304]{1,0:T(8,128)(2,1)S(1)}, bf16[32,2304]{1,0:T(8,128)(2,1)S(1)}, u32[]{:S(2)}, u32[]{:S(2)}) %collective-permute-start.23) | collective-permute-done | bytes 147488 | tf_op jit(solution)/shard_map/ppermute | solution.py:38
  89.0 1.5 %collective-permute-start.26 = (bf16[32,2304]{1,0:T(8,128)(2,1)S(1)}, bf16[32,2304]{1,0:T(8,128)(2,1)S(1)}, u32[]{:S(2)}, u32[]{:S(2)}) collective-permute-start(bf16[32,2304]{1,0:T(8,128)(2,1)S(1)} %fusion.7), channel_id=1, source_target_pairs={{0,65},{32,97},{2,67},{34,99},{4,69},{36,101},{6,71},{38,103},{64,... | collective-permute-start | bytes 442376 | tf_op jit(solution)/shard_map/ppermute | solution.py:38
  91.0 4.3 %collective-permute-start.30 = (bf16[32,2304]{1,0:T(8,128)(2,1)S(1)}, bf16[32,2304]{1,0:T(8,128)(2,1)S(1)}, u32[]{:S(2)}, u32[]{:S(2)}) collective-permute-start(bf16[32,2304]{1,0:T(8,128)(2,1)S(1)} %fusion.7), channel_id=1, source_target_pairs={{0,16},{32,36},{2,18},{34,38},{4,20},{36,32},{6,22},{38,34},{64,80... | collective-permute-start | bytes 442376 | tf_op jit(solution)/shard_map/ppermute | solution.py:38
  95.5 6.5 %collective-permute-start.34 = (bf16[128,2304]{1,0:T(8,128)(2,1)S(1)}, bf16[128,2304]{1,0:T(8,128)(2,1)S(1)}, u32[]{:S(2)}, u32[]{:S(2)}) collective-permute-start(bf16[128,2304]{1,0:T(8,128)(2,1)S(1)} %bitcast.79), channel_id=1, source_target_pairs={{0,8},{32,34},{2,10},{34,36},{4,12},{36,38},{6,14},{38,32},{64,72}... | collective-permute-start | bytes 1769480 | tf_op jit(solution)/shard_map/ppermute | solution.py:38
  104.7 3.0 %collective-permute-done.33 = bf16[32,2304]{1,0:T(8,128)(2,1)S(1)} collective-permute-done((bf16[32,2304]{1,0:T(8,128)(2,1)S(1)}, bf16[32,2304]{1,0:T(8,128)(2,1)S(1)}, u32[]{:S(2)}, u32[]{:S(2)}) %collective-permute-start.33) | collective-permute-done | bytes 147488 | tf_op jit(solution)/shard_map/ppermute | solution.py:38
  107.6 1.8 %collective-permute-done.32 = bf16[32,2304]{1,0:T(8,128)(2,1)S(1)} collective-permute-done((bf16[32,2304]{1,0:T(8,128)(2,1)S(1)}, bf16[32,2304]{1,0:T(8,128)(2,1)S(1)}, u32[]{:S(2)}, u32[]{:S(2)}) %collective-permute-start.32) | collective-permute-done | bytes 147488 | tf_op jit(solution)/shard_map/ppermute | solution.py:38
  109.5 6.1 %collective-permute-start.37 = (bf16[128,2304]{1,0:T(8,128)(2,1)S(1)}, bf16[128,2304]{1,0:T(8,128)(2,1)S(1)}, u32[]{:S(2)}, u32[]{:S(2)}) collective-permute-start(bf16[128,2304]{1,0:T(8,128)(2,1)S(1)} %bitcast.83), channel_id=1, source_target_pairs={{0,32},{32,0},{2,34},{34,2},{4,36},{36,4},{6,38},{38,6},{64,96},{9... | collective-permute-start | bytes 1769480 | tf_op jit(solution)/shard_map/ppermute | solution.py:38
  116.4 2.9 %shard_map.112 = (f32[512,512]{1,0:T(8,128)S(1)}, bf16[512,4608]{1,0:T(8,128)(2,1)}) custom-call(s32[1]{0:T(128)} %bitcast.half_ref.core, bf16[128,2304]{1,0:T(8,128)(2,1)S(1)} %bitcast.82, bf16[128,2304]{1,0:T(8,128)(2,1)S(1)} %collective-permute-done.29.refs_1_, bf16[128,2304]{1,0:T(8,128)(2,1)S(1)} %bitcast.84, ...), custom_call_target="tpu_custom_call" | custom-call | flops 2415919104 | bytes 8388608 | tf_op jit(solution)/shard_map/pallas_call | solution.py:114
  119.7 6.9 %shard_map.113 = (bf16[512,4608]{1,0:T(8,128)(2,1)}, bf16[4608,512]{1,0:T(8,128)(2,1)}, f32[1,512]{1,0:T(1,128)}) custom-call(s32[1]{0:T(128)} %bitcast.half_ref.core, bf16[512,4608]{1,0:T(8,128)(2,1)} %get-tuple-element.56._, f32[512,512]{1,0:T(8,128)S(1)} %get-tuple-element.57.own_acts, ...), custom_call_target="tpu_custom_call", output_to_operand_aliasing={{0}: (1, {})} | custom-call | flops 4831838208 | bytes 16777216 | tf_op jit(solution)/shard_map/pallas_call | solution.py:114
  (131 shorter events, 30.0 us)
Async XLA Ops:
  7.1 5.7 %collective-permute-start.1 = (f32[16,2304]{1,0:T(8,128)S(1)}, f32[16,2304]{1,0:T(8,128)S(1)}, u32[]{:S(2)}, u32[]{:S(2)}) collective-permute-start(f32[16,2304]{1,0:T(8,128)S(1)} %select_add_fusion.after_ref), channel_id=1, source_target_pairs={{0,64},{64,0},{32,96},{96,32},{1,65},{65,1},{33,97},{97,33},{2,66}... | collective-permute-start | bytes 442376 | tf_op jit(solution)/shard_map/ppermute | solution.py:312
  14.8 5.0 %collective-permute-start.3 = (bf16[16,2304]{1,0:T(8,128)(2,1)S(1)}, bf16[16,2304]{1,0:T(8,128)(2,1)S(1)}, u32[]{:S(2)}, u32[]{:S(2)}) collective-permute-start(bf16[16,2304]{1,0:T(8,128)(2,1)S(1)} %maximum_select_fusion), channel_id=1, source_target_pairs={{0,65},{32,97},{2,67},{34,99},{4,69},{36,101},{6,71},{38,103},{64,... | collective-permute-start | bytes 221192 | tf_op jit(solution)/shard_map/ppermute | solution.py:38
  17.7 12.0 %collective-permute-start.7 = (bf16[2304,512]{1,0:T(8,128)(2,1)}, bf16[2304,512]{1,0:T(8,128)(2,1)S(1)}, u32[]{:S(2)}, u32[]{:S(2)}) collective-permute-start(bf16[2304,512]{1,0:T(8,128)(2,1)} %copy-done.5), channel_id=1, source_target_pairs={{0,32},{32,0},{2,34},{34,2},{4,36},{36,4},{6,38},{38,6},{64,96},{9... | collective-permute-start | bytes 7077896 | tf_op jit(solution)/shard_map/ppermute | solution.py:38
  18.3 11.4 %collective-permute-start.8 = (bf16[512,2304]{1,0:T(8,128)(2,1)S(1)}, bf16[512,2304]{1,0:T(8,128)(2,1)S(1)}, u32[]{:S(2)}, u32[]{:S(2)}) collective-permute-start(bf16[512,2304]{1,0:T(8,128)(2,1)S(1)} %shard_map.104), channel_id=1, source_target_pairs={{0,32},{32,0},{2,34},{34,2},{4,36},{36,4},{6,38},{38,6},{64,96},{9... | collective-permute-start | bytes 7077896 | tf_op jit(solution)/shard_map/ppermute | solution.py:38
  22.4 7.1 %collective-permute-start.6 = (bf16[32,2304]{1,0:T(8,128)(2,1)S(1)}, bf16[32,2304]{1,0:T(8,128)(2,1)S(1)}, u32[]{:S(2)}, u32[]{:S(2)}) collective-permute-start(bf16[32,2304]{1,0:T(8,128)(2,1)S(1)} %get-tuple-element.72), channel_id=1, source_target_pairs={{0,2},{32,40},{2,4},{34,42},{4,6},{36,44},{6,0},{38,46},{64,66},{9... | collective-permute-start | bytes 442376 | tf_op jit(solution)/shard_map/ppermute | solution.py:38
  22.4 5.9 %collective-permute-start.5 = (bf16[32,2304]{1,0:T(8,128)(2,1)S(1)}, bf16[32,2304]{1,0:T(8,128)(2,1)S(1)}, u32[]{:S(2)}, u32[]{:S(2)}) collective-permute-start(bf16[32,2304]{1,0:T(8,128)(2,1)S(1)} %get-tuple-element.72), channel_id=1, source_target_pairs={{0,4},{32,48},{2,6},{34,50},{4,0},{36,52},{6,2},{38,54},{64,68},{9... | collective-permute-start | bytes 442376 | tf_op jit(solution)/shard_map/ppermute | solution.py:38
  29.7 12.3 %collective-permute-start.11 = (bf16[128,2304]{1,0:T(8,128)(2,1)S(1)}, bf16[128,2304]{1,0:T(8,128)(2,1)S(1)}, u32[]{:S(2)}, u32[]{:S(2)}) collective-permute-start(bf16[128,2304]{1,0:T(8,128)(2,1)S(1)} %subtract_convert_fusion.after_ref._.refs_0_), channel_id=1, source_target_pairs={{0,8},{32,34},{2,10},{34,36},{4,12},{36,38},{6,14},{38,32},{64,72}... | collective-permute-start | bytes 1769480 | tf_op jit(solution)/shard_map/ppermute | solution.py:38
  31.2 17.3 %collective-permute-start.10 = (bf16[128,2304]{1,0:T(8,128)(2,1)S(1)}, bf16[128,2304]{1,0:T(8,128)(2,1)S(1)}, u32[]{:S(2)}, u32[]{:S(2)}) collective-permute-start(bf16[128,2304]{1,0:T(8,128)(2,1)S(1)} %subtract_convert_fusion.after_ref._.refs_0_), channel_id=1, source_target_pairs={{0,16},{32,36},{2,18},{34,38},{4,20},{36,32},{6,22},{38,34},{64,80... | collective-permute-start | bytes 1769480 | tf_op jit(solution)/shard_map/ppermute | solution.py:38
  34.7 14.4 %collective-permute-start.9 = (bf16[128,2304]{1,0:T(8,128)(2,1)S(1)}, bf16[128,2304]{1,0:T(8,128)(2,1)S(1)}, u32[]{:S(2)}, u32[]{:S(2)}) collective-permute-start(bf16[128,2304]{1,0:T(8,128)(2,1)S(1)} %subtract_convert_fusion.after_ref._.refs_0_), channel_id=1, source_target_pairs={{0,24},{32,38},{2,26},{34,32},{4,28},{36,34},{6,30},{38,36},{64,88... | collective-permute-start | bytes 1769480 | tf_op jit(solution)/shard_map/ppermute | solution.py:38
  49.6 4.7 %collective-permute-start.12 = (bf16[512,512]{1,0:T(8,128)(2,1)S(1)}, bf16[512,512]{1,0:T(8,128)(2,1)S(1)}, u32[]{:S(2)}, u32[]{:S(2)}) collective-permute-start(bf16[512,512]{1,0:T(8,128)(2,1)S(1)} %bitcast.92), channel_id=1, source_target_pairs={{0,32},{32,0},{2,34},{34,2},{4,36},{36,4},{6,38},{38,6},{64,96},{9... | collective-permute-start | bytes 1572872 | tf_op jit(solution)/shard_map/ppermute | solution.py:38
  57.3 6.1 %collective-permute-start.19 = (bf16[4,2,8,2304]{3,2,1,0:T(8,128)(2,1)S(1)}, bf16[4,2,8,2304]{3,2,1,0:T(8,128)(2,1)S(1)}, u32[]{:S(2)}, u32[]{:S(2)}) collective-permute-start(bf16[4,2,8,2304]{3,2,1,0:T(8,128)(2,1)S(1)} %slice_select_fusion), channel_id=1, source_target_pairs={{0,65},{32,96},{2,67},{34,98},{4,69},{36,100},{6,71},{38,102},{64,... | collective-permute-start | bytes 884744 | tf_op jit(solution)/shard_map/ppermute | solution.py:38
  58.1 12.1 %collective-permute-start.14 = (bf16[128,2304]{1,0:T(8,128)(2,1)S(1)}, bf16[128,2304]{1,0:T(8,128)(2,1)S(1)}, u32[]{:S(2)}, u32[]{:S(2)}) collective-permute-start(bf16[128,2304]{1,0:T(8,128)(2,1)S(1)} %fusion.1), channel_id=1, source_target_pairs={{0,8},{32,34},{2,10},{34,36},{4,12},{36,38},{6,14},{38,32},{64,72}... | collective-permute-start | bytes 1769480 | tf_op jit(solution)/shard_map/ppermute | solution.py:38
  58.6 11.6 %collective-permute-start.15 = (bf16[128,2304]{1,0:T(8,128)(2,1)S(1)}, bf16[128,2304]{1,0:T(8,128)(2,1)S(1)}, u32[]{:S(2)}, u32[]{:S(2)}) collective-permute-start(bf16[128,2304]{1,0:T(8,128)(2,1)S(1)} %fusion.2), channel_id=1, source_target_pairs={{0,24},{32,38},{2,26},{34,32},{4,28},{36,34},{6,30},{38,36},{64,88... | collective-permute-start | bytes 1769480 | tf_op jit(solution)/shard_map/ppermute | solution.py:38
  63.5 6.2 %collective-permute-start.20 = (bf16[4,8,2304]{2,1,0:T(8,128)(2,1)S(1)}, bf16[4,8,2304]{2,1,0:T(8,128)(2,1)S(1)}, u32[]{:S(2)}, u32[]{:S(2)}) collective-permute-start(bf16[4,8,2304]{2,1,0:T(8,128)(2,1)S(1)} %slice_bitcast_fusion.1), channel_id=1, source_target_pairs={{0,64},{32,97},{2,66},{34,99},{4,68},{36,101},{6,70},{38,103},{64,... | collective-permute-start | bytes 442376 | tf_op jit(solution)/shard_map/ppermute | solution.py:38
  69.8 9.3 %collective-permute-start.21 = (bf16[32,2304]{1,0:T(8,128)(2,1)S(1)}, bf16[32,2304]{1,0:T(8,128)(2,1)S(1)}, u32[]{:S(2)}, u32[]{:S(2)}) collective-permute-start(bf16[32,2304]{1,0:T(8,128)(2,1)S(1)} %fusion.13), channel_id=1, source_target_pairs={{0,16},{32,36},{2,18},{34,38},{4,20},{36,32},{6,22},{38,34},{64,80... | collective-permute-start | bytes 442376 | tf_op jit(solution)/shard_map/ppermute | solution.py:38
  70.5 8.6 %collective-permute-start.16 = (bf16[32,2304]{1,0:T(8,128)(2,1)S(1)}, bf16[32,2304]{1,0:T(8,128)(2,1)S(1)}, u32[]{:S(2)}, u32[]{:S(2)}) collective-permute-start(bf16[32,2304]{1,0:T(8,128)(2,1)S(1)} %get-tuple-element.67), channel_id=1, source_target_pairs={{0,64},{32,96},{2,66},{34,98},{4,68},{36,100},{6,70},{38,102},{64,... | collective-permute-start | bytes 442376 | tf_op jit(solution)/shard_map/ppermute | solution.py:38
  70.5 8.5 %collective-permute-start.18 = (bf16[32,2304]{1,0:T(8,128)(2,1)S(1)}, bf16[32,2304]{1,0:T(8,128)(2,1)S(1)}, u32[]{:S(2)}, u32[]{:S(2)}) collective-permute-start(bf16[32,2304]{1,0:T(8,128)(2,1)S(1)} %get-tuple-element.68), channel_id=1, source_target_pairs={{0,1},{32,33},{2,3},{34,35},{4,5},{36,37},{6,7},{38,39},{64,65},{9... | collective-permute-start | bytes 442376 | tf_op jit(solution)/shard_map/ppermute | solution.py:38
  73.7 5.7 %collective-permute-start.17 = (bf16[32,2304]{1,0:T(8,128)(2,1)S(1)}, bf16[32,2304]{1,0:T(8,128)(2,1)S(1)}, u32[]{:S(2)}, u32[]{:S(2)}) collective-permute-start(bf16[32,2304]{1,0:T(8,128)(2,1)S(1)} %get-tuple-element.69), channel_id=1, source_target_pairs={{0,65},{32,97},{2,67},{34,99},{4,69},{36,101},{6,71},{38,103},{64,... | collective-permute-start | bytes 442376 | tf_op jit(solution)/shard_map/ppermute | solution.py:38
  74.4 21.1 %collective-permute-start.28 = (bf16[2304,512]{1,0:T(8,128)(2,1)S(1)}, bf16[2304,512]{1,0:T(8,128)(2,1)S(1)}, u32[]{:S(2)}, u32[]{:S(2)}) collective-permute-start(bf16[2304,512]{1,0:T(8,128)(2,1)S(1)} %get-tuple-element.52.refs_9_), channel_id=1, source_target_pairs={{0,32},{32,0},{2,34},{34,2},{4,36},{36,4},{6,38},{38,6},{64,96},{9... | collective-permute-start | bytes 7077896 | tf_op jit(solution)/shard_map/ppermute | solution.py:38
  79.5 5.3 %collective-permute-start.24 = (bf16[32,2304]{1,0:T(8,128)(2,1)S(1)}, bf16[32,2304]{1,0:T(8,128)(2,1)S(1)}, u32[]{:S(2)}, u32[]{:S(2)}) collective-permute-start(bf16[32,2304]{1,0:T(8,128)(2,1)S(1)} %fusion.12), channel_id=1, source_target_pairs={{0,2},{32,40},{2,4},{34,42},{4,6},{36,44},{6,0},{38,46},{64,66},{9... | collective-permute-start | bytes 442376 | tf_op jit(solution)/shard_map/ppermute | solution.py:38
  80.4 5.5 %collective-permute-start.22 = (bf16[32,2304]{1,0:T(8,128)(2,1)S(1)}, bf16[32,2304]{1,0:T(8,128)(2,1)S(1)}, u32[]{:S(2)}, u32[]{:S(2)}) collective-permute-start(bf16[32,2304]{1,0:T(8,128)(2,1)S(1)} %fusion.12), channel_id=1, source_target_pairs={{0,6},{32,56},{2,0},{34,58},{4,2},{36,60},{6,4},{38,62},{64,70},{9... | collective-permute-start | bytes 442376 | tf_op jit(solution)/shard_map/ppermute | solution.py:38
  82.3 5.5 %collective-permute-start.23 = (bf16[32,2304]{1,0:T(8,128)(2,1)S(1)}, bf16[32,2304]{1,0:T(8,128)(2,1)S(1)}, u32[]{:S(2)}, u32[]{:S(2)}) collective-permute-start(bf16[32,2304]{1,0:T(8,128)(2,1)S(1)} %fusion.12), channel_id=1, source_target_pairs={{0,4},{32,48},{2,6},{34,50},{4,0},{36,52},{6,2},{38,54},{64,68},{9... | collective-permute-start | bytes 442376 | tf_op jit(solution)/shard_map/ppermute | solution.py:38
  87.9 7.4 %collective-permute-start.27 = (bf16[32,2304]{1,0:T(8,128)(2,1)S(1)}, bf16[32,2304]{1,0:T(8,128)(2,1)S(1)}, u32[]{:S(2)}, u32[]{:S(2)}) collective-permute-start(bf16[32,2304]{1,0:T(8,128)(2,1)S(1)} %fusion.7), channel_id=1, source_target_pairs={{0,1},{32,33},{2,3},{34,35},{4,5},{36,37},{6,7},{38,39},{64,65},{9... | collective-permute-start | bytes 442376 | tf_op jit(solution)/shard_map/ppermute | solution.py:38
  89.0 6.3 %collective-permute-start.26 = (bf16[32,2304]{1,0:T(8,128)(2,1)S(1)}, bf16[32,2304]{1,0:T(8,128)(2,1)S(1)}, u32[]{:S(2)}, u32[]{:S(2)}) collective-permute-start(bf16[32,2304]{1,0:T(8,128)(2,1)S(1)} %fusion.7), channel_id=1, source_target_pairs={{0,65},{32,97},{2,67},{34,99},{4,69},{36,101},{6,71},{38,103},{64,... | collective-permute-start | bytes 442376 | tf_op jit(solution)/shard_map/ppermute | solution.py:38
  90.5 4.8 %collective-permute-start.25 = (bf16[32,2304]{1,0:T(8,128)(2,1)S(1)}, bf16[32,2304]{1,0:T(8,128)(2,1)S(1)}, u32[]{:S(2)}, u32[]{:S(2)}) collective-permute-start(bf16[32,2304]{1,0:T(8,128)(2,1)S(1)} %fusion.7), channel_id=1, source_target_pairs={{0,64},{32,96},{2,66},{34,98},{4,68},{36,100},{6,70},{38,102},{64,... | collective-permute-start | bytes 442376 | tf_op jit(solution)/shard_map/ppermute | solution.py:38
  91.0 11.0 %collective-permute-start.30 = (bf16[32,2304]{1,0:T(8,128)(2,1)S(1)}, bf16[32,2304]{1,0:T(8,128)(2,1)S(1)}, u32[]{:S(2)}, u32[]{:S(2)}) collective-permute-start(bf16[32,2304]{1,0:T(8,128)(2,1)S(1)} %fusion.7), channel_id=1, source_target_pairs={{0,16},{32,36},{2,18},{34,38},{4,20},{36,32},{6,22},{38,34},{64,80... | collective-permute-start | bytes 442376 | tf_op jit(solution)/shard_map/ppermute | solution.py:38
  95.5 20.2 %collective-permute-start.34 = (bf16[128,2304]{1,0:T(8,128)(2,1)S(1)}, bf16[128,2304]{1,0:T(8,128)(2,1)S(1)}, u32[]{:S(2)}, u32[]{:S(2)}) collective-permute-start(bf16[128,2304]{1,0:T(8,128)(2,1)S(1)} %bitcast.79), channel_id=1, source_target_pairs={{0,8},{32,34},{2,10},{34,36},{4,12},{36,38},{6,14},{38,32},{64,72}... | collective-permute-start | bytes 1769480 | tf_op jit(solution)/shard_map/ppermute | solution.py:38
  102.0 14.1 %collective-permute-start.29 = (bf16[128,2304]{1,0:T(8,128)(2,1)S(1)}, bf16[128,2304]{1,0:T(8,128)(2,1)S(1)}, u32[]{:S(2)}, u32[]{:S(2)}) collective-permute-start(bf16[128,2304]{1,0:T(8,128)(2,1)S(1)} %bitcast.80), channel_id=1, source_target_pairs={{0,24},{32,38},{2,26},{34,32},{4,28},{36,34},{6,30},{38,36},{64,88... | collective-permute-start | bytes 1769480 | tf_op jit(solution)/shard_map/ppermute | solution.py:38
  102.0 5.6 %collective-permute-start.33 = (bf16[32,2304]{1,0:T(8,128)(2,1)S(1)}, bf16[32,2304]{1,0:T(8,128)(2,1)S(1)}, u32[]{:S(2)}, u32[]{:S(2)}) collective-permute-start(bf16[32,2304]{1,0:T(8,128)(2,1)S(1)} %collective-permute-done.30), channel_id=1, source_target_pairs={{0,1},{32,33},{2,3},{34,35},{4,5},{36,37},{6,7},{38,39},{64,65},{9... | collective-permute-start | bytes 442376 | tf_op jit(solution)/shard_map/ppermute | solution.py:38
  102.3 7.1 %collective-permute-start.32 = (bf16[32,2304]{1,0:T(8,128)(2,1)S(1)}, bf16[32,2304]{1,0:T(8,128)(2,1)S(1)}, u32[]{:S(2)}, u32[]{:S(2)}) collective-permute-start(bf16[32,2304]{1,0:T(8,128)(2,1)S(1)} %collective-permute-done.30), channel_id=1, source_target_pairs={{0,65},{32,97},{2,67},{34,99},{4,69},{36,101},{6,71},{38,103},{64,... | collective-permute-start | bytes 442376 | tf_op jit(solution)/shard_map/ppermute | solution.py:38
  103.4 5.9 %collective-permute-start.31 = (bf16[32,2304]{1,0:T(8,128)(2,1)S(1)}, bf16[32,2304]{1,0:T(8,128)(2,1)S(1)}, u32[]{:S(2)}, u32[]{:S(2)}) collective-permute-start(bf16[32,2304]{1,0:T(8,128)(2,1)S(1)} %collective-permute-done.30), channel_id=1, source_target_pairs={{0,64},{32,96},{2,66},{34,98},{4,68},{36,100},{6,70},{38,102},{64,... | collective-permute-start | bytes 442376 | tf_op jit(solution)/shard_map/ppermute | solution.py:38
  109.5 9.8 %collective-permute-start.37 = (bf16[128,2304]{1,0:T(8,128)(2,1)S(1)}, bf16[128,2304]{1,0:T(8,128)(2,1)S(1)}, u32[]{:S(2)}, u32[]{:S(2)}) collective-permute-start(bf16[128,2304]{1,0:T(8,128)(2,1)S(1)} %bitcast.83), channel_id=1, source_target_pairs={{0,32},{32,0},{2,34},{34,2},{4,36},{36,4},{6,38},{38,6},{64,96},{9... | collective-permute-start | bytes 1769480 | tf_op jit(solution)/shard_map/ppermute | solution.py:38
  (19 other events, 78.5 us)
